TPU v7x, 512 devices: a whole 4x4x16 slice. The times are simulated.
512 devices in a mesh: section: 8 (over y_hi, x), dp: 64 (over z, y_lo, core).
Axes of the slice: x: 4, y: 4 (y_hi: 2, y_lo: 2; y = y_hi * 2 + y_lo), z: 16, core: 2. Of those that a mesh axis runs over, the one named last changes fastest.
Arguments:
- inputs: bfloat16 [4, 2048, 4096], P(None, 'dp'), may hold values from -6 to 6
- out_grad: bfloat16 [4, 2048, 4096], P(None, 'dp'), may hold values from -6 to 6
- doc_ids: int32 [4, 2048], P(None, 'dp'), may hold values from 0 to 255, never falling along the last dimension, each value on 1 to 16 neighbouring positions
- query_weight: bfloat16 [8, 4096, 512], P('section', 'dp'), may hold values from -0.09375 to 0.09375
- out_weight: bfloat16 [8, 4096, 512], P('section', 'dp'), may hold values from -0.25 to 0.25
- master: float32 [8, 2, 4096, 128], P('section', None, 'dp'), may hold values from -0.09375 to 0.09375
- first_moment: float32 [8, 2, 4096, 128], P('section', None, 'dp'), may hold values from -0.00390625 to 0.00390625
- second_moment: float32 [8, 2, 4096, 128], P('section', None, 'dp'), may hold values from 1e-08 to 1e-06
Outputs:
- update: float32 [8, 2, 4096, 128], P('section', None, 'dp')
- new_weights: bfloat16 [8, 2, 4096, 128], P('section', None, 'dp')
Inputs may be any that keep to these rules, and one draw needn't show every extreme that they name: `doc_ids`: ids never fall along a row; each id covers 1 to 16 consecutive positions.
All inputs are finite; a program needn't handle non-finite values.
Results may differ from a plain program's by a relative error of at most 0.02.
Values may be sent and summed in bfloat16 or wider, within the bound.
No kernel may reach another device: no remote copies, remote signals or barrier semaphores. Data moves between devices by JAX's collectives and lax.ppermute only.
A program may use at most 128 MiB of HBM per device.

v0:
```python
import math

import jax
import jax.numpy as jnp
from jax import lax
from jax.sharding import PartitionSpec as P

NORM_EPS = 1e-05
BETA_FIRST = 0.9
BETA_SECOND = 0.95
ADAM_EPSILON = 1e-08
LEARN_RATE = 0.001
CLIP_NORM = 1.0


def shifted(block, axis, distance):
    devices = range(lax.axis_size(axis))
    route = [(i - distance, i) for i in devices if i - distance in devices]
    return lax.ppermute(block, axis, route)


def matmul_tn(left_rows, right_rows):
    return lax.dot_general(
        left_rows, right_rows, (((0,), (0,)), ((), ())), preferred_element_type=jnp.float32
    )


def matmul_nt(left_rows, right_rows):
    return lax.dot_general(
        left_rows, right_rows, (((1,), (1,)), ((), ())), preferred_element_type=jnp.float32
    )


def allowed_pairs(segment):
    length = segment.shape[0]
    row_ids = lax.broadcasted_iota(jnp.int32, (length, length), 0)
    col_ids = lax.broadcasted_iota(jnp.int32, (length, length), 1)
    return (segment[:, None] == segment[None, :]) & (col_ids <= row_ids)


def forward_parts(layer_in, segment, w_query, w_keys, w_values, w_out):
    head_size = w_keys.shape[1]
    head_count = w_query.shape[1] // head_size
    length = layer_in.shape[0]
    score_scale = 1.0 / math.sqrt(head_size)
    signal = layer_in.astype(jnp.float32)
    inverse = lax.rsqrt(jnp.mean(signal * signal, axis=-1, keepdims=True) + NORM_EPS)
    normed = (signal * inverse).astype(jnp.bfloat16)
    query_rows = jnp.dot(normed, w_query, preferred_element_type=jnp.float32).astype(jnp.bfloat16)
    key_rows = jnp.dot(normed, w_keys, preferred_element_type=jnp.float32).astype(jnp.bfloat16)
    values = jnp.dot(normed, w_values, preferred_element_type=jnp.float32).astype(jnp.bfloat16)
    stacked_query = query_rows.reshape(length * head_count, head_size)
    mask = jnp.repeat(allowed_pairs(segment), head_count, axis=0)
    scores = matmul_nt(stacked_query, key_rows) * score_scale
    exp_scores = jnp.where(mask, jnp.exp(scores), 0.0)
    attn_probs = exp_scores / jnp.sum(exp_scores, axis=-1, keepdims=True)
    attn_low = attn_probs.astype(jnp.bfloat16)
    context_heads = jnp.dot(attn_low, values, preferred_element_type=jnp.float32).astype(
        jnp.bfloat16
    )
    context = context_heads.reshape(length, head_count * head_size)
    branch = matmul_nt(context, w_out)
    return (
        signal,
        inverse,
        normed,
        stacked_query,
        key_rows,
        values,
        attn_probs,
        attn_low,
        context,
        branch,
    )


def backward_parts(layer_in, segment, upstream, w_query, w_keys, w_values, w_out):
    head_size = w_keys.shape[1]
    head_count = w_query.shape[1] // head_size
    length = layer_in.shape[0]
    score_scale = 1.0 / math.sqrt(head_size)
    parts = forward_parts(layer_in, segment, w_query, w_keys, w_values, w_out)
    (
        signal,
        inverse,
        normed,
        stacked_query,
        key_rows,
        values,
        attn_probs,
        attn_low,
        context,
        branch,
    ) = parts
    grad_context = jnp.dot(upstream, w_out, preferred_element_type=jnp.float32).astype(jnp.bfloat16)
    context_grad_heads = grad_context.reshape(length * head_count, head_size)
    grad_probs = matmul_nt(context_grad_heads, values)
    grad_values = matmul_tn(attn_low, context_grad_heads).astype(jnp.bfloat16)
    centred = grad_probs - jnp.sum(attn_probs * grad_probs, axis=-1, keepdims=True)
    grad_scores = (attn_probs * centred * score_scale).astype(jnp.bfloat16)
    grad_query_heads = jnp.dot(grad_scores, key_rows, preferred_element_type=jnp.float32).astype(
        jnp.bfloat16
    )
    grad_query = grad_query_heads.reshape(length, head_count * head_size)
    grad_keys = matmul_tn(grad_scores, stacked_query).astype(jnp.bfloat16)
    grad_normed = (
        matmul_nt(grad_query, w_query)
        + matmul_nt(grad_keys, w_keys)
        + matmul_nt(grad_values, w_values)
    )
    grad_signal = inverse * grad_normed - signal * inverse**3 * jnp.mean(
        grad_normed * signal, axis=-1, keepdims=True
    )
    grad_input = (upstream.astype(jnp.float32) + grad_signal).astype(jnp.bfloat16)
    return (grad_input, normed, grad_keys, grad_values)


def shards(
    inputs, out_grad, doc_ids, query_weight, out_weight, master, first_moment, second_moment
):
    section_pos = lax.axis_index("section")
    sections = lax.axis_size("section")
    micro_count, length, features = inputs.shape
    head_size = master.shape[3]
    shard_parts = (
        query_weight[0],
        master[0, 0].astype(jnp.bfloat16),
        master[0, 1].astype(jnp.bfloat16),
        out_weight[0],
    )
    w_query, w_keys, w_values, w_out = (
        lax.all_gather(shard_parts[0], "dp", axis=0, tiled=True),
        lax.all_gather(shard_parts[1], "dp", axis=0, tiled=True),
        lax.all_gather(shard_parts[2], "dp", axis=0, tiled=True),
        lax.all_gather(shard_parts[3], "dp", axis=0, tiled=True),
    )
    ticks = sections + micro_count - 1
    zero_rows = jnp.zeros((length, features), jnp.bfloat16)

    def layer_output(layer_in, segment):
        parts = forward_parts(layer_in, segment, w_query, w_keys, w_values, w_out)
        return (parts[0] + parts[9]).astype(jnp.bfloat16)

    def skip_output(layer_in, segment):
        return zero_rows

    def forward_tick(tick_index, state_in):
        arrived, stored = state_in
        micro_index = tick_index - section_pos
        active = (micro_index >= 0) & (micro_index < micro_count)
        slot_index = jnp.clip(micro_index, 0, micro_count - 1)
        first_rows = lax.dynamic_index_in_dim(inputs, slot_index, 0, keepdims=False)
        layer_in = jnp.where(section_pos == 0, first_rows, arrived)
        segment = lax.dynamic_index_in_dim(doc_ids, slot_index, 0, keepdims=False)
        result = lax.cond(active, layer_output, skip_output, layer_in, segment)
        kept = lax.dynamic_index_in_dim(stored, slot_index, 0, keepdims=False)
        stored = lax.dynamic_update_index_in_dim(
            stored, jnp.where(active, layer_in, kept), slot_index, 0
        )
        arrived = shifted(result, "section", 1)
        return (arrived, stored)

    arrived, stored = lax.fori_loop(0, ticks, forward_tick, (zero_rows, jnp.zeros_like(inputs)))
    zero_heads = jnp.zeros((length, head_size), jnp.bfloat16)
    zero_grad = jnp.zeros((2, features, head_size), jnp.float32)

    def compute(layer_in, segment, upstream):
        grad_input, normed, grad_keys, grad_values = backward_parts(
            layer_in, segment, upstream, w_query, w_keys, w_values, w_out
        )
        increment = jnp.stack([matmul_tn(normed, grad_keys), matmul_tn(normed, grad_values)])
        return (grad_input, normed, grad_keys, grad_values, increment)

    def skipped(layer_in, segment, upstream):
        return (zero_rows, zero_rows, zero_heads, zero_heads, zero_grad)

    def backward_tick(tick_index, state_in):
        arrived, normed_buf, key_buf, value_buf, grad_acc = state_in
        micro_index = tick_index - (sections - 1 - section_pos)
        active = (micro_index >= 0) & (micro_index < micro_count)
        slot_index = jnp.clip(micro_index, 0, micro_count - 1)
        last_rows = lax.dynamic_index_in_dim(out_grad, slot_index, 0, keepdims=False)
        upstream = jnp.where(section_pos == sections - 1, last_rows, arrived)
        layer_in = lax.dynamic_index_in_dim(stored, slot_index, 0, keepdims=False)
        segment = lax.dynamic_index_in_dim(doc_ids, slot_index, 0, keepdims=False)
        grad_input, normed, grad_keys, grad_values, increment = lax.cond(
            active, compute, skipped, layer_in, segment, upstream
        )

        def keep_slot(buffer, fresh_rows):
            kept = lax.dynamic_index_in_dim(buffer, slot_index, 0, keepdims=False)
            return lax.dynamic_update_index_in_dim(
                buffer, jnp.where(active, fresh_rows, kept), slot_index, 0
            )

        normed_buf = keep_slot(normed_buf, normed)
        key_buf = keep_slot(key_buf, grad_keys)
        value_buf = keep_slot(value_buf, grad_values)
        grad_acc = grad_acc + increment
        arrived = shifted(grad_input, "section", -1)
        return (arrived, normed_buf, key_buf, value_buf, grad_acc)

    head_buf = jnp.zeros((micro_count, length, head_size), jnp.bfloat16)
    start_state = (zero_rows, jnp.zeros_like(inputs), head_buf, head_buf, zero_grad)
    final_state = lax.fori_loop(0, ticks, backward_tick, start_state)
    arrived, normed_buf, key_buf, value_buf, grad_acc = final_state
    grad_shard = lax.psum_scatter(grad_acc, "dp", scatter_dimension=1, tiled=True)
    local_sq = jnp.sum(grad_shard * grad_shard)
    total_sq = lax.psum(local_sq, ("section", "dp"))
    factor = jnp.minimum(1.0, CLIP_NORM / jnp.sqrt(total_sq))
    clipped = grad_shard * factor
    first_new = BETA_FIRST * first_moment[0] + (1.0 - BETA_FIRST) * clipped
    second_new = BETA_SECOND * second_moment[0] + (1.0 - BETA_SECOND) * clipped * clipped
    adam_step = first_new / (jnp.sqrt(second_new) + ADAM_EPSILON)
    fresh_shard = (master[0] - LEARN_RATE * adam_step).astype(jnp.bfloat16)
    return (adam_step[None], fresh_shard[None])


def solution(mesh):
    placed = (
        P(None, "dp", None),
        P(None, "dp", None),
        P(None, "dp"),
        P("section", "dp", None),
        P("section", "dp", None),
        P("section", None, "dp", None),
        P("section", None, "dp", None),
        P("section", None, "dp", None),
    )
    return jax.shard_map(
        shards,
        mesh=mesh,
        in_specs=placed,
        out_specs=(P("section", None, "dp", None), P("section", None, "dp", None)),
        check_vma=False,
    )
```

profile of v0, /device:TPU:1, one launch (start us, length us, event | category | flops | bytes accessed | tf_op | source)
XLA Modules:
  0.0 1397.6 jit_solution(4715061362269076411)
XLA Ops:
  10.8 126.2 %all-gather.11.cloned.1.call-done = bf16[1,1,4096,128]{3,2,1,0:T(8,128)(2,1)} async-done(((bf16[1,1,64,128]{3,2,1,0:T(8,128)(2,1)}), bf16[1,1,4096,128]{3,2,1,0:T(8,128)(2,1)}) %all-gather.11.cloned.1.call-update) | async-done | bytes 1048592 | tf_op jit(solution)/shard_map/all_gather | solution.py:133
  137.0 119.7 %all-gather.13.cloned.1.call-done = bf16[1,1,4096,128]{3,2,1,0:T(8,128)(2,1)} async-done(((bf16[1,1,64,128]{3,2,1,0:T(8,128)(2,1)}), bf16[1,1,4096,128]{3,2,1,0:T(8,128)(2,1)}) %all-gather.13.cloned.1.call-update) | async-done | bytes 1048592 | tf_op jit(solution)/shard_map/all_gather | solution.py:134
  256.7 123.1 %all-gather.9.cloned.1.call-done = bf16[1,4096,512]{2,1,0:T(8,128)(2,1)} async-done(((bf16[1,64,512]{2,1,0:T(8,128)(2,1)}), bf16[1,4096,512]{2,1,0:T(8,128)(2,1)}) %all-gather.9.cloned.1.call-update) | async-done | bytes 4194320 | tf_op jit(solution)/shard_map/all_gather | solution.py:132
  379.8 122.6 %all-gather.15.cloned.1.call-done = bf16[1,4096,512]{2,1,0:T(8,128)(2,1)} async-done(((bf16[1,64,512]{2,1,0:T(8,128)(2,1)}), bf16[1,4096,512]{2,1,0:T(8,128)(2,1)}) %all-gather.15.cloned.1.call-update) | async-done | bytes 4194320 | tf_op jit(solution)/shard_map/all_gather | solution.py:135
  502.5 185.0 %while.34 = (s32[]{:T(128)}, bf16[32,4096]{1,0:T(8,128)(2,1)S(1)}, bf16[4,32,4096]{2,1,0:T(8,128)(2,1)S(1)}, s32[]{:T(128)}, pred[]{:T(512)}, /*index=5*/bf16[4,...) while((s32[]{:T(128)}, bf16[32,4096]{1,0:T(8,128)(2,1)S(1)}, ...), condition=%wide.region_5.6_spmd, body=%wide.region_0.5_spmd.sunk | while | flops 339934112 | bytes 23646712 | solution.py:163
  503.7 9.5 conditional.5
  521.6 9.5 conditional.5
  541.4 9.5 conditional.5
  560.3 9.5 conditional.5
  579.3 12.5 collective-permute-start
  606.4 11.6 collective-permute-start
  633.5 16.1 %collective-permute-start = (bf16[32,4096]{1,0:T(8,128)(2,1)}, bf16[32,4096]{1,0:T(8,128)(2,1)S(1)}, u32[]{:S(2)}, u32[]{:S(2)}) collective-permute-start(bf16[32,4096]{1,0:T(8,128)(2,1)} %get-tuple-element.985), channel_id=1, source_target_pairs={{0,64},{64,128},{128,192},{192,256},{256,320},{320,384},{384,448},... | collective-permute-start | bytes 786440 | tf_op jit(solution)/shard_map/while/body/eval_jaxpr/ppermute | solution.py:19
  655.0 7.3 collective-permute-start
  667.8 16.1 %collective-permute-start = (bf16[32,4096]{1,0:T(8,128)(2,1)}, bf16[32,4096]{1,0:T(8,128)(2,1)S(1)}, u32[]{:S(2)}, u32[]{:S(2)}) collective-permute-start(bf16[32,4096]{1,0:T(8,128)(2,1)} %get-tuple-element.985), channel_id=1, source_target_pairs={{0,64},{64,128},{128,192},{192,256},{256,320},{320,384},{384,448},... | collective-permute-start | bytes 786440 | tf_op jit(solution)/shard_map/while/body/eval_jaxpr/ppermute | solution.py:19
  687.6 352.1 %while.35 = (s32[]{:T(128)}, bf16[32,4096]{1,0:T(8,128)(2,1)S(1)}, f32[2,4096,128]{2,1,0:T(8,128)}, s32[]{:T(128)}, pred[]{:T(512)}, /*index=5*/bf16[4,32,4096]{...) while((s32[]{:T(128)}, bf16[32,4096]{1,0:T(8,128)(2,1)S(1)}, ...), condition=%wide.region_13.14_spmd.clone, body=%wide.region_6.13_spmd.clone.sunk | while | flops 616815488 | bytes 58615864 | solution.py:205
  755.7 8.2 collective-permute-done.1
  774.1 6.9 collective-permute-done.1
  791.0 122.0 %collective-permute-done.1 = bf16[32,4096]{1,0:T(8,128)(2,1)S(1)} collective-permute-done((bf16[32,4096]{1,0:T(8,128)(2,1)}, bf16[32,4096]{1,0:T(8,128)(2,1)S(1)}, u32[]{:S(2)}, u32[]{:S(2)}) %collective-permute-start.1) | collective-permute-done | bytes 262176 | tf_op jit(solution)/shard_map/while/body/eval_jaxpr/ppermute | solution.py:19
  913.1 21.6 %conditional.6 = (bf16[32,4096]{1,0:T(8,128)(2,1)}, f32[2,4096,128]{2,1,0:T(8,128)}) conditional(s32[]{:T(128)} %convert_element_type.212, () %tuple.113, (pred[]{:T(512)}, s32[]{:T(128)}, bf16[4,32,4096]{2,1,0:T(8,128)(2,1)}, bf16[32,4096]{1,0:T(8,128)(2,1)S(1)}, bf16[4,32,4096]{2,1,0:T(8,128)(2,1)S(1)}, /*index=5*/s32[4,32]{1,0:T(4,128)}, ...), branch_computations={%region_7.7_spmd, %region_8.12_spmd} | conditional | flops 614718336 | bytes 44984072 | solution.py:186
  945.6 21.6 %conditional.6 = (bf16[32,4096]{1,0:T(8,128)(2,1)}, f32[2,4096,128]{2,1,0:T(8,128)}) conditional(s32[]{:T(128)} %convert_element_type.212, () %tuple.113, (pred[]{:T(512)}, s32[]{:T(128)}, bf16[4,32,4096]{2,1,0:T(8,128)(2,1)}, bf16[32,4096]{1,0:T(8,128)(2,1)S(1)}, bf16[4,32,4096]{2,1,0:T(8,128)(2,1)S(1)}, /*index=5*/s32[4,32]{1,0:T(4,128)}, ...), branch_computations={%region_7.7_spmd, %region_8.12_spmd} | conditional | flops 614718336 | bytes 44984072 | solution.py:186
  978.1 21.6 %conditional.6 = (bf16[32,4096]{1,0:T(8,128)(2,1)}, f32[2,4096,128]{2,1,0:T(8,128)}) conditional(s32[]{:T(128)} %convert_element_type.212, () %tuple.113, (pred[]{:T(512)}, s32[]{:T(128)}, bf16[4,32,4096]{2,1,0:T(8,128)(2,1)}, bf16[32,4096]{1,0:T(8,128)(2,1)S(1)}, bf16[4,32,4096]{2,1,0:T(8,128)(2,1)S(1)}, /*index=5*/s32[4,32]{1,0:T(4,128)}, ...), branch_computations={%region_7.7_spmd, %region_8.12_spmd} | conditional | flops 614718336 | bytes 44984072 | solution.py:186
  1010.7 21.6 %conditional.6 = (bf16[32,4096]{1,0:T(8,128)(2,1)}, f32[2,4096,128]{2,1,0:T(8,128)}) conditional(s32[]{:T(128)} %convert_element_type.212, () %tuple.113, (pred[]{:T(512)}, s32[]{:T(128)}, bf16[4,32,4096]{2,1,0:T(8,128)(2,1)}, bf16[32,4096]{1,0:T(8,128)(2,1)S(1)}, bf16[4,32,4096]{2,1,0:T(8,128)(2,1)S(1)}, /*index=5*/s32[4,32]{1,0:T(4,128)}, ...), branch_computations={%region_7.7_spmd, %region_8.12_spmd} | conditional | flops 614718336 | bytes 44984072 | solution.py:186
  1039.7 241.3 %reduce-scatter.2.cloned.1.call-done = f32[2,64,128]{2,1,0:T(8,128)} async-done(((f32[2,4096,128]{2,1,0:T(8,128)}), f32[2,64,128]{2,1,0:T(8,128)}) %reduce-scatter.2.cloned.1.call-update) | async-done | bytes 65552 | tf_op jit(solution)/shard_map/reduce_scatter | solution.py:207
  1282.4 106.4 %psum.7 = f32[]{:T(128)} all-reduce(f32[]{:T(128)} %multiply_reduce_fusion.1), channel_id=1, replica_groups=mesh['section'=8,'dp'=64] {'section','dp'}, use_global_device_ids=true, to_apply=%region_16.17 | all-reduce | flops 1 | bytes 8 | tf_op jit(solution)/shard_map/psum | solution.py:209
  (312 shorter events, 367.4 us)
Async XLA Ops:
  7.2 129.9 %all-gather.11.cloned.1.call-start = ((), (), s32[]{:S(2)}) async-start(), calls=%async_computation.3 | async-start | bytes 1064960 | tf_op jit(solution)/shard_map/all_gather | solution.py:133
  8.7 248.0 %all-gather.13.cloned.1.call-start = ((), (), s32[]{:S(2)}) async-start(), calls=%async_computation.4 | async-start | bytes 1064960 | tf_op jit(solution)/shard_map/all_gather | solution.py:134
  9.4 370.4 %all-gather.9.cloned.1.call-start = ((), (), s32[]{:S(2)}) async-start(), calls=%async_computation.2 | async-start | bytes 4259840 | tf_op jit(solution)/shard_map/all_gather | solution.py:132
  10.2 492.2 %all-gather.15.cloned.1.call-start = ((), (), s32[]{:S(2)}) async-start(), calls=%async_computation.5 | async-start | bytes 4259840 | tf_op jit(solution)/shard_map/all_gather | solution.py:135
  10.8 1270.1 %reduce-scatter.2.cloned.1.call-start = ((), (), s32[]{:S(2)}) async-start(), calls=%async_computation.1 | async-start | bytes 4259840 | tf_op jit(solution)/shard_map/reduce_scatter | solution.py:207
  531.2 9.1 collective-permute-start
  550.9 8.2 collective-permute-start
  569.8 7.6 collective-permute-start
  579.3 16.1 %collective-permute-start = (bf16[32,4096]{1,0:T(8,128)(2,1)}, bf16[32,4096]{1,0:T(8,128)(2,1)S(1)}, u32[]{:S(2)}, u32[]{:S(2)}) collective-permute-start(bf16[32,4096]{1,0:T(8,128)(2,1)} %get-tuple-element.985), channel_id=1, source_target_pairs={{0,64},{64,128},{128,192},{192,256},{256,320},{320,384},{384,448},... | collective-permute-start | bytes 786440 | tf_op jit(solution)/shard_map/while/body/eval_jaxpr/ppermute | solution.py:19
  606.4 15.2 %collective-permute-start = (bf16[32,4096]{1,0:T(8,128)(2,1)}, bf16[32,4096]{1,0:T(8,128)(2,1)S(1)}, u32[]{:S(2)}, u32[]{:S(2)}) collective-permute-start(bf16[32,4096]{1,0:T(8,128)(2,1)} %get-tuple-element.985), channel_id=1, source_target_pairs={{0,64},{64,128},{128,192},{192,256},{256,320},{320,384},{384,448},... | collective-permute-start | bytes 786440 | tf_op jit(solution)/shard_map/while/body/eval_jaxpr/ppermute | solution.py:19
  623.4 8.2 collective-permute-start
  633.5 19.7 %collective-permute-start = (bf16[32,4096]{1,0:T(8,128)(2,1)}, bf16[32,4096]{1,0:T(8,128)(2,1)S(1)}, u32[]{:S(2)}, u32[]{:S(2)}) collective-permute-start(bf16[32,4096]{1,0:T(8,128)(2,1)} %get-tuple-element.985), channel_id=1, source_target_pairs={{0,64},{64,128},{128,192},{192,256},{256,320},{320,384},{384,448},... | collective-permute-start | bytes 786440 | tf_op jit(solution)/shard_map/while/body/eval_jaxpr/ppermute | solution.py:19
  655.0 10.9 collective-permute-start
  667.8 19.7 %collective-permute-start = (bf16[32,4096]{1,0:T(8,128)(2,1)}, bf16[32,4096]{1,0:T(8,128)(2,1)S(1)}, u32[]{:S(2)}, u32[]{:S(2)}) collective-permute-start(bf16[32,4096]{1,0:T(8,128)(2,1)} %get-tuple-element.985), channel_id=1, source_target_pairs={{0,64},{64,128},{128,192},{192,256},{256,320},{320,384},{384,448},... | collective-permute-start | bytes 786440 | tf_op jit(solution)/shard_map/while/body/eval_jaxpr/ppermute | solution.py:19
  690.5 11.3 collective-permute-start.1
  704.7 11.3 collective-permute-start.1
  718.9 11.3 collective-permute-start.1
  733.1 12.6 collective-permute-start.1
  748.6 15.4 %collective-permute-start.1 = (bf16[32,4096]{1,0:T(8,128)(2,1)}, bf16[32,4096]{1,0:T(8,128)(2,1)S(1)}, u32[]{:S(2)}, u32[]{:S(2)}) collective-permute-start(bf16[32,4096]{1,0:T(8,128)(2,1)} %get-tuple-element.889), channel_id=1, source_target_pairs={{64,0},{128,64},{192,128},{256,192},{320,256},{384,320},{448,384},... | collective-permute-start | bytes 786440 | tf_op jit(solution)/shard_map/while/body/eval_jaxpr/ppermute | solution.py:19
  766.9 14.0 %collective-permute-start.1 = (bf16[32,4096]{1,0:T(8,128)(2,1)}, bf16[32,4096]{1,0:T(8,128)(2,1)S(1)}, u32[]{:S(2)}, u32[]{:S(2)}) collective-permute-start(bf16[32,4096]{1,0:T(8,128)(2,1)} %get-tuple-element.889), channel_id=1, source_target_pairs={{64,0},{128,64},{192,128},{256,192},{320,256},{384,320},{448,384},... | collective-permute-start | bytes 786440 | tf_op jit(solution)/shard_map/while/body/eval_jaxpr/ppermute | solution.py:19
  783.9 129.2 %collective-permute-start.1 = (bf16[32,4096]{1,0:T(8,128)(2,1)}, bf16[32,4096]{1,0:T(8,128)(2,1)S(1)}, u32[]{:S(2)}, u32[]{:S(2)}) collective-permute-start(bf16[32,4096]{1,0:T(8,128)(2,1)} %get-tuple-element.889), channel_id=1, source_target_pairs={{64,0},{128,64},{192,128},{256,192},{320,256},{384,320},{448,384},... | collective-permute-start | bytes 786440 | tf_op jit(solution)/shard_map/while/body/eval_jaxpr/ppermute | solution.py:19
  934.7 10.9 collective-permute-start.1
  967.2 10.9 collective-permute-start.1
  999.8 10.9 collective-permute-start.1
  (22 other events, 1147.7 us)
Sparse Core Ops, SparseCore 0:
  10.7 126.2 all-gather.10
  139.7 116.9 all-gather.12
  258.9 120.8 all-gather.8
  381.8 120.5 all-gather.14
  1039.8 241.0 reduce-scatter.1
where the time goes:
time: 1400 us
  waiting for transfers between devices  947 us (68%)
  blocking collectives  106 us (8%)
  other arithmetic  103 us (7%)
  starting transfers between devices  99.6 us (7%)
  matrix products  92.2 us (7%)
  local copies, waits for them, and re-layouts  33.6 us (2%)
  between operations  14.5 us (1%)
    reduce_scatter x1, waiting for transfers between devices, shards(): lax.psum_scatter(grad_acc, 'dp', scatter_dimension=1, tiled=True)  241 us
    ppermute x22, waiting for transfers between devices, shifted(): return lax.ppermute(block, axis, route)  212 us
    all_gather x1, waiting for transfers between devices, shards(): lax.all_gather(shard_parts[1], 'dp', axis=0, tiled=True)  126 us
    all_gather x1, waiting for transfers between devices, shards(): lax.all_gather(shard_parts[0], 'dp', axis=0, tiled=True)  123 us
    all_gather x1, waiting for transfers between devices, shards(): lax.all_gather(shard_parts[3], 'dp', axis=0, tiled=True)  123 us
    all_gather x1, waiting for transfers between devices, shards(): lax.all_gather(shard_parts[2], 'dp', axis=0, tiled=True)  120 us
    psum x1, blocking collectives, shards(): total_sq = lax.psum(local_sq, ('section', 'dp'))  106 us
    ppermute x22, starting transfers between devices, shifted(): return lax.ppermute(block, axis, route)  99.4 us
  transfers between devices with their start and end apart: 27, of which 27 were waited for; matrix products, arithmetic and copies ran while one was open for 5% of the time, Pallas kernels for 0%

commit v1 on v0

v1 whole, which is shorter than its diff:
```python
import functools
import math

import jax
import jax.numpy as jnp
from jax import lax
from jax.experimental import pallas as pl
from jax.experimental.pallas import tpu as pltpu
from jax.sharding import Mesh, PartitionSpec as P

NORM_EPS = 1e-05
BETA_FIRST = 0.9
BETA_SECOND = 0.95
ADAM_EPSILON = 1e-08
LEARN_RATE = 0.001
CLIP_NORM = 1.0

FINE = {"yh": 2, "x": 4, "z1": 4, "z2": 4, "yl": 2, "c": 2}
DP = ("z1", "z2", "yl", "c")
LAYERS = 4
LENGTH = 32
WIDTH = 4096
HEAD = 128
HEADS = 4
QW = HEAD * HEADS
KVW = QW + 2 * HEAD
COLS = KVW + QW
CHUNK = 1024
SCALE = 1.0 / math.sqrt(HEAD)
VMEM_LIMIT = 60 * 1024 * 1024
F32 = jnp.float32
BF16 = jnp.bfloat16


def dot_nn(a, b):
    return lax.dot_general(a, b, (((1,), (0,)), ((), ())), preferred_element_type=F32)


def dot_nt(a, b):
    return lax.dot_general(a, b, (((1,), (1,)), ((), ())), preferred_element_type=F32)


def dot_tn(a, b):
    return lax.dot_general(a, b, (((0,), (0,)), ((), ())), preferred_element_type=F32)


def weight_copies(w_hbm, w_vmem, sems, layer):
    copies = []
    for c in range(2):
        for yl in range(2):
            for z2 in range(4):
                at = (c * 2 + yl) * 4 + z2
                copies.append(
                    pltpu.make_async_copy(
                        w_hbm.at[:, z2, yl, c, layer], w_vmem.at[layer, at], sems.at[layer, at]
                    )
                )
    return copies


def stack_heads(rows):
    return jnp.concatenate([rows[:, h * HEAD : (h + 1) * HEAD] for h in range(HEADS)], axis=0)


def unstack_heads(rows):
    return jnp.concatenate([rows[h * LENGTH : (h + 1) * LENGTH] for h in range(HEADS)], axis=1)


def inverse_norm(h_ref, layer):
    total = jnp.zeros((LENGTH, 1), F32)
    for at in range(0, WIDTH, CHUNK):
        signal = h_ref[layer, :, at : at + CHUNK].astype(F32)
        total = total + jnp.sum(signal * signal, axis=-1, keepdims=True)
    return lax.rsqrt(total * (1.0 / WIDTH) + NORM_EPS)


def weight_rows(w_vmem, layer, at, first, last):
    per = CHUNK // 256
    block = w_vmem[layer, at // 256 : at // 256 + per, :, :, first:last]
    return block.reshape(CHUNK, last - first)


def forward_kernel(
    h_ref, seg_col, seg_row, w_hbm, out_ref, h_all, n_all, q_all, k_all, v_all, p_all, w_vmem, sems
):
    for layer in range(LAYERS):
        for copy in weight_copies(w_hbm, w_vmem, sems, layer):
            copy.start()
    row_ids = lax.broadcasted_iota(jnp.int32, (LENGTH, LENGTH), 0)
    col_ids = lax.broadcasted_iota(jnp.int32, (LENGTH, LENGTH), 1)
    allowed = ((seg_col[...] == seg_row[...]) & (col_ids <= row_ids)).astype(F32)
    mask = jnp.concatenate([allowed] * HEADS, axis=0) > 0.0
    h_all[0] = h_ref[...]
    for layer in range(LAYERS):
        inverse = inverse_norm(h_all, layer)
        for at in range(0, WIDTH, CHUNK):
            signal = h_all[layer, :, at : at + CHUNK].astype(F32)
            n_all[layer, :, at : at + CHUNK] = (signal * inverse).astype(BF16)
        for copy in weight_copies(w_hbm, w_vmem, sems, layer):
            copy.wait()
        acc = jnp.zeros((LENGTH, KVW), F32)
        for at in range(0, WIDTH, CHUNK):
            acc = acc + dot_nn(
                n_all[layer, :, at : at + CHUNK], weight_rows(w_vmem, layer, at, 0, KVW)
            )
        rows = acc.astype(BF16)
        query = stack_heads(rows[:, :QW])
        keys = rows[:, QW : QW + HEAD]
        values = rows[:, QW + HEAD :]
        scores = dot_nt(query, keys) * SCALE
        exp_scores = jnp.where(mask, jnp.exp(scores), 0.0)
        probs = exp_scores / jnp.sum(exp_scores, axis=-1, keepdims=True)
        context = unstack_heads(dot_nn(probs.astype(BF16), values).astype(BF16))
        q_all[layer] = query
        k_all[layer] = keys
        v_all[layer] = values
        p_all[layer] = probs
        for at in range(0, WIDTH, CHUNK):
            signal = h_all[layer, :, at : at + CHUNK].astype(F32)
            branch = dot_nt(context, weight_rows(w_vmem, layer, at, KVW, COLS))
            result = (signal + branch).astype(BF16)
            if layer + 1 < LAYERS:
                h_all[layer + 1, :, at : at + CHUNK] = result
            else:
                out_ref[:, at : at + CHUNK] = result


def backward_kernel(
    need_up, up_ref, h_all, q_all, k_all, v_all, p_all, w_hbm, out_ref, g_all, w_vmem, gn, sems
):
    for layer in reversed(range(LAYERS)):
        for copy in weight_copies(w_hbm, w_vmem, sems, layer):
            copy.start()
    out_ref[...] = up_ref[...]
    for layer in reversed(range(LAYERS)):
        for copy in weight_copies(w_hbm, w_vmem, sems, layer):
            copy.wait()
        acc = jnp.zeros((LENGTH, QW), F32)
        for at in range(0, WIDTH, CHUNK):
            acc = acc + dot_nn(
                out_ref[:, at : at + CHUNK], weight_rows(w_vmem, layer, at, KVW, COLS)
            )
        grad_context = stack_heads(acc.astype(BF16))
        query, keys, values, probs = q_all[layer], k_all[layer], v_all[layer], p_all[layer]
        grad_probs = dot_nt(grad_context, values)
        grad_values = dot_tn(probs.astype(BF16), grad_context).astype(BF16)
        centred = grad_probs - jnp.sum(probs * grad_probs, axis=-1, keepdims=True)
        grad_scores = (probs * centred * SCALE).astype(BF16)
        grad_query = unstack_heads(dot_nn(grad_scores, keys).astype(BF16))
        grad_keys = dot_tn(grad_scores, query).astype(BF16)
        g_all[layer, :, :HEAD] = grad_keys
        g_all[layer, :, HEAD:] = grad_values
        if layer == 0 and not need_up:
            continue
        grads = jnp.concatenate([grad_query, grad_keys, grad_values], axis=1)
        inverse = inverse_norm(h_all, layer)
        total = jnp.zeros((LENGTH, 1), F32)
        for at in range(0, WIDTH, CHUNK):
            part = dot_nt(grads, weight_rows(w_vmem, layer, at, 0, KVW))
            gn[:, at : at + CHUNK] = part
            signal = h_all[layer, :, at : at + CHUNK].astype(F32)
            total = total + jnp.sum(part * signal, axis=-1, keepdims=True)
        pull = inverse * inverse * inverse * (total * (1.0 / WIDTH))
        for at in range(0, WIDTH, CHUNK):
            signal = h_all[layer, :, at : at + CHUNK].astype(F32)
            upstream = out_ref[:, at : at + CHUNK].astype(F32)
            out_ref[:, at : at + CHUNK] = (
                upstream + inverse * gn[:, at : at + CHUNK] - signal * pull
            ).astype(BF16)


VM = pl.BlockSpec(memory_space=pltpu.VMEM)
ANY = pl.BlockSpec(memory_space=pl.ANY)
WEIGHT_SCRATCH = pltpu.VMEM((LAYERS, 16, 4, 64, COLS), BF16)
WEIGHT_SEMS = pltpu.SemaphoreType.DMA((LAYERS, 16))
STATE_SHAPES = (
    jax.ShapeDtypeStruct((LAYERS, LENGTH, WIDTH), BF16),
    jax.ShapeDtypeStruct((LAYERS, LENGTH, WIDTH), BF16),
    jax.ShapeDtypeStruct((LAYERS, LENGTH * HEADS, HEAD), BF16),
    jax.ShapeDtypeStruct((LAYERS, LENGTH, HEAD), BF16),
    jax.ShapeDtypeStruct((LAYERS, LENGTH, HEAD), BF16),
    jax.ShapeDtypeStruct((LAYERS, LENGTH * HEADS, LENGTH), F32),
)


def cost(products):
    return pl.CostEstimate(
        flops=products * 2 * LENGTH * WIDTH * COLS,
        bytes_accessed=LAYERS * WIDTH * COLS * 2,
        transcendentals=0,
    )


def run_forward(h, seg_col, seg_row, weights):
    return pl.pallas_call(
        forward_kernel,
        out_shape=(jax.ShapeDtypeStruct((LENGTH, WIDTH), BF16),) + STATE_SHAPES,
        in_specs=[VM, VM, VM, ANY],
        out_specs=(VM,) * 7,
        scratch_shapes=[WEIGHT_SCRATCH, WEIGHT_SEMS],
        compiler_params=pltpu.CompilerParams(vmem_limit_bytes=VMEM_LIMIT),
        cost_estimate=cost(LAYERS),
        name="layers_forward",
    )(h, seg_col, seg_row, weights)


def run_backward(upstream, states, weights, need_up):
    h_all, n_all, q_all, k_all, v_all, p_all = states
    return pl.pallas_call(
        functools.partial(backward_kernel, need_up),
        out_shape=(
            jax.ShapeDtypeStruct((LENGTH, WIDTH), BF16),
            jax.ShapeDtypeStruct((LAYERS, LENGTH, 2 * HEAD), BF16),
        ),
        in_specs=[VM] * 6 + [ANY],
        out_specs=(VM, VM),
        scratch_shapes=[WEIGHT_SCRATCH, pltpu.VMEM((LENGTH, WIDTH), F32), WEIGHT_SEMS],
        compiler_params=pltpu.CompilerParams(vmem_limit_bytes=VMEM_LIMIT),
        cost_estimate=cost(LAYERS),
        name="layers_backward",
    )(upstream, h_all, q_all, k_all, v_all, p_all, weights)


def reorder(rows):
    split = rows.reshape(LENGTH, 4, 4, 2, 2, 64)
    return split.transpose(0, 4, 3, 2, 1, 5).reshape(LENGTH, WIDTH)


def swap(block, axis):
    return lax.ppermute(block, axis, [(0, 1), (1, 0)])


def turned(block, axis, distance):
    return lax.ppermute(block, axis, [(i, (i + distance) % 4) for i in range(4)])


def pick(block, index, size, axis):
    return lax.dynamic_slice_in_dim(block, index * size, size, axis)


def to_layer(block):
    me = lax.axis_index("x")
    parts = [pick(block, me, 1, 0)]
    for distance in range(1, 4):
        parts.append(turned(pick(block, (me + distance) % 4, 1, 0), "x", distance))
    return jnp.concatenate(parts, axis=0)


def shards(
    inputs, out_grad, doc_ids, query_weight, out_weight, master, first_moment, second_moment
):
    yh, x = lax.axis_index("yh"), lax.axis_index("x")
    z1, z2, yl, c = (lax.axis_index(name) for name in DP)
    own = jnp.concatenate(
        [
            query_weight[0],
            master[0, 0].astype(BF16),
            master[0, 1].astype(BF16),
            out_weight[0],
        ],
        axis=1,
    )
    with jax.named_scope("gather_weights"):
        own = lax.all_gather(own, "x", axis=0)
        weights = lax.all_gather(own, DP, axis=0)
        weights = weights.reshape(4, 4, 2, 2, LAYERS, 64, COLS)

    rows_in = reorder(lax.dynamic_index_in_dim(inputs, x, 0, keepdims=False))
    up_in = reorder(lax.dynamic_index_in_dim(out_grad, x, 0, keepdims=False))
    segment = lax.dynamic_index_in_dim(doc_ids, x, 0, keepdims=False)
    seg_col, seg_row = segment[:, None], segment[None, :]

    first_half = run_forward(rows_in, seg_col, seg_row, weights)[0]
    arrived = swap(first_half, "yh")
    layer_in = jnp.where(yh == 1, arrived, rows_in)
    states = run_forward(layer_in, seg_col, seg_row, weights)[1:]

    half_up = run_backward(up_in, states, weights, True)[0]
    arrived = swap(half_up, "yh")
    upstream = jnp.where(yh == 0, arrived, up_in)
    grads = run_backward(upstream, states, weights, False)[1]

    with jax.named_scope("normed_slices"):
        rows = to_layer(states[1]).reshape(1, 4 * LENGTH, WIDTH)
        half = WIDTH // 2
        rows = jnp.concatenate(
            [pick(rows, c, half, 2), swap(pick(rows, 1 - c, half, 2), "c")], axis=0
        )
        half = half // 2
        rows = jnp.concatenate(
            [pick(rows, yl, half, 2), swap(pick(rows, 1 - yl, half, 2), "yl")], axis=0
        )
        quarter = half // 4
        parts = [pick(rows, z2, quarter, 2)]
        for distance in range(1, 4):
            parts.append(turned(pick(rows, (z2 + distance) % 4, quarter, 2), "z2", distance))
        rows = jnp.concatenate(parts, axis=0).reshape(-1, quarter)

    with jax.named_scope("gather_grads"):
        cols = to_layer(grads).reshape(1, 4 * LENGTH, 2 * HEAD)
        cols = jnp.concatenate([cols, swap(cols, "c")], axis=0)
        cols = jnp.concatenate([cols, swap(cols, "yl")], axis=0)
        parts = [cols] + [turned(cols, "z2", distance) for distance in range(1, 4)]
        cols = jnp.concatenate(parts, axis=0).reshape(-1, 2 * HEAD)

    with jax.named_scope("sum_grads"):
        partial = dot_tn(rows, cols)
        grad = pick(partial, z1, 64, 0)
        for distance in range(1, 4):
            grad = grad + turned(pick(partial, (z1 + distance) % 4, 64, 0), "z1", distance)
        grad = jnp.stack([grad[:, :HEAD], grad[:, HEAD:]])

    with jax.named_scope("clip"):
        total_sq = jnp.full((8, 128), jnp.sum(grad * grad))
        for axes in (("yl", "c"), "x", "z2", "z1", "yh"):
            total_sq = jnp.sum(lax.all_gather(total_sq, axes, axis=0), axis=0)
        factor = jnp.minimum(1.0, CLIP_NORM / jnp.sqrt(total_sq[0, 0]))
    clipped = grad * factor
    first_new = BETA_FIRST * first_moment[0] + (1.0 - BETA_FIRST) * clipped
    second_new = BETA_SECOND * second_moment[0] + (1.0 - BETA_SECOND) * clipped * clipped
    adam_step = first_new / (jnp.sqrt(second_new) + ADAM_EPSILON)
    fresh_shard = (master[0] - LEARN_RATE * adam_step).astype(BF16)
    return (adam_step[None], fresh_shard[None])


def solution(mesh):
    fine = Mesh(mesh.devices.reshape(tuple(FINE.values())), tuple(FINE))
    section = ("yh", "x")
    placed = (
        P(None, DP, None),
        P(None, DP, None),
        P(None, DP),
        P(section, DP, None),
        P(section, DP, None),
        P(section, None, DP, None),
        P(section, None, DP, None),
        P(section, None, DP, None),
    )
    return jax.shard_map(
        shards,
        mesh=fine,
        in_specs=placed,
        out_specs=(P(section, None, DP, None), P(section, None, DP, None)),
        check_vma=False,
    )
```

time: 1400 us -> 566 us (0.40)
  waiting for transfers between devices: 947 us -> 303 us
  other arithmetic: 103 us -> 6.02 us
  matrix products: 92.2 us -> 0.44 us
  Pallas kernels: 0 us -> 74.9 us
  blocking collectives: 106 us -> 59.4 us
  local copies, waits for them, and re-layouts: 33.6 us -> 13.6 us
  starting transfers between devices: 99.6 us -> 83.4 us
    all_gather x4 -> x1, waiting for transfers between devices: 492 us -> 241 us  [shards(): weights = lax.all_gather(own, DP, axis=0)]
    reduce_scatter x1 -> x0, waiting for transfers between devices: 241 us -> none  [shards(): lax.psum_scatter(grad_acc, 'dp', scatter_dimension=1, tiled=True)]
    ppermute x22 -> x21, waiting for transfers between devices: 212 us -> 61.6 us  [the longest x15 42.4 us: turned(): lax.ppermute(block, axis, [(i, (i + distance) % 4) for i in range(4)])]
    psum x1 -> x0, blocking collectives: 106 us -> none  [shards(): total_sq = lax.psum(local_sq, ('section', 'dp'))]
    dot_general x68 -> x1, matrix products: 92.2 us -> 0.44 us  [dot_tn(): lax.dot_general(a, b, (((0,), (0,)), ((), ())), preferred_element_type=F32)]
    pallas_call x0 -> x4, Pallas kernels: none -> 74.9 us  [the longest x2 38.2 us: run_forward(): pl.pallas_call(forward_kernel, out_shape=(jax.ShapeDtypeStruct((LENGTH, W...]
    add x11 -> x1, other arithmetic: 63.1 us -> 0.02 us  [shards(): grad + turned(pick(partial, (z1 + distance) % 4, 64, 0), 'z1', distance)]
    all_gather x0 -> x5, blocking collectives: none -> 51.1 us  [the longest x4 38.4 us: shards(): total_sq = jnp.sum(lax.all_gather(total_sq, axes, axis=0), axis=0)]
  transfers between devices with their start and end apart: 27 -> 22, of which waited for: 27 -> 9; matrix products, arithmetic and copies ran while one was open for 5% -> 2% of each run, Pallas kernels for 0% -> 7%
where the time goes in v1:
time: 566 us; the launch traced here: 556 us
  waiting for transfers between devices  303 us (54%)
  starting transfers between devices  83.4 us (15%)
  Pallas kernels  74.9 us (13%)
  blocking collectives  59.4 us (10%)
  between operations  15.4 us (3%)
  local copies, waits for them, and re-layouts  13.6 us (2%)
  other arithmetic  6.02 us (1%)
    all_gather x1, waiting for transfers between devices, shards(): weights = lax.all_gather(own, DP, axis=0)  241 us
    ppermute x15, starting transfers between devices, turned(): lax.ppermute(block, axis, [(i, (i + distance) % 4) for i in range(4)])  57.7 us
    ppermute x15, waiting for transfers between devices, turned(): lax.ppermute(block, axis, [(i, (i + distance) % 4) for i in range(4)])  42.4 us
    all_gather x4, blocking collectives, shards(): total_sq = jnp.sum(lax.all_gather(total_sq, axes, axis=0), axis=0)  38.4 us
    pallas_call x2, Pallas kernels, run_forward(): pl.pallas_call(forward_kernel, out_shape=(jax.ShapeDtypeStruct((LENGTH, W...  38.2 us
    pallas_call x2, Pallas kernels, run_backward(): pl.pallas_call(functools.partial(backward_kernel, need_up), out_shape=(ja...  36.7 us
    ppermute x6, starting transfers between devices, swap(): return lax.ppermute(block, axis, [(0, 1), (1, 0)])  25.7 us
    ppermute x6, waiting for transfers between devices, swap(): return lax.ppermute(block, axis, [(0, 1), (1, 0)])  19.2 us
  transfers between devices with their start and end apart: 22, of which 9 were waited for; matrix products, arithmetic and copies ran while one was open for 2% of the time, Pallas kernels for 7%

profile of v1, /device:TPU:1, one launch (start us, length us, event | category | flops | bytes accessed | tf_op | source)
XLA Modules:
  0.0 556.1 jit_solution(15705882562095013458)
XLA Ops:
  9.1 12.7 %all-gather = bf16[256,1280]{1,0:T(8,128)(2,1)} all-gather(bf16[64,1280]{1,0:T(8,128)(2,1)S(1)} %pad_maximum_fusion.2), channel_id=3, replica_groups=mesh['yh'=2,'x'=4,'z1'=4,'z2'=4,'yl'=2,'c'=2] {'x'}, dimensions={0}, use_global_device_ids=true | all-gather | bytes 819200 | tf_op jit(solution)/shard_map/gather_weights/all_gather | solution.py:264
  26.4 241.3 %all-gather.8.cloned.1.call-done = bf16[256,64,1280]{2,1,0:T(8,128)(2,1)} async-done(((bf16[4,64,1280]{2,1,0:T(8,128)(2,1)}), bf16[256,64,1280]{2,1,0:T(8,128)(2,1)}) %all-gather.8.cloned.1.call-update) | async-done | bytes 41943056 | tf_op jit(solution)/shard_map/gather_weights/all_gather | solution.py:265
  267.8 19.1 %layers_forward.2 = (bf16[32,4096]{1,0:T(8,128)(2,1)}, bf16[4,32,4096]{2,1,0:T(8,128)(2,1)}, bf16[4,32,4096]{2,1,0:T(8,128)(2,1)}, bf16[4,128,128]{2,1,0:T(8,128...) custom-call(bf16[32,4096]{1,0:T(8,128)(2,1)} %reshape.92.h_ref, ...), custom_call_target="tpu_custom_call" | custom-call | flops 1342177280 | bytes 41943040 | tf_op jit(solution)/shard_map/layers_forward/pallas_call | solution.py:195
  286.9 4.8 collective-permute-start
  291.7 6.4 %collective-permute-done = bf16[32,4096]{1,0:T(8,128)(2,1)S(1)} collective-permute-done((bf16[32,4096]{1,0:T(8,128)(2,1)}, bf16[32,4096]{1,0:T(8,128)(2,1)S(1)}, u32[]{:S(2)}, u32[]{:S(2)}) %collective-permute-start) | collective-permute-done | bytes 262176 | tf_op jit(solution)/shard_map/ppermute | solution.py:230
  298.8 19.1 %layers_forward.3 = (bf16[32,4096]{1,0:T(8,128)(2,1)}, bf16[4,32,4096]{2,1,0:T(8,128)(2,1)}, bf16[4,32,4096]{2,1,0:T(8,128)(2,1)}, bf16[4,128,128]{2,1,0:T(8,128...) custom-call(bf16[32,4096]{1,0:T(8,128)(2,1)} %broadcast_select_fusion.1.h_ref, ...), custom_call_target="tpu_custom_call" | custom-call | flops 1342177280 | bytes 41943040 | tf_op jit(solution)/shard_map/layers_forward/pallas_call | solution.py:195
  331.7 19.4 %layers_backward.2 = (bf16[32,4096]{1,0:T(8,128)(2,1)}, bf16[4,32,256]{2,1,0:T(8,128)(2,1)}) custom-call(bf16[32,4096]{1,0:T(8,128)(2,1)} %reshape.96.up_ref, bf16[4,32,4096]{2,1,0:T(8,128)(2,1)} %get-tuple-element.13.h_all, bf16[4,128,128]{2,1,0:T(8,128)(2,1)} %get-tuple-element.14.q_all, bf16[4,32,128]{2,1,0:T(8,128)(2,1)} %get-tuple-element.15.k_all, ...), custom_call_target="tpu_custom_call" | custom-call | flops 1342177280 | bytes 41943040 | tf_op jit(solution)/shard_map/layers_backward/pallas_call | solution.py:209
  351.2 4.8 collective-permute-start.9
  362.6 17.3 %layers_backward.3 = (bf16[32,4096]{1,0:T(8,128)(2,1)}, bf16[4,32,256]{2,1,0:T(8,128)(2,1)}) custom-call(bf16[32,4096]{1,0:T(8,128)(2,1)} %broadcast_select_fusion.up_ref, bf16[4,32,4096]{2,1,0:T(8,128)(2,1)} %get-tuple-element.13.h_all, bf16[4,128,128]{2,1,0:T(8,128)(2,1)} %get-tuple-element.14.q_all, bf16[4,32,128]{2,1,0:T(8,128)(2,1)} %get-tuple-element.15.k_all, ...), custom_call_target="tpu_custom_call" | custom-call | flops 1342177280 | bytes 41943040 | tf_op jit(solution)/shard_map/layers_backward/pallas_call | solution.py:209
  393.5 6.4 %collective-permute-start.13 = (bf16[1,128,256]{2,1,0:T(8,128)(2,1)S(1)}, bf16[1,128,256]{2,1,0:T(8,128)(2,1)S(1)}, u32[]{:S(2)}, u32[]{:S(2)}) collective-permute-start(bf16[1,128,256]{2,1,0:T(8,128)(2,1)S(1)} %bitcast.46), channel_id=1, source_target_pairs={{0,1},{1,0},{2,3},{3,2},{4,5},{5,4},{6,7},{7,6},{8,9},{9,8},{10,11... | collective-permute-start | bytes 196616 | tf_op jit(solution)/shard_map/gather_grads/ppermute | solution.py:230
  405.5 12.8 %collective-permute-done.14 = bf16[2,128,256]{2,1,0:T(8,128)(2,1)S(1)} collective-permute-done((bf16[2,128,256]{2,1,0:T(8,128)(2,1)S(1)}, bf16[2,128,256]{2,1,0:T(8,128)(2,1)S(1)}, u32[]{:S(2)}, u32[]{:S(2)}) %collective-permute-start.14) | collective-permute-done | bytes 131104 | tf_op jit(solution)/shard_map/gather_grads/ppermute | solution.py:230
  421.5 5.4 collective-permute-start.16
  437.4 5.3 collective-permute-done.16
  442.8 4.7 collective-permute-done.8
  447.5 23.3 %collective-permute-done.7 = bf16[4,128,256]{1,2,0:T(8,128)(2,1)S(1)} collective-permute-done((bf16[4,128,256]{1,2,0:T(8,128)(2,1)S(1)}, bf16[4,128,256]{1,2,0:T(8,128)(2,1)S(1)}, u32[]{:S(2)}, u32[]{:S(2)}) %collective-permute-start.7) | collective-permute-done | bytes 262176 | tf_op jit(solution)/shard_map/normed_slices/ppermute | solution.py:234
  471.3 7.8 %collective-permute-start.20 = (f32[64,256]{1,0:T(8,128)S(1)}, f32[64,256]{1,0:T(8,128)S(1)}, u32[]{:S(2)}, u32[]{:S(2)}) collective-permute-start(f32[64,256]{1,0:T(8,128)S(1)} %get-tuple-element.35), channel_id=1, source_target_pairs={{0,48},{16,0},{32,16},{48,32},{1,49},{17,1},{33,17},{49,33},{2,50}... | collective-permute-start | bytes 196616 | tf_op jit(solution)/shard_map/sum_grads/ppermute | solution.py:234
  479.1 7.3 %collective-permute-start.19 = (f32[64,256]{1,0:T(8,128)S(1)}, f32[64,256]{1,0:T(8,128)S(1)}, u32[]{:S(2)}, u32[]{:S(2)}) collective-permute-start(f32[64,256]{1,0:T(8,128)S(1)} %get-tuple-element.36), channel_id=1, source_target_pairs={{0,32},{16,48},{32,0},{48,16},{1,33},{17,49},{33,1},{49,17},{2,34}... | collective-permute-start | bytes 196616 | tf_op jit(solution)/shard_map/sum_grads/ppermute | solution.py:234
  486.4 5.3 collective-permute-start.18
  492.9 5.5 collective-permute-done.19
  500.6 8.3 %all-reduce = f32[4]{0:T(128)S(1)} all-reduce(f32[4]{0:T(128)S(1)} %dynamic-update-slice), channel_id=2, replica_groups=mesh['yh'=2,'x'=4,'z1'=4,'z2'=4,'yl'=2,'c'=2] {'yl','c'}, use_global_device_ids=true, to_apply=%add | all-reduce | flops 4 | bytes 32
  508.9 9.0 %all-gather.2 = f32[32,128]{1,0:T(8,128)S(1)} all-gather(f32[8,128]{1,0:T(8,128)S(1)} %broadcast_reduce_fusion), channel_id=5, replica_groups=mesh['yh'=2,'x'=4,'z1'=4,'z2'=4,'yl'=2,'c'=2] {'x'}, dimensions={0}, use_global_device_ids=true | all-gather | bytes 20480 | tf_op jit(solution)/shard_map/clip/all_gather | solution.py:316
  517.9 10.2 %all-gather.3 = f32[32,128]{1,0:T(8,128)S(1)} all-gather(f32[8,128]{1,0:T(8,128)S(1)} %bitcast_reduce_fusion.2), channel_id=6, replica_groups=mesh['yh'=2,'x'=4,'z1'=4,'z2'=4,'yl'=2,'c'=2] {'z2'}, dimensions={0}, use_global_device_ids=true | all-gather | bytes 20480 | tf_op jit(solution)/shard_map/clip/all_gather | solution.py:316
  528.2 14.4 %all-gather.4 = f32[32,128]{1,0:T(8,128)S(1)} all-gather(f32[8,128]{1,0:T(8,128)S(1)} %bitcast_reduce_fusion.1), channel_id=7, replica_groups=mesh['yh'=2,'x'=4,'z1'=4,'z2'=4,'yl'=2,'c'=2] {'z1'}, dimensions={0}, use_global_device_ids=true | all-gather | bytes 20480 | tf_op jit(solution)/shard_map/clip/all_gather | solution.py:316
  542.6 4.7 all-gather.5
  (93 shorter events, 65.2 us)
Async XLA Ops:
  7.2 260.6 %all-gather.8.cloned.1.call-start = ((), (), s32[]{:S(2)}) async-start(), calls=%async_computation | async-start | bytes 42598400 | tf_op jit(solution)/shard_map/gather_weights/all_gather | solution.py:265
  23.8 274.3 %copy-start.3 = (bf16[32,4096]{1,0:T(8,128)(2,1)S(1)}, bf16[32,4096]{1,0:T(8,128)(2,1)}, u32[]{:S(2)}) copy-start(bf16[32,4096]{1,0:T(8,128)(2,1)} %reshape.92.h_ref) | copy-start | bytes 786436
  286.9 11.3 %collective-permute-start = (bf16[32,4096]{1,0:T(8,128)(2,1)}, bf16[32,4096]{1,0:T(8,128)(2,1)S(1)}, u32[]{:S(2)}, u32[]{:S(2)}) collective-permute-start(bf16[32,4096]{1,0:T(8,128)(2,1)} %get-tuple-element.11), channel_id=1, source_target_pairs={{0,256},{256,0},{1,257},{257,1},{2,258},{258,2},{3,259},{259,3},{4... | collective-permute-start | bytes 786440 | tf_op jit(solution)/shard_map/ppermute | solution.py:230
  319.2 36.8 %collective-permute-start.3 = (bf16[1,32,4096]{2,1,0:T(8,128)(2,1)S(1)}, bf16[1,32,4096]{2,1,0:T(8,128)(2,1)S(1)}, u32[]{:S(2)}, u32[]{:S(2)}) collective-permute-start(bf16[1,32,4096]{2,1,0:T(8,128)(2,1)S(1)} %get-tuple-element.31), channel_id=1, source_target_pairs={{0,192},{64,0},{128,64},{192,128},{1,193},{65,1},{129,65},{193,129... | collective-permute-start | bytes 786440 | tf_op jit(solution)/shard_map/normed_slices/ppermute | solution.py:234
  323.5 32.5 %collective-permute-start.2 = (bf16[1,32,4096]{2,1,0:T(8,128)(2,1)S(1)}, bf16[1,32,4096]{2,1,0:T(8,128)(2,1)S(1)}, u32[]{:S(2)}, u32[]{:S(2)}) collective-permute-start(bf16[1,32,4096]{2,1,0:T(8,128)(2,1)S(1)} %get-tuple-element.32), channel_id=1, source_target_pairs={{0,128},{64,192},{128,0},{192,64},{1,129},{65,193},{129,1},{193,65... | collective-permute-start | bytes 786440 | tf_op jit(solution)/shard_map/normed_slices/ppermute | solution.py:234
  326.0 30.0 %collective-permute-start.1 = (bf16[1,32,4096]{2,1,0:T(8,128)(2,1)S(1)}, bf16[1,32,4096]{2,1,0:T(8,128)(2,1)S(1)}, u32[]{:S(2)}, u32[]{:S(2)}) collective-permute-start(bf16[1,32,4096]{2,1,0:T(8,128)(2,1)S(1)} %get-tuple-element.33), channel_id=1, source_target_pairs={{0,64},{64,128},{128,192},{192,0},{1,65},{65,129},{129,193},{193,1... | collective-permute-start | bytes 786440 | tf_op jit(solution)/shard_map/normed_slices/ppermute | solution.py:234
  331.7 217.5 %copy-start.1 = (bf16[4,32,4096]{2,1,0:T(8,128)(2,1)S(1)}, bf16[4,32,4096]{2,1,0:T(8,128)(2,1)}, u32[]{:S(2)}) copy-start(bf16[4,32,4096]{2,1,0:T(8,128)(2,1)} %param.8) | copy-start | bytes 3145732
  351.2 9.7 %collective-permute-start.9 = (bf16[32,4096]{1,0:T(8,128)(2,1)}, bf16[32,4096]{1,0:T(8,128)(2,1)}, u32[]{:S(2)}, u32[]{:S(2)}) collective-permute-start(bf16[32,4096]{1,0:T(8,128)(2,1)} %get-tuple-element.18), channel_id=1, source_target_pairs={{0,256},{256,0},{1,257},{257,1},{2,258},{258,2},{3,259},{259,3},{4... | collective-permute-start | bytes 786440 | tf_op jit(solution)/shard_map/ppermute | solution.py:230
  356.5 43.4 %collective-permute-start.4 = (bf16[1,128,2048]{1,2,0:T(8,128)(2,1)S(1)}, bf16[1,128,2048]{1,2,0:T(8,128)(2,1)S(1)}, u32[]{:S(2)}, u32[]{:S(2)}) collective-permute-start(bf16[1,128,2048]{1,2,0:T(8,128)(2,1)S(1)} %copy.33), channel_id=1, source_target_pairs={{0,1},{1,0},{2,3},{3,2},{4,5},{5,4},{6,7},{7,6},{8,9},{9,8},{10,11... | collective-permute-start | bytes 1572872 | tf_op jit(solution)/shard_map/normed_slices/ppermute | solution.py:230
  380.7 9.3 %collective-permute-start.12 = (bf16[1,32,256]{2,1,0:T(8,128)(2,1)S(1)}, bf16[1,32,256]{2,1,0:T(8,128)(2,1)S(1)}, u32[]{:S(2)}, u32[]{:S(2)}) collective-permute-start(bf16[1,32,256]{2,1,0:T(8,128)(2,1)S(1)} %get-tuple-element.42), channel_id=1, source_target_pairs={{0,192},{64,0},{128,64},{192,128},{1,193},{65,1},{129,65},{193,129... | collective-permute-start | bytes 49160 | tf_op jit(solution)/shard_map/gather_grads/ppermute | solution.py:234
  384.7 6.0 %collective-permute-start.11 = (bf16[1,32,256]{2,1,0:T(8,128)(2,1)S(1)}, bf16[1,32,256]{2,1,0:T(8,128)(2,1)S(1)}, u32[]{:S(2)}, u32[]{:S(2)}) collective-permute-start(bf16[1,32,256]{2,1,0:T(8,128)(2,1)S(1)} %get-tuple-element.43), channel_id=1, source_target_pairs={{0,128},{64,192},{128,0},{192,64},{1,129},{65,193},{129,1},{193,65... | collective-permute-start | bytes 49160 | tf_op jit(solution)/shard_map/gather_grads/ppermute | solution.py:234
  387.8 5.7 %collective-permute-start.10 = (bf16[1,32,256]{2,1,0:T(8,128)(2,1)S(1)}, bf16[1,32,256]{2,1,0:T(8,128)(2,1)S(1)}, u32[]{:S(2)}, u32[]{:S(2)}) collective-permute-start(bf16[1,32,256]{2,1,0:T(8,128)(2,1)S(1)} %get-tuple-element.44), channel_id=1, source_target_pairs={{0,64},{64,128},{128,192},{192,0},{1,65},{65,129},{129,193},{193,1... | collective-permute-start | bytes 49160 | tf_op jit(solution)/shard_map/gather_grads/ppermute | solution.py:234
  393.5 9.6 %collective-permute-start.13 = (bf16[1,128,256]{2,1,0:T(8,128)(2,1)S(1)}, bf16[1,128,256]{2,1,0:T(8,128)(2,1)S(1)}, u32[]{:S(2)}, u32[]{:S(2)}) collective-permute-start(bf16[1,128,256]{2,1,0:T(8,128)(2,1)S(1)} %bitcast.46), channel_id=1, source_target_pairs={{0,1},{1,0},{2,3},{3,2},{4,5},{5,4},{6,7},{7,6},{8,9},{9,8},{10,11... | collective-permute-start | bytes 196616 | tf_op jit(solution)/shard_map/gather_grads/ppermute | solution.py:230
  400.1 28.8 %collective-permute-start.5 = (bf16[2,128,1024]{1,2,0:T(8,128)(2,1)S(1)}, bf16[2,128,1024]{1,2,0:T(8,128)(2,1)S(1)}, u32[]{:S(2)}, u32[]{:S(2)}) collective-permute-start(bf16[2,128,1024]{1,2,0:T(8,128)(2,1)S(1)} %get-tuple-element.26), channel_id=1, source_target_pairs={{0,2},{2,0},{1,3},{3,1},{4,6},{6,4},{5,7},{7,5},{8,10},{10,8},{9,1... | collective-permute-start | bytes 1572872 | tf_op jit(solution)/shard_map/normed_slices/ppermute | solution.py:230
  403.1 15.2 %collective-permute-start.14 = (bf16[2,128,256]{2,1,0:T(8,128)(2,1)S(1)}, bf16[2,128,256]{2,1,0:T(8,128)(2,1)S(1)}, u32[]{:S(2)}, u32[]{:S(2)}) collective-permute-start(bf16[2,128,256]{2,1,0:T(8,128)(2,1)S(1)} %pad_maximum_fusion.3), channel_id=1, source_target_pairs={{0,2},{2,0},{1,3},{3,1},{4,6},{6,4},{5,7},{7,5},{8,10},{10,8},{9,1... | collective-permute-start | bytes 393224 | tf_op jit(solution)/shard_map/gather_grads/ppermute | solution.py:230
  418.3 17.1 %collective-permute-start.15 = (bf16[4,128,256]{2,1,0:T(8,128)(2,1)S(1)}, bf16[4,128,256]{2,1,0:T(8,128)(2,1)S(1)}, u32[]{:S(2)}, u32[]{:S(2)}) collective-permute-start(bf16[4,128,256]{2,1,0:T(8,128)(2,1)S(1)} %pad_maximum_fusion.1), channel_id=1, source_target_pairs={{0,4},{4,8},{8,12},{12,0},{1,5},{5,9},{9,13},{13,1},{2,6},{6,10},{... | collective-permute-start | bytes 786440 | tf_op jit(solution)/shard_map/gather_grads/ppermute | solution.py:234
  421.5 21.2 %collective-permute-start.16 = (bf16[4,128,256]{2,1,0:T(8,128)(2,1)S(1)}, bf16[4,128,256]{2,1,0:T(8,128)(2,1)S(1)}, u32[]{:S(2)}, u32[]{:S(2)}) collective-permute-start(bf16[4,128,256]{2,1,0:T(8,128)(2,1)S(1)} %pad_maximum_fusion.1), channel_id=1, source_target_pairs={{0,8},{4,12},{8,0},{12,4},{1,9},{5,13},{9,1},{13,5},{2,10},{6,14},... | collective-permute-start | bytes 786440 | tf_op jit(solution)/shard_map/gather_grads/ppermute | solution.py:234
  426.9 15.8 %collective-permute-start.17 = (bf16[4,128,256]{2,1,0:T(8,128)(2,1)S(1)}, bf16[4,128,256]{2,1,0:T(8,128)(2,1)S(1)}, u32[]{:S(2)}, u32[]{:S(2)}) collective-permute-start(bf16[4,128,256]{2,1,0:T(8,128)(2,1)S(1)} %pad_maximum_fusion.1), channel_id=1, source_target_pairs={{0,12},{4,0},{8,4},{12,8},{1,13},{5,1},{9,5},{13,9},{2,14},{6,2},{... | collective-permute-start | bytes 786440 | tf_op jit(solution)/shard_map/gather_grads/ppermute | solution.py:234
  429.0 18.5 %collective-permute-start.8 = (bf16[4,128,256]{1,2,0:T(8,128)(2,1)S(1)}, bf16[4,128,256]{1,2,0:T(8,128)(2,1)S(1)}, u32[]{:S(2)}, u32[]{:S(2)}) collective-permute-start(bf16[4,128,256]{1,2,0:T(8,128)(2,1)S(1)} %get-tuple-element.25), channel_id=1, source_target_pairs={{0,12},{4,0},{8,4},{12,8},{1,13},{5,1},{9,5},{13,9},{2,14},{6,2},{... | collective-permute-start | bytes 786440 | tf_op jit(solution)/shard_map/normed_slices/ppermute | solution.py:234
  432.1 38.7 %collective-permute-start.7 = (bf16[4,128,256]{1,2,0:T(8,128)(2,1)S(1)}, bf16[4,128,256]{1,2,0:T(8,128)(2,1)S(1)}, u32[]{:S(2)}, u32[]{:S(2)}) collective-permute-start(bf16[4,128,256]{1,2,0:T(8,128)(2,1)S(1)} %get-tuple-element.24), channel_id=1, source_target_pairs={{0,8},{4,12},{8,0},{12,4},{1,9},{5,13},{9,1},{13,5},{2,10},{6,14},... | collective-permute-start | bytes 786440 | tf_op jit(solution)/shard_map/normed_slices/ppermute | solution.py:234
  435.5 35.4 %collective-permute-start.6 = (bf16[4,128,256]{1,2,0:T(8,128)(2,1)S(1)}, bf16[4,128,256]{1,2,0:T(8,128)(2,1)S(1)}, u32[]{:S(2)}, u32[]{:S(2)}) collective-permute-start(bf16[4,128,256]{1,2,0:T(8,128)(2,1)S(1)} %get-tuple-element.23), channel_id=1, source_target_pairs={{0,4},{4,8},{8,12},{12,0},{1,5},{5,9},{9,13},{13,1},{2,6},{6,10},{... | collective-permute-start | bytes 786440 | tf_op jit(solution)/shard_map/normed_slices/ppermute | solution.py:234
  471.3 21.6 %collective-permute-start.20 = (f32[64,256]{1,0:T(8,128)S(1)}, f32[64,256]{1,0:T(8,128)S(1)}, u32[]{:S(2)}, u32[]{:S(2)}) collective-permute-start(f32[64,256]{1,0:T(8,128)S(1)} %get-tuple-element.35), channel_id=1, source_target_pairs={{0,48},{16,0},{32,16},{48,32},{1,49},{17,1},{33,17},{49,33},{2,50}... | collective-permute-start | bytes 196616 | tf_op jit(solution)/shard_map/sum_grads/ppermute | solution.py:234
  479.1 19.4 %collective-permute-start.19 = (f32[64,256]{1,0:T(8,128)S(1)}, f32[64,256]{1,0:T(8,128)S(1)}, u32[]{:S(2)}, u32[]{:S(2)}) collective-permute-start(f32[64,256]{1,0:T(8,128)S(1)} %get-tuple-element.36), channel_id=1, source_target_pairs={{0,32},{16,48},{32,0},{48,16},{1,33},{17,49},{33,1},{49,17},{2,34}... | collective-permute-start | bytes 196616 | tf_op jit(solution)/shard_map/sum_grads/ppermute | solution.py:234
  486.4 12.1 %collective-permute-start.18 = (f32[64,256]{1,0:T(8,128)S(1)}, f32[64,256]{1,0:T(8,128)S(1)}, u32[]{:S(2)}, u32[]{:S(2)}) collective-permute-start(f32[64,256]{1,0:T(8,128)S(1)} %get-tuple-element.34), channel_id=1, source_target_pairs={{0,16},{16,32},{32,48},{48,0},{1,17},{17,33},{33,49},{49,1},{2,18}... | collective-permute-start | bytes 196616 | tf_op jit(solution)/shard_map/sum_grads/ppermute | solution.py:234
  (5 other events, 636.0 us)
Sparse Core Ops, SparseCore 0:
  21.9 245.7 all-gather.7

commit v2 on v1

--- a/solution.py
+++ b/solution.py
@@ -15,8 +15,9 @@
 LEARN_RATE = 0.001
 CLIP_NORM = 1.0
 
-FINE = {"yh": 2, "x": 4, "z1": 4, "z2": 4, "yl": 2, "c": 2}
-DP = ("z1", "z2", "yl", "c")
+FINE = {"yh": 2, "x": 4, "z": 16, "yl": 2, "c": 2}
+DP = ("z", "yl", "c")
+PLANE = ("x", "yl", "c")
 LAYERS = 4
 LENGTH = 32
 WIDTH = 4096
@@ -48,13 +49,12 @@
     copies = []
     for c in range(2):
         for yl in range(2):
-            for z2 in range(4):
-                at = (c * 2 + yl) * 4 + z2
-                copies.append(
-                    pltpu.make_async_copy(
-                        w_hbm.at[:, z2, yl, c, layer], w_vmem.at[layer, at], sems.at[layer, at]
-                    )
+            at = c * 2 + yl
+            copies.append(
+                pltpu.make_async_copy(
+                    w_hbm.at[:, yl, c, layer], w_vmem.at[layer, at], sems.at[layer, at]
                 )
+            )
     return copies
 
 
@@ -75,9 +75,7 @@
 
 
 def weight_rows(w_vmem, layer, at, first, last):
-    per = CHUNK // 256
-    block = w_vmem[layer, at // 256 : at // 256 + per, :, :, first:last]
-    return block.reshape(CHUNK, last - first)
+    return w_vmem[layer, at // CHUNK, :, :, first:last].reshape(CHUNK, last - first)
 
 
 def forward_kernel(
@@ -96,10 +94,10 @@
         for at in range(0, WIDTH, CHUNK):
             signal = h_all[layer, :, at : at + CHUNK].astype(F32)
             n_all[layer, :, at : at + CHUNK] = (signal * inverse).astype(BF16)
-        for copy in weight_copies(w_hbm, w_vmem, sems, layer):
-            copy.wait()
+        copies = weight_copies(w_hbm, w_vmem, sems, layer)
         acc = jnp.zeros((LENGTH, KVW), F32)
         for at in range(0, WIDTH, CHUNK):
+            copies[at // CHUNK].wait()
             acc = acc + dot_nn(
                 n_all[layer, :, at : at + CHUNK], weight_rows(w_vmem, layer, at, 0, KVW)
             )
@@ -133,10 +131,10 @@
             copy.start()
     out_ref[...] = up_ref[...]
     for layer in reversed(range(LAYERS)):
-        for copy in weight_copies(w_hbm, w_vmem, sems, layer):
-            copy.wait()
+        copies = weight_copies(w_hbm, w_vmem, sems, layer)
         acc = jnp.zeros((LENGTH, QW), F32)
         for at in range(0, WIDTH, CHUNK):
+            copies[at // CHUNK].wait()
             acc = acc + dot_nn(
                 out_ref[:, at : at + CHUNK], weight_rows(w_vmem, layer, at, KVW, COLS)
             )
@@ -171,8 +169,8 @@
 
 VM = pl.BlockSpec(memory_space=pltpu.VMEM)
 ANY = pl.BlockSpec(memory_space=pl.ANY)
-WEIGHT_SCRATCH = pltpu.VMEM((LAYERS, 16, 4, 64, COLS), BF16)
-WEIGHT_SEMS = pltpu.SemaphoreType.DMA((LAYERS, 16))
+WEIGHT_SCRATCH = pltpu.VMEM((LAYERS, WIDTH // CHUNK, 16, 64, COLS), BF16)
+WEIGHT_SEMS = pltpu.SemaphoreType.DMA((LAYERS, WIDTH // CHUNK))
 STATE_SHAPES = (
     jax.ShapeDtypeStruct((LAYERS, LENGTH, WIDTH), BF16),
     jax.ShapeDtypeStruct((LAYERS, LENGTH, WIDTH), BF16),
@@ -222,35 +220,23 @@
 
 
 def reorder(rows):
-    split = rows.reshape(LENGTH, 4, 4, 2, 2, 64)
-    return split.transpose(0, 4, 3, 2, 1, 5).reshape(LENGTH, WIDTH)
+    split = rows.reshape(LENGTH, 16, 2, 2, 64)
+    return split.transpose(0, 3, 2, 1, 4).reshape(LENGTH, WIDTH)
 
 
 def swap(block, axis):
     return lax.ppermute(block, axis, [(0, 1), (1, 0)])
 
 
-def turned(block, axis, distance):
-    return lax.ppermute(block, axis, [(i, (i + distance) % 4) for i in range(4)])
-
-
-def pick(block, index, size, axis):
-    return lax.dynamic_slice_in_dim(block, index * size, size, axis)
-
-
-def to_layer(block):
-    me = lax.axis_index("x")
-    parts = [pick(block, me, 1, 0)]
-    for distance in range(1, 4):
-        parts.append(turned(pick(block, (me + distance) % 4, 1, 0), "x", distance))
-    return jnp.concatenate(parts, axis=0)
+def sum_over(value, axes, count):
+    spread = jnp.broadcast_to(value, (count, 8, 128))
+    return jnp.sum(lax.all_to_all(spread, axes, 0, 0, tiled=True), axis=0)
 
 
 def shards(
     inputs, out_grad, doc_ids, query_weight, out_weight, master, first_moment, second_moment
 ):
     yh, x = lax.axis_index("yh"), lax.axis_index("x")
-    z1, z2, yl, c = (lax.axis_index(name) for name in DP)
     own = jnp.concatenate(
         [
             query_weight[0],
@@ -263,7 +249,7 @@
     with jax.named_scope("gather_weights"):
         own = lax.all_gather(own, "x", axis=0)
         weights = lax.all_gather(own, DP, axis=0)
-        weights = weights.reshape(4, 4, 2, 2, LAYERS, 64, COLS)
+        weights = weights.reshape(16, 2, 2, LAYERS, 64, COLS)
 
     rows_in = reorder(lax.dynamic_index_in_dim(inputs, x, 0, keepdims=False))
     up_in = reorder(lax.dynamic_index_in_dim(out_grad, x, 0, keepdims=False))
@@ -276,44 +262,30 @@
     states = run_forward(layer_in, seg_col, seg_row, weights)[1:]
 
     half_up = run_backward(up_in, states, weights, True)[0]
-    arrived = swap(half_up, "yh")
+    with jax.named_scope("normed_slices"):
+        half_up, rows = lax.optimization_barrier((half_up, states[1]))
+        arrived = swap(half_up, "yh")
+        rows = rows.reshape(LAYERS, LENGTH, 2, 2, CHUNK).transpose(0, 3, 2, 1, 4)
+        rows = rows.reshape(4 * LAYERS, LENGTH, CHUNK)
+        rows = lax.all_to_all(rows, PLANE, 0, 0, tiled=True).reshape(-1, CHUNK)
+        arrived, rows = lax.optimization_barrier((arrived, rows))
     upstream = jnp.where(yh == 0, arrived, up_in)
     grads = run_backward(upstream, states, weights, False)[1]
 
-    with jax.named_scope("normed_slices"):
-        rows = to_layer(states[1]).reshape(1, 4 * LENGTH, WIDTH)
-        half = WIDTH // 2
-        rows = jnp.concatenate(
-            [pick(rows, c, half, 2), swap(pick(rows, 1 - c, half, 2), "c")], axis=0
-        )
-        half = half // 2
-        rows = jnp.concatenate(
-            [pick(rows, yl, half, 2), swap(pick(rows, 1 - yl, half, 2), "yl")], axis=0
-        )
-        quarter = half // 4
-        parts = [pick(rows, z2, quarter, 2)]
-        for distance in range(1, 4):
-            parts.append(turned(pick(rows, (z2 + distance) % 4, quarter, 2), "z2", distance))
-        rows = jnp.concatenate(parts, axis=0).reshape(-1, quarter)
-
     with jax.named_scope("gather_grads"):
-        cols = to_layer(grads).reshape(1, 4 * LENGTH, 2 * HEAD)
-        cols = jnp.concatenate([cols, swap(cols, "c")], axis=0)
-        cols = jnp.concatenate([cols, swap(cols, "yl")], axis=0)
-        parts = [cols] + [turned(cols, "z2", distance) for distance in range(1, 4)]
-        cols = jnp.concatenate(parts, axis=0).reshape(-1, 2 * HEAD)
+        cols = jnp.broadcast_to(grads[:, None], (LAYERS, 4, LENGTH, 2 * HEAD))
+        cols = cols.reshape(4 * LAYERS, LENGTH, 2 * HEAD)
+        cols = lax.all_to_all(cols, PLANE, 0, 0, tiled=True).reshape(-1, 2 * HEAD)
 
     with jax.named_scope("sum_grads"):
-        partial = dot_tn(rows, cols)
-        grad = pick(partial, z1, 64, 0)
-        for distance in range(1, 4):
-            grad = grad + turned(pick(partial, (z1 + distance) % 4, 64, 0), "z1", distance)
+        partial = dot_tn(rows, cols).astype(BF16).reshape(16, 64, 2 * HEAD)
+        parts = lax.all_to_all(partial, "z", 0, 0, tiled=True)
+        grad = jnp.sum(parts.astype(F32), axis=0)
         grad = jnp.stack([grad[:, :HEAD], grad[:, HEAD:]])
 
     with jax.named_scope("clip"):
-        total_sq = jnp.full((8, 128), jnp.sum(grad * grad))
-        for axes in (("yl", "c"), "x", "z2", "z1", "yh"):
-            total_sq = jnp.sum(lax.all_gather(total_sq, axes, axis=0), axis=0)
+        total_sq = sum_over(jnp.sum(grad * grad), "z", 16)
+        total_sq = sum_over(total_sq, ("yh",) + PLANE, 32)
         factor = jnp.minimum(1.0, CLIP_NORM / jnp.sqrt(total_sq[0, 0]))
     clipped = grad * factor
     first_new = BETA_FIRST * first_moment[0] + (1.0 - BETA_FIRST) * clipped

time: 566 us -> 478 us (0.84); the launches traced: 556 us -> 477 us
  starting transfers between devices: 83.4 us -> 15.4 us
  waiting for transfers between devices: 303 us -> 263 us
  blocking collectives: 59.4 us -> 97.1 us
    all_to_all x0 -> x4, blocking collectives: none -> 84.4 us  [the longest x2 38.1 us: sum_over(): return jnp.sum(lax.all_to_all(spread, axes, 0, 0, tiled=True), axis=0)]
    ppermute x15 -> x0, starting transfers between devices: 57.7 us -> none  [turned(): lax.ppermute(block, axis, [(i, (i + distance) % 4) for i in range(4)])]
    ppermute x15 -> x0, waiting for transfers between devices: 42.4 us -> none  [turned(): lax.ppermute(block, axis, [(i, (i + distance) % 4) for i in range(4)])]
    all_gather x4 -> x0, blocking collectives: 38.4 us -> none  [shards(): total_sq = jnp.sum(lax.all_gather(total_sq, axes, axis=0), axis=0)]
    ppermute x6 -> x2, starting transfers between devices: 25.7 us -> 9.19 us  [swap(): return lax.ppermute(block, axis, [(0, 1), (1, 0)])]
    unnamed x1 -> x0, blocking collectives: 8.27 us -> none
    all_to_all x0 -> x1, starting transfers between devices: none -> 6.15 us  [shards(): rows = lax.all_to_all(rows, PLANE, 0, 0, tiled=True).reshape(-1, CHUNK)]
    ppermute x6 -> x2, waiting for transfers between devices: 19.2 us -> 20.7 us  [swap(): return lax.ppermute(block, axis, [(0, 1), (1, 0)])]
  transfers between devices with their start and end apart: 22 -> 4, of which waited for: 9 -> 3; matrix products, arithmetic and copies ran while one was open for 2% -> 1% of each run, Pallas kernels for 7% -> 0%
where the time goes in v2:
time: 478 us; the launch traced here: 477 us
  waiting for transfers between devices  263 us (55%)
  blocking collectives  97.1 us (20%)
  Pallas kernels  71.9 us (15%)
  starting transfers between devices  15.4 us (3%)
  between operations  15 us (3%)
  local copies, waits for them, and re-layouts  10.1 us (2%)
    all_gather x1, waiting for transfers between devices, shards(): weights = lax.all_gather(own, DP, axis=0)  242 us
    all_to_all x2, blocking collectives, sum_over(): return jnp.sum(lax.all_to_all(spread, axes, 0, 0, tiled=True), axis=0)  38.1 us
    pallas_call x2, Pallas kernels, run_forward(): pl.pallas_call(forward_kernel, out_shape=(jax.ShapeDtypeStruct((LENGTH, W...  36.4 us
    pallas_call x2, Pallas kernels, run_backward(): pl.pallas_call(functools.partial(backward_kernel, need_up), out_shape=(ja...  35.5 us
    all_to_all x1, blocking collectives, shards(): parts = lax.all_to_all(partial, 'z', 0, 0, tiled=True)  33.7 us
    ppermute x2, waiting for transfers between devices, swap(): return lax.ppermute(block, axis, [(0, 1), (1, 0)])  20.7 us
    all_gather x1, blocking collectives, shards(): own = lax.all_gather(own, 'x', axis=0)  12.7 us
    all_to_all x1, blocking collectives, shards(): cols = lax.all_to_all(cols, PLANE, 0, 0, tiled=True).reshape(-1, 2 * HEAD)  12.6 us
  transfers between devices with their start and end apart: 4, of which 3 were waited for; matrix products, arithmetic and copies ran while one was open for 1% of the time, Pallas kernels for 0%

profile of v2, /device:TPU:1, one launch (start us, length us, event | category | flops | bytes accessed | tf_op | source)
XLA Modules:
  0.0 477.2 jit_solution(17825513124789535701)
XLA Ops:
  7.2 0.8 convert.4
  8.1 0.9 pad_maximum_fusion
  9.0 12.7 %all-gather = bf16[256,1280]{1,0:T(8,128)(2,1)} all-gather(bf16[64,1280]{1,0:T(8,128)(2,1)S(1)} %pad_maximum_fusion), channel_id=2, replica_groups=mesh['yh'=2,'x'=4,'z'=16,'yl'=2,'c'=2] {'x'}, dimensions={0}, use_global_device_ids=true | all-gather | bytes 819200 | tf_op jit(solution)/shard_map/gather_weights/all_gather | solution.py:250
  22.4 1.1 constant_dynamic-slice_fusion.1
  24.1 1.2 reshape.105.h_ref
  25.8 241.8 %all-gather.4.cloned.1.call-done = bf16[256,64,1280]{2,1,0:T(8,128)(2,1)} async-done(((bf16[4,64,1280]{2,1,0:T(8,128)(2,1)}), bf16[256,64,1280]{2,1,0:T(8,128)(2,1)}) %all-gather.4.cloned.1.call-update) | async-done | bytes 41943056 | tf_op jit(solution)/shard_map/gather_weights/all_gather | solution.py:251
  267.7 18.1 %layers_forward.2 = (bf16[32,4096]{1,0:T(8,128)(2,1)}, bf16[4,32,4096]{2,1,0:T(8,128)(2,1)}, bf16[4,32,4096]{2,1,0:T(8,128)(2,1)}, bf16[4,128,128]{2,1,0:T(8,128...) custom-call(bf16[32,4096]{1,0:T(8,128)(2,1)} %reshape.105.h_ref, ...), custom_call_target="tpu_custom_call" | custom-call | flops 1342177280 | bytes 41943040 | tf_op jit(solution)/shard_map/layers_forward/pallas_call | solution.py:193
  285.8 4.8 %collective-permute-start = (bf16[32,4096]{1,0:T(8,128)(2,1)}, bf16[32,4096]{1,0:T(8,128)(2,1)S(1)}, u32[]{:S(2)}, u32[]{:S(2)}) collective-permute-start(bf16[32,4096]{1,0:T(8,128)(2,1)} %get-tuple-element.15), channel_id=1, source_target_pairs={{0,256},{256,0},{1,257},{257,1},{2,258},{258,2},{3,259},{259,3},{4... | collective-permute-start | bytes 786440 | tf_op jit(solution)/shard_map/ppermute | solution.py:228
  291.3 1.2 reshape.103.up_ref
  292.5 4.6 collective-permute-done
  297.8 18.2 %layers_forward.3 = (bf16[32,4096]{1,0:T(8,128)(2,1)}, bf16[4,32,4096]{2,1,0:T(8,128)(2,1)}, bf16[4,32,4096]{2,1,0:T(8,128)(2,1)}, bf16[4,128,128]{2,1,0:T(8,128...) custom-call(bf16[32,4096]{1,0:T(8,128)(2,1)} %broadcast_select_fusion.1.h_ref, ...), custom_call_target="tpu_custom_call" | custom-call | flops 1342177280 | bytes 41943040 | tf_op jit(solution)/shard_map/layers_forward/pallas_call | solution.py:193
  316.1 18.9 %layers_backward.2 = (bf16[32,4096]{1,0:T(8,128)(2,1)}, bf16[4,32,256]{2,1,0:T(8,128)(2,1)}) custom-call(bf16[32,4096]{1,0:T(8,128)(2,1)} %reshape.103.up_ref, bf16[4,32,4096]{2,1,0:T(8,128)(2,1)} %get-tuple-element.16.h_all, bf16[4,128,128]{2,1,0:T(8,128)(2,1)} %get-tuple-element.17.q_all, bf16[4,32,128]{2,1,0:T(8,128)(2,1)} %get-tuple-element.18.k_all, ...), custom_call_target="tpu_custom_call" | custom-call | flops 1342177280 | bytes 41943040 | tf_op jit(solution)/shard_map/layers_backward/pallas_call | solution.py:207
  335.0 0.8 reshape.107
  335.8 1.3 copy.26
  337.2 6.2 %all-to-all-start = ((bf16[16,32,1024]{2,1,0:T(8,128)(2,1)}), bf16[16,32,1024]{2,1,0:T(8,128)(2,1)S(1)}, u32[]{:S(2)}, u32[]{:S(2)}) async-start(bf16[16,32,1024]{2,1,0:T(8,128)(2,1)} %bitcast.10), calls=%async_computation | async-start | bytes 2097152 | tf_op jit(solution)/shard_map/normed_slices/all_to_all | solution.py:270
  343.3 4.4 collective-permute-start.1
  347.7 16.1 %collective-permute-done.1 = bf16[32,4096]{1,0:T(8,128)(2,1)S(1)} collective-permute-done((bf16[32,4096]{1,0:T(8,128)(2,1)}, bf16[32,4096]{1,0:T(8,128)(2,1)S(1)}, u32[]{:S(2)}, u32[]{:S(2)}) %collective-permute-start.1) | collective-permute-done | bytes 262176 | tf_op jit(solution)/shard_map/normed_slices/ppermute | solution.py:228
  363.9 0.7 broadcast_select_fusion.up_ref
  364.6 16.6 %layers_backward.3 = (bf16[32,4096]{1,0:T(8,128)(2,1)}, bf16[4,32,256]{2,1,0:T(8,128)(2,1)}) custom-call(bf16[32,4096]{1,0:T(8,128)(2,1)} %broadcast_select_fusion.up_ref, bf16[4,32,4096]{2,1,0:T(8,128)(2,1)} %get-tuple-element.16.h_all, bf16[4,128,128]{2,1,0:T(8,128)(2,1)} %get-tuple-element.17.q_all, bf16[4,32,128]{2,1,0:T(8,128)(2,1)} %get-tuple-element.18.k_all, ...), custom_call_target="tpu_custom_call" | custom-call | flops 1342177280 | bytes 41943040 | tf_op jit(solution)/shard_map/layers_backward/pallas_call | solution.py:207
  381.2 0.9 broadcast_in_dim.9
  382.1 12.6 %all_to_all.25 = bf16[16,32,256]{2,1,0:T(8,128)(2,1)S(1)} all-to-all(bf16[16,32,256]{2,1,0:T(8,128)(2,1)S(1)} %bitcast.41), channel_id=1, replica_groups=mesh['yh'=2,'x'=4,'z'=16,'yl'=2,'c'=2] {'x','yl','c'}, dimensions={0} | all-to-all | bytes 524288 | tf_op jit(solution)/shard_map/gather_grads/all_to_all | solution.py:278
  395.1 33.7 %all_to_all.26 = bf16[16,64,256]{2,1,0:T(8,128)(2,1)S(1)} all-to-all(bf16[16,64,256]{2,1,0:T(8,128)(2,1)S(1)} %bitcast.43), channel_id=1, replica_groups=mesh['yh'=2,'x'=4,'z'=16,'yl'=2,'c'=2] {'z'}, dimensions={0} | all-to-all | bytes 1048576 | tf_op jit(solution)/shard_map/sum_grads/all_to_all | solution.py:282
  430.2 24.2 %all_to_all.27 = f32[16,8,128]{2,1,0:T(8,128)S(1)} all-to-all(f32[16,8,128]{2,1,0:T(8,128)S(1)} %broadcast_in_dim.20), channel_id=1, replica_groups=mesh['yh'=2,'x'=4,'z'=16,'yl'=2,'c'=2] {'z'}, dimensions={0} | all-to-all | bytes 131072 | tf_op jit(solution)/shard_map/clip/all_to_all | solution.py:233
  454.4 14.0 %all_to_all.28 = f32[32,8,128]{2,1,0:T(8,128)S(1)} all-to-all(f32[32,8,128]{2,1,0:T(8,128)S(1)} %broadcast_in_dim.21), channel_id=1, replica_groups=mesh['yh'=2,'x'=4,'z'=16,'yl'=2,'c'=2] {'yh','x','yl','c'}, dimensions={0} | all-to-all | bytes 262144 | tf_op jit(solution)/shard_map/clip/all_to_all | solution.py:233
  (36 shorter events, 6.4 us)
Async XLA Ops:
  7.2 14.6 %copy-start = (s32[4,32]{1,0:T(4,128)S(1)}, s32[4,32]{1,0:T(4,128)}, u32[]{:S(2)}) copy-start(s32[4,32]{1,0:T(4,128)} %param.10) | copy-start | bytes 1540
  7.2 260.5 %all-gather.4.cloned.1.call-start = ((), (), s32[]{:S(2)}) async-start(), calls=%async_computation.5 | async-start | bytes 42598400 | tf_op jit(solution)/shard_map/gather_weights/all_gather | solution.py:251
  25.3 271.8 %copy-start.2 = (bf16[32,4096]{1,0:T(8,128)(2,1)S(1)}, bf16[32,4096]{1,0:T(8,128)(2,1)}, u32[]{:S(2)}) copy-start(bf16[32,4096]{1,0:T(8,128)(2,1)} %reshape.105.h_ref) | copy-start | bytes 786436
  285.8 11.3 %collective-permute-start = (bf16[32,4096]{1,0:T(8,128)(2,1)}, bf16[32,4096]{1,0:T(8,128)(2,1)S(1)}, u32[]{:S(2)}, u32[]{:S(2)}) collective-permute-start(bf16[32,4096]{1,0:T(8,128)(2,1)} %get-tuple-element.15), channel_id=1, source_target_pairs={{0,256},{256,0},{1,257},{257,1},{2,258},{258,2},{3,259},{259,3},{4... | collective-permute-start | bytes 786440 | tf_op jit(solution)/shard_map/ppermute | solution.py:228
  297.8 66.0 %copy-start.1 = (bf16[32,4096]{1,0:T(8,128)(2,1)S(1)}, bf16[32,4096]{1,0:T(8,128)(2,1)}, u32[]{:S(2)}) copy-start(bf16[32,4096]{1,0:T(8,128)(2,1)} %reshape.103.up_ref) | copy-start | bytes 786436
  316.1 19.0 %copy-start.3 = (bf16[4,32,4096]{2,1,0:T(8,128)(2,1)S(1)}, bf16[4,32,4096]{2,1,0:T(8,128)(2,1)}, u32[]{:S(2)}) copy-start(bf16[4,32,4096]{2,1,0:T(8,128)(2,1)} %get-tuple-element.24) | copy-start | bytes 3145732
  316.1 153.5 %copy-start.4 = (f32[1,2,64,128]{3,2,1,0:T(8,128)S(1)}, f32[1,2,64,128]{3,2,1,0:T(8,128)}, u32[]{:S(2)}) copy-start(f32[1,2,64,128]{3,2,1,0:T(8,128)} %param.13) | copy-start | bytes 196612
  316.1 153.5 %copy-start.5 = (f32[1,2,64,128]{3,2,1,0:T(8,128)S(1)}, f32[1,2,64,128]{3,2,1,0:T(8,128)}, u32[]{:S(2)}) copy-start(f32[1,2,64,128]{3,2,1,0:T(8,128)} %param.15) | copy-start | bytes 196612
  316.1 153.5 %copy-start.6 = (f32[1,2,64,128]{3,2,1,0:T(8,128)S(1)}, f32[1,2,64,128]{3,2,1,0:T(8,128)}, u32[]{:S(2)}) copy-start(f32[1,2,64,128]{3,2,1,0:T(8,128)} %param.14) | copy-start | bytes 196612
  337.2 26.7 %all-to-all-start = ((bf16[16,32,1024]{2,1,0:T(8,128)(2,1)}), bf16[16,32,1024]{2,1,0:T(8,128)(2,1)S(1)}, u32[]{:S(2)}, u32[]{:S(2)}) async-start(bf16[16,32,1024]{2,1,0:T(8,128)(2,1)} %bitcast.10), calls=%async_computation | async-start | bytes 2097152 | tf_op jit(solution)/shard_map/normed_slices/all_to_all | solution.py:270
  343.3 20.5 %collective-permute-start.1 = (bf16[32,4096]{1,0:T(8,128)(2,1)}, bf16[32,4096]{1,0:T(8,128)(2,1)S(1)}, u32[]{:S(2)}, u32[]{:S(2)}) collective-permute-start(bf16[32,4096]{1,0:T(8,128)(2,1)} %get-tuple-element.23), channel_id=1, source_target_pairs={{0,256},{256,0},{1,257},{257,1},{2,258},{258,2},{3,259},{259,3},{4... | collective-permute-start | bytes 786440 | tf_op jit(solution)/shard_map/normed_slices/ppermute | solution.py:228
Sparse Core Ops, SparseCore 0:
  21.8 245.7 all-gather.3

commit v3 on v2

--- a/solution.py
+++ b/solution.py
@@ -27,6 +27,8 @@
 KVW = QW + 2 * HEAD
 COLS = KVW + QW
 CHUNK = 1024
+UPPER = 32
+SOURCES = 10
 SCALE = 1.0 / math.sqrt(HEAD)
 VMEM_LIMIT = 60 * 1024 * 1024
 F32 = jnp.float32
@@ -45,17 +47,47 @@
     return lax.dot_general(a, b, (((0,), (0,)), ((), ())), preferred_element_type=F32)
 
 
-def weight_copies(w_hbm, w_vmem, sems, layer):
-    copies = []
-    for c in range(2):
-        for yl in range(2):
-            at = c * 2 + yl
-            copies.append(
-                pltpu.make_async_copy(
-                    w_hbm.at[:, yl, c, layer], w_vmem.at[layer, at], sems.at[layer, at]
-                )
-            )
-    return copies
+def start_copies(at, layer, distance, core, sources, w_vmem, sems):
+    whole, rest, *moved = sources
+
+    def start(source, target):
+        pltpu.make_async_copy(source, target, sems.at[layer, at]).start()
+
+    c, yl = at // 2, at % 2
+    target = w_vmem.at[layer, at]
+    if distance == 0:
+        start(whole.at[:, c, yl], target)
+        return
+    start(rest.at[:, c, distance - 1, yl], target.at[:, UPPER:])
+    upper = target.at[:, :UPPER]
+    for own in range(2):
+        near, far, twice, back = moved[own::2]
+
+        @pl.when((core == c) == (own == 0))
+        def _(near=near, far=far, twice=twice, back=back):
+            if distance == 1:
+                start(near.at[:, yl], upper)
+            elif distance == 3:
+                start(far.at[:, yl], upper)
+            else:
+                start(twice.at[:, yl], upper.at[:8])
+                start(back.at[:, yl], upper.at[8:])
+
+
+def start_layers(order, place, sources, w_vmem, sems):
+    x, core = place[0], place[1]
+    for layer in order:
+        for distance in range(4):
+
+            @pl.when(((x - layer + 4) & 3) == distance)
+            def _(layer=layer, distance=distance):
+                for at in range(WIDTH // CHUNK):
+                    start_copies(at, layer, distance, core, sources, w_vmem, sems)
+
+
+def wait_rows(w_vmem, sems, layer, at):
+    block = w_vmem.at[layer, at // CHUNK]
+    pltpu.make_async_copy(block, block, sems.at[layer, at // CHUNK]).wait()
 
 
 def stack_heads(rows):
@@ -78,12 +110,10 @@
     return w_vmem[layer, at // CHUNK, :, :, first:last].reshape(CHUNK, last - first)
 
 
-def forward_kernel(
-    h_ref, seg_col, seg_row, w_hbm, out_ref, h_all, n_all, q_all, k_all, v_all, p_all, w_vmem, sems
-):
-    for layer in range(LAYERS):
-        for copy in weight_copies(w_hbm, w_vmem, sems, layer):
-            copy.start()
+def forward_kernel(place, h_ref, seg_col, seg_row, *refs):
+    sources, refs = refs[:SOURCES], refs[SOURCES:]
+    out_ref, h_all, n_all, q_all, k_all, v_all, p_all, w_vmem, sems = refs
+    start_layers(range(LAYERS), place, sources, w_vmem, sems)
     row_ids = lax.broadcasted_iota(jnp.int32, (LENGTH, LENGTH), 0)
     col_ids = lax.broadcasted_iota(jnp.int32, (LENGTH, LENGTH), 1)
     allowed = ((seg_col[...] == seg_row[...]) & (col_ids <= row_ids)).astype(F32)
@@ -94,10 +124,9 @@
         for at in range(0, WIDTH, CHUNK):
             signal = h_all[layer, :, at : at + CHUNK].astype(F32)
             n_all[layer, :, at : at + CHUNK] = (signal * inverse).astype(BF16)
-        copies = weight_copies(w_hbm, w_vmem, sems, layer)
         acc = jnp.zeros((LENGTH, KVW), F32)
         for at in range(0, WIDTH, CHUNK):
-            copies[at // CHUNK].wait()
+            wait_rows(w_vmem, sems, layer, at)
             acc = acc + dot_nn(
                 n_all[layer, :, at : at + CHUNK], weight_rows(w_vmem, layer, at, 0, KVW)
             )
@@ -123,18 +152,15 @@
                 out_ref[:, at : at + CHUNK] = result
 
 
-def backward_kernel(
-    need_up, up_ref, h_all, q_all, k_all, v_all, p_all, w_hbm, out_ref, g_all, w_vmem, gn, sems
-):
-    for layer in reversed(range(LAYERS)):
-        for copy in weight_copies(w_hbm, w_vmem, sems, layer):
-            copy.start()
+def backward_kernel(need_up, place, up_ref, h_all, q_all, k_all, v_all, p_all, *refs):
+    sources, refs = refs[:SOURCES], refs[SOURCES:]
+    out_ref, g_all, w_vmem, gn, sems = refs
+    start_layers(reversed(range(LAYERS)), place, sources, w_vmem, sems)
     out_ref[...] = up_ref[...]
     for layer in reversed(range(LAYERS)):
-        copies = weight_copies(w_hbm, w_vmem, sems, layer)
         acc = jnp.zeros((LENGTH, QW), F32)
         for at in range(0, WIDTH, CHUNK):
-            copies[at // CHUNK].wait()
+            wait_rows(w_vmem, sems, layer, at)
             acc = acc + dot_nn(
                 out_ref[:, at : at + CHUNK], weight_rows(w_vmem, layer, at, KVW, COLS)
             )
@@ -168,6 +194,7 @@
 
 
 VM = pl.BlockSpec(memory_space=pltpu.VMEM)
+SM = pl.BlockSpec(memory_space=pltpu.SMEM)
 ANY = pl.BlockSpec(memory_space=pl.ANY)
 WEIGHT_SCRATCH = pltpu.VMEM((LAYERS, WIDTH // CHUNK, 16, 64, COLS), BF16)
 WEIGHT_SEMS = pltpu.SemaphoreType.DMA((LAYERS, WIDTH // CHUNK))
@@ -189,20 +216,20 @@
     )
 
 
-def run_forward(h, seg_col, seg_row, weights):
+def run_forward(place, h, seg_col, seg_row, weights):
     return pl.pallas_call(
         forward_kernel,
         out_shape=(jax.ShapeDtypeStruct((LENGTH, WIDTH), BF16),) + STATE_SHAPES,
-        in_specs=[VM, VM, VM, ANY],
+        in_specs=[SM, VM, VM, VM] + [ANY] * SOURCES,
         out_specs=(VM,) * 7,
         scratch_shapes=[WEIGHT_SCRATCH, WEIGHT_SEMS],
         compiler_params=pltpu.CompilerParams(vmem_limit_bytes=VMEM_LIMIT),
         cost_estimate=cost(LAYERS),
         name="layers_forward",
-    )(h, seg_col, seg_row, weights)
-
-
-def run_backward(upstream, states, weights, need_up):
+    )(place, h, seg_col, seg_row, *weights)
+
+
+def run_backward(place, upstream, states, weights, need_up):
     h_all, n_all, q_all, k_all, v_all, p_all = states
     return pl.pallas_call(
         functools.partial(backward_kernel, need_up),
@@ -210,13 +237,13 @@
             jax.ShapeDtypeStruct((LENGTH, WIDTH), BF16),
             jax.ShapeDtypeStruct((LAYERS, LENGTH, 2 * HEAD), BF16),
         ),
-        in_specs=[VM] * 6 + [ANY],
+        in_specs=[SM] + [VM] * 6 + [ANY] * SOURCES,
         out_specs=(VM, VM),
         scratch_shapes=[WEIGHT_SCRATCH, pltpu.VMEM((LENGTH, WIDTH), F32), WEIGHT_SEMS],
         compiler_params=pltpu.CompilerParams(vmem_limit_bytes=VMEM_LIMIT),
         cost_estimate=cost(LAYERS),
         name="layers_backward",
-    )(upstream, h_all, q_all, k_all, v_all, p_all, weights)
+    )(place, upstream, h_all, q_all, k_all, v_all, p_all, *weights)
 
 
 def reorder(rows):
@@ -226,6 +253,26 @@
 
 def swap(block, axis):
     return lax.ppermute(block, axis, [(0, 1), (1, 0)])
+
+
+def turned(block, distance):
+    return lax.ppermute(block, "x", [(i, (i + distance) % 4) for i in range(4)])
+
+
+def gather_layers(own, yl, c):
+    other = swap(own, "yl")
+    pair = jnp.stack([jnp.where(yl == 0, own, other), jnp.where(yl == 0, other, own)])
+    whole = lax.all_gather(pair, ("z", "c"), axis=0).reshape(16, 2, 2, 64, COLS)
+    lower = pair[:, UPPER:]
+    lower = jnp.stack([turned(lower, distance) for distance in range(1, 4)])
+    rest = lax.all_gather(lower, ("z", "c"), axis=0).reshape(16, 2, 3, 2, 64 - UPPER, COLS)
+    share = lax.dynamic_slice(whole, (0, c, 0, 0, 0), (16, 1, 2, UPPER, COLS))[:, 0]
+    near, far = turned(share, 1), turned(share, 3)
+    twice, back = turned(near[:8], 1), turned(far[8:], 3)
+    moved = []
+    for block in (near, far, twice, back):
+        moved += [block, swap(block, "c")]
+    return [whole, rest] + moved
 
 
 def sum_over(value, axes, count):
@@ -247,30 +294,28 @@
         axis=1,
     )
     with jax.named_scope("gather_weights"):
-        own = lax.all_gather(own, "x", axis=0)
-        weights = lax.all_gather(own, DP, axis=0)
-        weights = weights.reshape(16, 2, 2, LAYERS, 64, COLS)
+        weights = gather_layers(own, lax.axis_index("yl"), lax.axis_index("c"))
+    place = jnp.stack([x, lax.axis_index("c")]).astype(jnp.int32)
 
     rows_in = reorder(lax.dynamic_index_in_dim(inputs, x, 0, keepdims=False))
     up_in = reorder(lax.dynamic_index_in_dim(out_grad, x, 0, keepdims=False))
     segment = lax.dynamic_index_in_dim(doc_ids, x, 0, keepdims=False)
     seg_col, seg_row = segment[:, None], segment[None, :]
 
-    first_half = run_forward(rows_in, seg_col, seg_row, weights)[0]
+    first_half = run_forward(place, rows_in, seg_col, seg_row, weights)[0]
     arrived = swap(first_half, "yh")
     layer_in = jnp.where(yh == 1, arrived, rows_in)
-    states = run_forward(layer_in, seg_col, seg_row, weights)[1:]
-
-    half_up = run_backward(up_in, states, weights, True)[0]
+    states = run_forward(place, layer_in, seg_col, seg_row, weights)[1:]
+
+    half_up = run_backward(place, up_in, states, weights, True)[0]
     with jax.named_scope("normed_slices"):
-        half_up, rows = lax.optimization_barrier((half_up, states[1]))
-        arrived = swap(half_up, "yh")
-        rows = rows.reshape(LAYERS, LENGTH, 2, 2, CHUNK).transpose(0, 3, 2, 1, 4)
+        rows = states[1].reshape(LAYERS, LENGTH, 2, 2, CHUNK).transpose(0, 3, 2, 1, 4)
         rows = rows.reshape(4 * LAYERS, LENGTH, CHUNK)
         rows = lax.all_to_all(rows, PLANE, 0, 0, tiled=True).reshape(-1, CHUNK)
-        arrived, rows = lax.optimization_barrier((arrived, rows))
+        half_up, rows = lax.optimization_barrier((half_up, rows))
+    arrived = swap(half_up, "yh")
     upstream = jnp.where(yh == 0, arrived, up_in)
-    grads = run_backward(upstream, states, weights, False)[1]
+    grads = run_backward(place, upstream, states, weights, False)[1]
 
     with jax.named_scope("gather_grads"):
         cols = jnp.broadcast_to(grads[:, None], (LAYERS, 4, LENGTH, 2 * HEAD))

time: 478 us -> 425 us (0.89)
  waiting for transfers between devices: 263 us -> 174 us
  starting transfers between devices: 15.4 us -> 54.4 us
  blocking collectives: 97.1 us -> 82.4 us
  local copies, waits for them, and re-layouts: 10.1 us -> 18.1 us
    all_gather x1 -> x2, waiting for transfers between devices: 242 us -> 72.8 us  [the longest x1 72.8 us: gather_layers(): whole = lax.all_gather(pair, ('z', 'c'), axis=0).reshape(16, 2, 2, 64, COLS)]
    ppermute x0 -> x7, waiting for transfers between devices: none -> 86.1 us  [turned(): return lax.ppermute(block, 'x', [(i, (i + distance) % 4) for i in range(4)])]
    ppermute x0 -> x7, starting transfers between devices: none -> 23.9 us  [turned(): return lax.ppermute(block, 'x', [(i, (i + distance) % 4) for i in range(4)])]
    ppermute x2 -> x7, starting transfers between devices: 9.19 us -> 26.2 us  [swap(): return lax.ppermute(block, axis, [(0, 1), (1, 0)])]
    all_gather x1 -> x0, blocking collectives: 12.7 us -> none  [shards(): own = lax.all_gather(own, 'x', axis=0)]
    ppermute x2 -> x7, waiting for transfers between devices: 20.7 us -> 15.3 us  [swap(): return lax.ppermute(block, axis, [(0, 1), (1, 0)])]
  transfers between devices with their start and end apart: 4 -> 17, of which waited for: 3 -> 9; matrix products, arithmetic and copies ran while one was open for 1% -> 3% of each run, Pallas kernels for 0% -> 4%
where the time goes in v3:
time: 425 us; the launch traced here: 424 us
  waiting for transfers between devices  174 us (41%)
  blocking collectives  82.4 us (19%)
  Pallas kernels  71.6 us (17%)
  starting transfers between devices  54.4 us (13%)
  local copies, waits for them, and re-layouts  18.1 us (4%)
  between operations  15.1 us (4%)
  other arithmetic  7.85 us (2%)
    ppermute x7, waiting for transfers between devices, turned(): return lax.ppermute(block, 'x', [(i, (i + distance) % 4) for i in range(4)])  86.1 us
    all_gather x1, waiting for transfers between devices, gather_layers(): whole = lax.all_gather(pair, ('z', 'c'), axis=0).reshape(16, 2, 2, 64, COLS)  72.8 us
    all_to_all x2, blocking collectives, sum_over(): return jnp.sum(lax.all_to_all(spread, axes, 0, 0, tiled=True), axis=0)  38.8 us
    pallas_call x2, Pallas kernels, run_forward(): pl.pallas_call(forward_kernel, out_shape=(jax.ShapeDtypeStruct((LENGTH, W...  36.4 us
    pallas_call x2, Pallas kernels, run_backward(): pl.pallas_call(functools.partial(backward_kernel, need_up), out_shape=(ja...  35.2 us
    all_to_all x1, blocking collectives, shards(): parts = lax.all_to_all(partial, 'z', 0, 0, tiled=True)  29.6 us
    ppermute x7, starting transfers between devices, swap(): return lax.ppermute(block, axis, [(0, 1), (1, 0)])  26.2 us
    ppermute x7, starting transfers between devices, turned(): return lax.ppermute(block, 'x', [(i, (i + distance) % 4) for i in range(4)])  23.9 us
  transfers between devices with their start and end apart: 17, of which 9 were waited for; matrix products, arithmetic and copies ran while one was open for 3% of the time, Pallas kernels for 4%

profile of v3, /device:TPU:1, one launch (start us, length us, event | category | flops | bytes accessed | tf_op | source)
XLA Modules:
  0.0 424.2 jit_solution(15048886513465451930)
XLA Ops:
  9.0 4.0 collective-permute-start
  17.5 5.4 %collective-permute-start.3 = (bf16[2,32,1280]{2,1,0:T(8,128)(2,1)S(1)}, bf16[2,32,1280]{2,1,0:T(8,128)(2,1)S(1)}, u32[]{:S(2)}, u32[]{:S(2)}) collective-permute-start(bf16[2,32,1280]{2,1,0:T(8,128)(2,1)S(1)} %fusion), channel_id=1, source_target_pairs={{0,192},{64,0},{128,64},{192,128},{1,193},{65,1},{129,65},{193,129... | collective-permute-start | bytes 491528 | tf_op jit(solution)/shard_map/gather_weights/ppermute | solution.py:259
  33.5 72.8 %all-gather.5.cloned.1.call-done = bf16[64,64,1280]{2,1,0:T(8,128)(2,1)} async-done(((bf16[2,64,1280]{2,1,0:T(8,128)(2,1)}), bf16[64,64,1280]{2,1,0:T(8,128)(2,1)}) %all-gather.5.cloned.1.call-update) | async-done | bytes 10485776 | tf_op jit(solution)/shard_map/gather_weights/all_gather | solution.py:265
  108.2 4.2 collective-permute-start.6
  114.4 54.0 %collective-permute-done.6.refs_4_ = bf16[16,2,32,1280]{3,2,1,0:T(8,128)(2,1)S(1)} collective-permute-done((bf16[16,2,32,1280]{3,2,1,0:T(8,128)(2,1)S(1)}, bf16[16,2,32,1280]{3,2,1,0:T(8,128)(2,1)S(1)}, u32[]{:S(2)}, u32[]{:S(2)}) %collective-permute-start.6) | collective-permute-done | bytes 2621472 | tf_op jit(solution)/shard_map/gather_weights/ppermute | solution.py:259
  168.6 5.4 %collective-permute-start.10 = (bf16[8,2,32,1280]{3,2,1,0:T(8,128)(2,1)S(1)}, bf16[8,2,32,1280]{3,2,1,0:T(8,128)(2,1)}, u32[]{:S(2)}, u32[]{:S(2)}) collective-permute-start(bf16[8,2,32,1280]{3,2,1,0:T(8,128)(2,1)S(1)} %slice.39), channel_id=1, source_target_pairs={{0,192},{64,0},{128,64},{192,128},{1,193},{65,1},{129,65},{193,129... | collective-permute-start | bytes 3932168 | tf_op jit(solution)/shard_map/gather_weights/ppermute | solution.py:259
  174.0 3.2 collective-permute-start.7
  182.5 18.6 %collective-permute-done.10.refs_8_ = bf16[8,2,32,1280]{3,2,1,0:T(8,128)(2,1)} collective-permute-done((bf16[8,2,32,1280]{3,2,1,0:T(8,128)(2,1)S(1)}, bf16[8,2,32,1280]{3,2,1,0:T(8,128)(2,1)}, u32[]{:S(2)}, u32[]{:S(2)}) %collective-permute-start.10) | collective-permute-done | bytes 1310752 | tf_op jit(solution)/shard_map/gather_weights/ppermute | solution.py:259
  201.1 3.8 collective-permute-start.11
  204.9 8.8 %collective-permute-done.8.refs_6_ = bf16[8,2,32,1280]{3,2,1,0:T(8,128)(2,1)} collective-permute-done((bf16[8,2,32,1280]{3,2,1,0:T(8,128)(2,1)S(1)}, bf16[8,2,32,1280]{3,2,1,0:T(8,128)(2,1)}, u32[]{:S(2)}, u32[]{:S(2)}) %collective-permute-start.8) | collective-permute-done | bytes 1310752 | tf_op jit(solution)/shard_map/gather_weights/ppermute | solution.py:259
  213.6 3.2 collective-permute-start.9
  225.2 18.2 %layers_forward.2 = (bf16[32,4096]{1,0:T(8,128)(2,1)}, bf16[4,32,4096]{2,1,0:T(8,128)(2,1)}, bf16[4,32,4096]{2,1,0:T(8,128)(2,1)}, bf16[4,128,128]{2,1,0:T(8,128...) custom-call(s32[2]{0:T(128)} %pad_add_fusion.place, ...), custom_call_target="tpu_custom_call" | custom-call | flops 1342177280 | bytes 41943040 | tf_op jit(solution)/shard_map/layers_forward/pallas_call | solution.py:220
  243.4 5.0 %collective-permute-start.12 = (bf16[32,4096]{1,0:T(8,128)(2,1)}, bf16[32,4096]{1,0:T(8,128)(2,1)S(1)}, u32[]{:S(2)}, u32[]{:S(2)}) collective-permute-start(bf16[32,4096]{1,0:T(8,128)(2,1)} %get-tuple-element.13), channel_id=1, source_target_pairs={{0,256},{256,0},{1,257},{257,1},{2,258},{258,2},{3,259},{259,3},{4... | collective-permute-start | bytes 786440 | tf_op jit(solution)/shard_map/ppermute | solution.py:255
  248.4 6.6 %collective-permute-done.12 = bf16[32,4096]{1,0:T(8,128)(2,1)S(1)} collective-permute-done((bf16[32,4096]{1,0:T(8,128)(2,1)}, bf16[32,4096]{1,0:T(8,128)(2,1)S(1)}, u32[]{:S(2)}, u32[]{:S(2)}) %collective-permute-start.12) | collective-permute-done | bytes 262176 | tf_op jit(solution)/shard_map/ppermute | solution.py:255
  255.7 18.1 %layers_forward.3 = (bf16[32,4096]{1,0:T(8,128)(2,1)}, bf16[4,32,4096]{2,1,0:T(8,128)(2,1)}, bf16[4,32,4096]{2,1,0:T(8,128)(2,1)}, bf16[4,128,128]{2,1,0:T(8,128...) custom-call(s32[2]{0:T(128)} %pad_add_fusion.place, ...), custom_call_target="tpu_custom_call" | custom-call | flops 1342177280 | bytes 41943040 | tf_op jit(solution)/shard_map/layers_forward/pallas_call | solution.py:220
  277.0 4.2 all-to-all-start
  283.1 18.6 %layers_backward.2 = (bf16[32,4096]{1,0:T(8,128)(2,1)}, bf16[4,32,256]{2,1,0:T(8,128)(2,1)}) custom-call(s32[2]{0:T(128)} %pad_add_fusion.place, bf16[32,4096]{1,0:T(8,128)(2,1)} %reshape.106.up_ref, bf16[4,32,4096]{2,1,0:T(8,128)(2,1)} %get-tuple-element.14.h_all, bf16[4,128,128]{2,1,0:T(8,128)(2,1)} %get-tuple-element.15.q_all, ...), custom_call_target="tpu_custom_call" | custom-call | flops 1342177280 | bytes 41943040 | tf_op jit(solution)/shard_map/layers_backward/pallas_call | solution.py:234
  301.7 5.0 %collective-permute-start.13 = (bf16[32,4096]{1,0:T(8,128)(2,1)}, bf16[32,4096]{1,0:T(8,128)(2,1)S(1)}, u32[]{:S(2)}, u32[]{:S(2)}) collective-permute-start(bf16[32,4096]{1,0:T(8,128)(2,1)} %get-tuple-element.22), channel_id=1, source_target_pairs={{0,256},{256,0},{1,257},{257,1},{2,258},{258,2},{3,259},{259,3},{4... | collective-permute-start | bytes 786440 | tf_op jit(solution)/shard_map/ppermute | solution.py:255
  306.8 6.0 %collective-permute-done.13 = bf16[32,4096]{1,0:T(8,128)(2,1)S(1)} collective-permute-done((bf16[32,4096]{1,0:T(8,128)(2,1)}, bf16[32,4096]{1,0:T(8,128)(2,1)S(1)}, u32[]{:S(2)}, u32[]{:S(2)}) %collective-permute-start.13) | collective-permute-done | bytes 262176 | tf_op jit(solution)/shard_map/ppermute | solution.py:255
  313.5 16.6 %layers_backward.3 = (bf16[32,4096]{1,0:T(8,128)(2,1)}, bf16[4,32,256]{2,1,0:T(8,128)(2,1)}) custom-call(s32[2]{0:T(128)} %pad_add_fusion.place, bf16[32,4096]{1,0:T(8,128)(2,1)} %broadcast_select_fusion.up_ref, bf16[4,32,4096]{2,1,0:T(8,128)(2,1)} %get-tuple-element.14.h_all, bf16[4,128,128]{2,1,0:T(8,128)(2,1)} %get-tuple-element.15.q_all, ...), custom_call_target="tpu_custom_call" | custom-call | flops 1342177280 | bytes 41943040 | tf_op jit(solution)/shard_map/layers_backward/pallas_call | solution.py:234
  331.0 14.1 %all_to_all.25 = bf16[16,32,256]{2,1,0:T(8,128)(2,1)S(1)} all-to-all(bf16[16,32,256]{2,1,0:T(8,128)(2,1)S(1)} %bitcast.56), channel_id=1, replica_groups=mesh['yh'=2,'x'=4,'z'=16,'yl'=2,'c'=2] {'x','yl','c'}, dimensions={0} | all-to-all | bytes 524288 | tf_op jit(solution)/shard_map/gather_grads/all_to_all | solution.py:323
  345.6 29.6 %all_to_all.26 = bf16[16,64,256]{2,1,0:T(8,128)(2,1)S(1)} all-to-all(bf16[16,64,256]{2,1,0:T(8,128)(2,1)S(1)} %bitcast.58), channel_id=1, replica_groups=mesh['yh'=2,'x'=4,'z'=16,'yl'=2,'c'=2] {'z'}, dimensions={0} | all-to-all | bytes 1048576 | tf_op jit(solution)/shard_map/sum_grads/all_to_all | solution.py:327
  376.5 24.2 %all_to_all.27 = f32[16,8,128]{2,1,0:T(8,128)S(1)} all-to-all(f32[16,8,128]{2,1,0:T(8,128)S(1)} %broadcast_in_dim.20), channel_id=1, replica_groups=mesh['yh'=2,'x'=4,'z'=16,'yl'=2,'c'=2] {'z'}, dimensions={0} | all-to-all | bytes 131072 | tf_op jit(solution)/shard_map/clip/all_to_all | solution.py:280
  400.7 14.6 %all_to_all.28 = f32[32,8,128]{2,1,0:T(8,128)S(1)} all-to-all(f32[32,8,128]{2,1,0:T(8,128)S(1)} %broadcast_in_dim.21), channel_id=1, replica_groups=mesh['yh'=2,'x'=4,'z'=16,'yl'=2,'c'=2] {'yh','x','yl','c'}, dimensions={0} | all-to-all | bytes 262144 | tf_op jit(solution)/shard_map/clip/all_to_all | solution.py:280
  (72 shorter events, 44.8 us)
Async XLA Ops:
  7.2 209.7 %copy-start = (s32[4,32]{1,0:T(4,128)S(1)}, s32[4,32]{1,0:T(4,128)}, u32[]{:S(2)}) copy-start(s32[4,32]{1,0:T(4,128)} %param.10) | copy-start | bytes 1540
  7.2 99.1 %all-gather.5.cloned.1.call-start = ((), (), s32[]{:S(2)}) async-start(), calls=%async_computation.5 | async-start | bytes 10813440 | tf_op jit(solution)/shard_map/gather_weights/all_gather | solution.py:265
  9.0 6.7 %collective-permute-start = (bf16[64,1280]{1,0:T(8,128)(2,1)S(1)}, bf16[64,1280]{1,0:T(8,128)(2,1)S(1)}, u32[]{:S(2)}, u32[]{:S(2)}) collective-permute-start(bf16[64,1280]{1,0:T(8,128)(2,1)S(1)} %pad_maximum_fusion.2), channel_id=1, source_target_pairs={{0,2},{2,0},{1,3},{3,1},{4,6},{6,4},{5,7},{7,5},{8,10},{10,8},{9,1... | collective-permute-start | bytes 491528 | tf_op jit(solution)/shard_map/gather_weights/ppermute | solution.py:255
  17.4 207.7 %all-gather.7.cloned.1.call-start = ((), (), s32[]{:S(2)}) async-start(), calls=%async_computation.6 | async-start | bytes 16220160 | tf_op jit(solution)/shard_map/gather_weights/all_gather | solution.py:268
  17.5 10.4 %collective-permute-start.3 = (bf16[2,32,1280]{2,1,0:T(8,128)(2,1)S(1)}, bf16[2,32,1280]{2,1,0:T(8,128)(2,1)S(1)}, u32[]{:S(2)}, u32[]{:S(2)}) collective-permute-start(bf16[2,32,1280]{2,1,0:T(8,128)(2,1)S(1)} %fusion), channel_id=1, source_target_pairs={{0,192},{64,0},{128,64},{192,128},{1,193},{65,1},{129,65},{193,129... | collective-permute-start | bytes 491528 | tf_op jit(solution)/shard_map/gather_weights/ppermute | solution.py:259
  23.0 7.6 %collective-permute-start.2 = (bf16[2,32,1280]{2,1,0:T(8,128)(2,1)S(1)}, bf16[2,32,1280]{2,1,0:T(8,128)(2,1)S(1)}, u32[]{:S(2)}, u32[]{:S(2)}) collective-permute-start(bf16[2,32,1280]{2,1,0:T(8,128)(2,1)S(1)} %fusion), channel_id=1, source_target_pairs={{0,128},{64,192},{128,0},{192,64},{1,129},{65,193},{129,1},{193,65... | collective-permute-start | bytes 491528 | tf_op jit(solution)/shard_map/gather_weights/ppermute | solution.py:259
  25.4 7.3 %collective-permute-start.1 = (bf16[2,32,1280]{2,1,0:T(8,128)(2,1)S(1)}, bf16[2,32,1280]{2,1,0:T(8,128)(2,1)S(1)}, u32[]{:S(2)}, u32[]{:S(2)}) collective-permute-start(bf16[2,32,1280]{2,1,0:T(8,128)(2,1)S(1)} %fusion), channel_id=1, source_target_pairs={{0,64},{64,128},{128,192},{192,0},{1,65},{65,129},{129,193},{193,1... | collective-permute-start | bytes 491528 | tf_op jit(solution)/shard_map/gather_weights/ppermute | solution.py:259
  108.2 60.2 %collective-permute-start.6 = (bf16[16,2,32,1280]{3,2,1,0:T(8,128)(2,1)S(1)}, bf16[16,2,32,1280]{3,2,1,0:T(8,128)(2,1)S(1)}, u32[]{:S(2)}, u32[]{:S(2)}) collective-permute-start(bf16[16,2,32,1280]{3,2,1,0:T(8,128)(2,1)S(1)} %dynamic-slice_bitcast_fusion), channel_id=1, source_target_pairs={{0,192},{64,0},{128,64},{192,128},{1,193},{65,1},{129,65},{193,129... | collective-permute-start | bytes 7864328 | tf_op jit(solution)/shard_map/gather_weights/ppermute | solution.py:259
  112.5 64.7 %collective-permute-start.4 = (bf16[16,2,32,1280]{3,2,1,0:T(8,128)(2,1)S(1)}, bf16[16,2,32,1280]{3,2,1,0:T(8,128)(2,1)}, u32[]{:S(2)}, u32[]{:S(2)}) collective-permute-start(bf16[16,2,32,1280]{3,2,1,0:T(8,128)(2,1)S(1)} %dynamic-slice_bitcast_fusion), channel_id=1, source_target_pairs={{0,64},{64,128},{128,192},{192,0},{1,65},{65,129},{129,193},{193,1... | collective-permute-start | bytes 7864328 | tf_op jit(solution)/shard_map/gather_weights/ppermute | solution.py:259
  168.6 32.5 %collective-permute-start.10 = (bf16[8,2,32,1280]{3,2,1,0:T(8,128)(2,1)S(1)}, bf16[8,2,32,1280]{3,2,1,0:T(8,128)(2,1)}, u32[]{:S(2)}, u32[]{:S(2)}) collective-permute-start(bf16[8,2,32,1280]{3,2,1,0:T(8,128)(2,1)S(1)} %slice.39), channel_id=1, source_target_pairs={{0,192},{64,0},{128,64},{192,128},{1,193},{65,1},{129,65},{193,129... | collective-permute-start | bytes 3932168 | tf_op jit(solution)/shard_map/gather_weights/ppermute | solution.py:259
  174.0 51.1 %collective-permute-start.7 = (bf16[16,2,32,1280]{3,2,1,0:T(8,128)(2,1)S(1)}, bf16[16,2,32,1280]{3,2,1,0:T(8,128)(2,1)}, u32[]{:S(2)}, u32[]{:S(2)}) collective-permute-start(bf16[16,2,32,1280]{3,2,1,0:T(8,128)(2,1)S(1)} %collective-permute-done.6.refs_4_), channel_id=1, source_target_pairs={{0,1},{1,0},{2,3},{3,2},{4,5},{5,4},{6,7},{7,6},{8,9},{9,8},{10,11... | collective-permute-start | bytes 7864328 | tf_op jit(solution)/shard_map/gather_weights/ppermute | solution.py:255
  178.6 46.5 %collective-permute-start.5 = (bf16[16,2,32,1280]{3,2,1,0:T(8,128)(2,1)}, bf16[16,2,32,1280]{3,2,1,0:T(8,128)(2,1)}, u32[]{:S(2)}, u32[]{:S(2)}) collective-permute-start(bf16[16,2,32,1280]{3,2,1,0:T(8,128)(2,1)} %collective-permute-done.4.refs_2_), channel_id=1, source_target_pairs={{0,1},{1,0},{2,3},{3,2},{4,5},{5,4},{6,7},{7,6},{8,9},{9,8},{10,11... | collective-permute-start | bytes 7864328 | tf_op jit(solution)/shard_map/gather_weights/ppermute | solution.py:255
  180.6 33.1 %collective-permute-start.8 = (bf16[8,2,32,1280]{3,2,1,0:T(8,128)(2,1)S(1)}, bf16[8,2,32,1280]{3,2,1,0:T(8,128)(2,1)}, u32[]{:S(2)}, u32[]{:S(2)}) collective-permute-start(bf16[8,2,32,1280]{3,2,1,0:T(8,128)(2,1)S(1)} %slice.38), channel_id=1, source_target_pairs={{0,64},{64,128},{128,192},{192,0},{1,65},{65,129},{129,193},{193,1... | collective-permute-start | bytes 3932168 | tf_op jit(solution)/shard_map/gather_weights/ppermute | solution.py:259
  201.1 24.1 %collective-permute-start.11 = (bf16[8,2,32,1280]{3,2,1,0:T(8,128)(2,1)}, bf16[8,2,32,1280]{3,2,1,0:T(8,128)(2,1)}, u32[]{:S(2)}, u32[]{:S(2)}) collective-permute-start(bf16[8,2,32,1280]{3,2,1,0:T(8,128)(2,1)} %collective-permute-done.10.refs_8_), channel_id=1, source_target_pairs={{0,1},{1,0},{2,3},{3,2},{4,5},{5,4},{6,7},{7,6},{8,9},{9,8},{10,11... | collective-permute-start | bytes 3932168 | tf_op jit(solution)/shard_map/gather_weights/ppermute | solution.py:255
  213.6 11.5 %collective-permute-start.9 = (bf16[8,2,32,1280]{3,2,1,0:T(8,128)(2,1)}, bf16[8,2,32,1280]{3,2,1,0:T(8,128)(2,1)}, u32[]{:S(2)}, u32[]{:S(2)}) collective-permute-start(bf16[8,2,32,1280]{3,2,1,0:T(8,128)(2,1)} %collective-permute-done.8.refs_6_), channel_id=1, source_target_pairs={{0,1},{1,0},{2,3},{3,2},{4,5},{5,4},{6,7},{7,6},{8,9},{9,8},{10,11... | collective-permute-start | bytes 3932168 | tf_op jit(solution)/shard_map/gather_weights/ppermute | solution.py:255
  225.2 29.8 %copy-start.3 = (bf16[32,4096]{1,0:T(8,128)(2,1)S(1)}, bf16[32,4096]{1,0:T(8,128)(2,1)}, u32[]{:S(2)}) copy-start(bf16[32,4096]{1,0:T(8,128)(2,1)} %reshape.108.h_ref) | copy-start | bytes 786436
  243.4 11.5 %collective-permute-start.12 = (bf16[32,4096]{1,0:T(8,128)(2,1)}, bf16[32,4096]{1,0:T(8,128)(2,1)S(1)}, u32[]{:S(2)}, u32[]{:S(2)}) collective-permute-start(bf16[32,4096]{1,0:T(8,128)(2,1)} %get-tuple-element.13), channel_id=1, source_target_pairs={{0,256},{256,0},{1,257},{257,1},{2,258},{258,2},{3,259},{259,3},{4... | collective-permute-start | bytes 786440 | tf_op jit(solution)/shard_map/ppermute | solution.py:255
  277.0 24.7 %all-to-all-start = ((bf16[16,32,1024]{2,1,0:T(8,128)(2,1)}), bf16[16,32,1024]{2,1,0:T(8,128)(2,1)S(1)}, u32[]{:S(2)}, u32[]{:S(2)}) async-start(bf16[16,32,1024]{2,1,0:T(8,128)(2,1)} %bitcast.18), calls=%async_computation | async-start | bytes 2097152 | tf_op jit(solution)/shard_map/normed_slices/all_to_all | solution.py:314
  283.1 29.7 %copy-start.4 = (bf16[32,4096]{1,0:T(8,128)(2,1)S(1)}, bf16[32,4096]{1,0:T(8,128)(2,1)}, u32[]{:S(2)}) copy-start(bf16[32,4096]{1,0:T(8,128)(2,1)} %reshape.106.up_ref) | copy-start | bytes 786436
  301.7 11.1 %collective-permute-start.13 = (bf16[32,4096]{1,0:T(8,128)(2,1)}, bf16[32,4096]{1,0:T(8,128)(2,1)S(1)}, u32[]{:S(2)}, u32[]{:S(2)}) collective-permute-start(bf16[32,4096]{1,0:T(8,128)(2,1)} %get-tuple-element.22), channel_id=1, source_target_pairs={{0,256},{256,0},{1,257},{257,1},{2,258},{258,2},{3,259},{259,3},{4... | collective-permute-start | bytes 786440 | tf_op jit(solution)/shard_map/ppermute | solution.py:255
  331.0 85.6 %copy-start.5 = (f32[1,2,64,128]{3,2,1,0:T(8,128)S(1)}, f32[1,2,64,128]{3,2,1,0:T(8,128)}, u32[]{:S(2)}) copy-start(f32[1,2,64,128]{3,2,1,0:T(8,128)} %param.13) | copy-start | bytes 196612
  331.0 85.6 %copy-start.6 = (f32[1,2,64,128]{3,2,1,0:T(8,128)S(1)}, f32[1,2,64,128]{3,2,1,0:T(8,128)}, u32[]{:S(2)}) copy-start(f32[1,2,64,128]{3,2,1,0:T(8,128)} %param.15) | copy-start | bytes 196612
  331.0 85.6 %copy-start.7 = (f32[1,2,64,128]{3,2,1,0:T(8,128)S(1)}, f32[1,2,64,128]{3,2,1,0:T(8,128)}, u32[]{:S(2)}) copy-start(f32[1,2,64,128]{3,2,1,0:T(8,128)} %param.14) | copy-start | bytes 196612
  345.1 72.2 %copy-start.1 = (s32[4,32]{1,0:T(4,128)S(1)}, s32[4,32]{1,0:T(4,128)}, u32[]{:S(2)}) copy-start(s32[4,32]{1,0:T(4,128)} %param.10) | copy-start | bytes 1540
  (1 other events, 10.2 us)
Sparse Core Ops, SparseCore 0:
  17.6 88.6 all-gather.4
  108.4 99.3 all-gather.6

commit v4 on v3

--- a/solution.py
+++ b/solution.py
@@ -28,7 +28,7 @@
 COLS = KVW + QW
 CHUNK = 1024
 UPPER = 32
-SOURCES = 10
+SOURCES = 14
 SCALE = 1.0 / math.sqrt(HEAD)
 VMEM_LIMIT = 60 * 1024 * 1024
 F32 = jnp.float32
@@ -61,17 +61,12 @@
     start(rest.at[:, c, distance - 1, yl], target.at[:, UPPER:])
     upper = target.at[:, :UPPER]
     for own in range(2):
-        near, far, twice, back = moved[own::2]
 
         @pl.when((core == c) == (own == 0))
-        def _(near=near, far=far, twice=twice, back=back):
-            if distance == 1:
-                start(near.at[:, yl], upper)
-            elif distance == 3:
-                start(far.at[:, yl], upper)
-            else:
-                start(twice.at[:, yl], upper.at[:8])
-                start(back.at[:, yl], upper.at[8:])
+        def _(own=own):
+            for half in range(2):
+                block = moved[(distance - 1) * 4 + half * 2 + own]
+                start(block.at[:, yl], upper.at[half * 8 : half * 8 + 8])
 
 
 def start_layers(order, place, sources, w_vmem, sems):
@@ -110,15 +105,14 @@
     return w_vmem[layer, at // CHUNK, :, :, first:last].reshape(CHUNK, last - first)
 
 
-def forward_kernel(place, h_ref, seg_col, seg_row, *refs):
-    sources, refs = refs[:SOURCES], refs[SOURCES:]
-    out_ref, h_all, n_all, q_all, k_all, v_all, p_all, w_vmem, sems = refs
-    start_layers(range(LAYERS), place, sources, w_vmem, sems)
+def attention_mask(seg_col, seg_row):
     row_ids = lax.broadcasted_iota(jnp.int32, (LENGTH, LENGTH), 0)
     col_ids = lax.broadcasted_iota(jnp.int32, (LENGTH, LENGTH), 1)
     allowed = ((seg_col[...] == seg_row[...]) & (col_ids <= row_ids)).astype(F32)
-    mask = jnp.concatenate([allowed] * HEADS, axis=0) > 0.0
-    h_all[0] = h_ref[...]
+    return jnp.concatenate([allowed] * HEADS, axis=0) > 0.0
+
+
+def forward_layers(mask, h_all, n_all, kept, out_ref, w_vmem, sems):
     for layer in range(LAYERS):
         inverse = inverse_norm(h_all, layer)
         for at in range(0, WIDTH, CHUNK):
@@ -138,10 +132,11 @@
         exp_scores = jnp.where(mask, jnp.exp(scores), 0.0)
         probs = exp_scores / jnp.sum(exp_scores, axis=-1, keepdims=True)
         context = unstack_heads(dot_nn(probs.astype(BF16), values).astype(BF16))
-        q_all[layer] = query
-        k_all[layer] = keys
-        v_all[layer] = values
-        p_all[layer] = probs
+        if kept is not None:
+            for ref, value in zip(kept, (query, keys, values, probs)):
+                ref[layer] = value
+        if out_ref is None and layer + 1 == LAYERS:
+            return
         for at in range(0, WIDTH, CHUNK):
             signal = h_all[layer, :, at : at + CHUNK].astype(F32)
             branch = dot_nt(context, weight_rows(w_vmem, layer, at, KVW, COLS))
@@ -152,30 +147,27 @@
                 out_ref[:, at : at + CHUNK] = result
 
 
-def backward_kernel(need_up, place, up_ref, h_all, q_all, k_all, v_all, p_all, *refs):
-    sources, refs = refs[:SOURCES], refs[SOURCES:]
-    out_ref, g_all, w_vmem, gn, sems = refs
-    start_layers(reversed(range(LAYERS)), place, sources, w_vmem, sems)
-    out_ref[...] = up_ref[...]
+def backward_layers(need_up, h_all, kept, up, g_all, w_vmem, gn, sems):
+    q_all, k_all, v_all, p_all = kept
     for layer in reversed(range(LAYERS)):
         acc = jnp.zeros((LENGTH, QW), F32)
         for at in range(0, WIDTH, CHUNK):
-            wait_rows(w_vmem, sems, layer, at)
-            acc = acc + dot_nn(
-                out_ref[:, at : at + CHUNK], weight_rows(w_vmem, layer, at, KVW, COLS)
-            )
+            if sems is not None:
+                wait_rows(w_vmem, sems, layer, at)
+            acc = acc + dot_nn(up[:, at : at + CHUNK], weight_rows(w_vmem, layer, at, KVW, COLS))
         grad_context = stack_heads(acc.astype(BF16))
         query, keys, values, probs = q_all[layer], k_all[layer], v_all[layer], p_all[layer]
         grad_probs = dot_nt(grad_context, values)
-        grad_values = dot_tn(probs.astype(BF16), grad_context).astype(BF16)
         centred = grad_probs - jnp.sum(probs * grad_probs, axis=-1, keepdims=True)
         grad_scores = (probs * centred * SCALE).astype(BF16)
+        grad_keys = dot_tn(grad_scores, query).astype(BF16)
+        grad_values = dot_tn(probs.astype(BF16), grad_context).astype(BF16)
+        if g_all is not None:
+            g_all[layer, :, :HEAD] = grad_keys
+            g_all[layer, :, HEAD:] = grad_values
+        if layer == 0 and not need_up:
+            return
         grad_query = unstack_heads(dot_nn(grad_scores, keys).astype(BF16))
-        grad_keys = dot_tn(grad_scores, query).astype(BF16)
-        g_all[layer, :, :HEAD] = grad_keys
-        g_all[layer, :, HEAD:] = grad_values
-        if layer == 0 and not need_up:
-            continue
         grads = jnp.concatenate([grad_query, grad_keys, grad_values], axis=1)
         inverse = inverse_norm(h_all, layer)
         total = jnp.zeros((LENGTH, 1), F32)
@@ -187,10 +179,54 @@
         pull = inverse * inverse * inverse * (total * (1.0 / WIDTH))
         for at in range(0, WIDTH, CHUNK):
             signal = h_all[layer, :, at : at + CHUNK].astype(F32)
-            upstream = out_ref[:, at : at + CHUNK].astype(F32)
-            out_ref[:, at : at + CHUNK] = (
+            upstream = up[:, at : at + CHUNK].astype(F32)
+            up[:, at : at + CHUNK] = (
                 upstream + inverse * gn[:, at : at + CHUNK] - signal * pull
             ).astype(BF16)
+
+
+def first_kernel(place, h_ref, seg_col, seg_row, *refs):
+    sources, refs = refs[:SOURCES], refs[SOURCES:]
+    out_ref, h_all, n_all, w_vmem, sems = refs
+    start_layers(range(LAYERS), place, sources, w_vmem, sems)
+    h_all[0] = h_ref[...]
+    forward_layers(attention_mask(seg_col, seg_row), h_all, n_all, None, out_ref, w_vmem, sems)
+
+
+def middle_kernel(place, h_ref, arrived, up_ref, seg_col, seg_row, *refs):
+    sources, refs = refs[:SOURCES], refs[SOURCES:]
+    out_ref, h_all, n_all, q_all, k_all, v_all, p_all, w_vmem, gn, sems = refs
+    start_layers(range(LAYERS), place, sources, w_vmem, sems)
+
+    @pl.when(place[2] == 1)
+    def _():
+        h_all[0] = arrived[...]
+
+    @pl.when(place[2] == 0)
+    def _():
+        h_all[0] = h_ref[...]
+
+    out_ref[...] = up_ref[...]
+    kept = (q_all, k_all, v_all, p_all)
+    forward_layers(attention_mask(seg_col, seg_row), h_all, n_all, kept, None, w_vmem, sems)
+    backward_layers(True, h_all, kept, out_ref, None, w_vmem, gn, None)
+
+
+def last_kernel(place, up_ref, arrived, h_all, q_all, k_all, v_all, p_all, *refs):
+    sources, refs = refs[:SOURCES], refs[SOURCES:]
+    g_all, up, w_vmem, gn, sems = refs
+    start_layers(reversed(range(LAYERS)), place, sources, w_vmem, sems)
+
+    @pl.when(place[2] == 0)
+    def _():
+        up[...] = arrived[...]
+
+    @pl.when(place[2] == 1)
+    def _():
+        up[...] = up_ref[...]
+
+    kept = (q_all, k_all, v_all, p_all)
+    backward_layers(False, h_all, kept, up, g_all, w_vmem, gn, sems)
 
 
 VM = pl.BlockSpec(memory_space=pltpu.VMEM)
@@ -198,6 +234,9 @@
 ANY = pl.BlockSpec(memory_space=pl.ANY)
 WEIGHT_SCRATCH = pltpu.VMEM((LAYERS, WIDTH // CHUNK, 16, 64, COLS), BF16)
 WEIGHT_SEMS = pltpu.SemaphoreType.DMA((LAYERS, WIDTH // CHUNK))
+ROWS = jax.ShapeDtypeStruct((LENGTH, WIDTH), BF16)
+ROWS_F32 = pltpu.VMEM((LENGTH, WIDTH), F32)
+ROWS_ALL = pltpu.VMEM((LAYERS, LENGTH, WIDTH), BF16)
 STATE_SHAPES = (
     jax.ShapeDtypeStruct((LAYERS, LENGTH, WIDTH), BF16),
     jax.ShapeDtypeStruct((LAYERS, LENGTH, WIDTH), BF16),
@@ -216,34 +255,17 @@
     )
 
 
-def run_forward(place, h, seg_col, seg_row, weights):
+def call(kernel, name, products, out_shape, inputs, sources, scratch):
     return pl.pallas_call(
-        forward_kernel,
-        out_shape=(jax.ShapeDtypeStruct((LENGTH, WIDTH), BF16),) + STATE_SHAPES,
-        in_specs=[SM, VM, VM, VM] + [ANY] * SOURCES,
-        out_specs=(VM,) * 7,
-        scratch_shapes=[WEIGHT_SCRATCH, WEIGHT_SEMS],
+        kernel,
+        out_shape=out_shape,
+        in_specs=[SM] + [VM] * (len(inputs) - 1) + [ANY] * SOURCES,
+        out_specs=(VM,) * len(out_shape),
+        scratch_shapes=scratch,
         compiler_params=pltpu.CompilerParams(vmem_limit_bytes=VMEM_LIMIT),
-        cost_estimate=cost(LAYERS),
-        name="layers_forward",
-    )(place, h, seg_col, seg_row, *weights)
-
-
-def run_backward(place, upstream, states, weights, need_up):
-    h_all, n_all, q_all, k_all, v_all, p_all = states
-    return pl.pallas_call(
-        functools.partial(backward_kernel, need_up),
-        out_shape=(
-            jax.ShapeDtypeStruct((LENGTH, WIDTH), BF16),
-            jax.ShapeDtypeStruct((LAYERS, LENGTH, 2 * HEAD), BF16),
-        ),
-        in_specs=[SM] + [VM] * 6 + [ANY] * SOURCES,
-        out_specs=(VM, VM),
-        scratch_shapes=[WEIGHT_SCRATCH, pltpu.VMEM((LENGTH, WIDTH), F32), WEIGHT_SEMS],
-        compiler_params=pltpu.CompilerParams(vmem_limit_bytes=VMEM_LIMIT),
-        cost_estimate=cost(LAYERS),
-        name="layers_backward",
-    )(place, upstream, h_all, q_all, k_all, v_all, p_all, *weights)
+        cost_estimate=cost(products),
+        name=name,
+    )(*inputs, *sources)
 
 
 def reorder(rows):
@@ -259,18 +281,27 @@
     return lax.ppermute(block, "x", [(i, (i + distance) % 4) for i in range(4)])
 
 
-def gather_layers(own, yl, c):
+def across(block):
+    return lax.ppermute(block, ("yh", "yl"), [(i, 3 - i) for i in range(4)])
+
+
+def pair_rows(own, yl):
     other = swap(own, "yl")
-    pair = jnp.stack([jnp.where(yl == 0, own, other), jnp.where(yl == 0, other, own)])
+    return jnp.stack([jnp.where(yl == 0, own, other), jnp.where(yl == 0, other, own)])
+
+
+def gather_layers(pair, lower, c):
     whole = lax.all_gather(pair, ("z", "c"), axis=0).reshape(16, 2, 2, 64, COLS)
-    lower = pair[:, UPPER:]
     lower = jnp.stack([turned(lower, distance) for distance in range(1, 4)])
     rest = lax.all_gather(lower, ("z", "c"), axis=0).reshape(16, 2, 3, 2, 64 - UPPER, COLS)
     share = lax.dynamic_slice(whole, (0, c, 0, 0, 0), (16, 1, 2, UPPER, COLS))[:, 0]
-    near, far = turned(share, 1), turned(share, 3)
-    twice, back = turned(near[:8], 1), turned(far[8:], 3)
+    low, high = share[:8], share[8:]
+    near_low, far_high = turned(low, 1), turned(high, 3)
+    near_low, far_high, low, high = lax.optimization_barrier((near_low, far_high, low, high))
+    twice_low, twice_high = turned(near_low, 1), turned(far_high, 3)
+    near_high, far_low = turned(high, 1), turned(low, 3)
     moved = []
-    for block in (near, far, twice, back):
+    for block in (near_low, near_high, twice_low, twice_high, far_low, far_high):
         moved += [block, swap(block, "c")]
     return [whole, rest] + moved
 
@@ -283,7 +314,7 @@
 def shards(
     inputs, out_grad, doc_ids, query_weight, out_weight, master, first_moment, second_moment
 ):
-    yh, x = lax.axis_index("yh"), lax.axis_index("x")
+    yh, x, yl, c = (lax.axis_index(name) for name in ("yh", "x", "yl", "c"))
     own = jnp.concatenate(
         [
             query_weight[0],
@@ -293,29 +324,54 @@
         ],
         axis=1,
     )
-    with jax.named_scope("gather_weights"):
-        weights = gather_layers(own, lax.axis_index("yl"), lax.axis_index("c"))
-    place = jnp.stack([x, lax.axis_index("c")]).astype(jnp.int32)
-
+    segment = lax.dynamic_index_in_dim(doc_ids, x, 0, keepdims=False)
     rows_in = reorder(lax.dynamic_index_in_dim(inputs, x, 0, keepdims=False))
     up_in = reorder(lax.dynamic_index_in_dim(out_grad, x, 0, keepdims=False))
-    segment = lax.dynamic_index_in_dim(doc_ids, x, 0, keepdims=False)
+    up_in = swap(up_in, "yl")
+    segment = jnp.where(yh == 1, swap(segment, "yl"), segment)
     seg_col, seg_row = segment[:, None], segment[None, :]
-
-    first_half = run_forward(place, rows_in, seg_col, seg_row, weights)[0]
-    arrived = swap(first_half, "yh")
-    layer_in = jnp.where(yh == 1, arrived, rows_in)
-    states = run_forward(place, layer_in, seg_col, seg_row, weights)[1:]
-
-    half_up = run_backward(place, up_in, states, weights, True)[0]
+    place = jnp.stack([x, c, yh]).astype(jnp.int32)
+    with jax.named_scope("gather_weights"):
+        pair = pair_rows(own, yl)
+        tied = lax.optimization_barrier(
+            (pair[:, UPPER:], place, rows_in, up_in, seg_col, seg_row)
+        )
+        lower, place, rows_in, up_in, seg_col, seg_row = tied
+        sources = gather_layers(pair, lower, c)
+
+    (arrived,) = call(
+        first_kernel,
+        "first_forward",
+        LAYERS,
+        (ROWS,),
+        (place, rows_in, seg_col, seg_row),
+        sources,
+        [ROWS_ALL, ROWS_ALL, WEIGHT_SCRATCH, WEIGHT_SEMS],
+    )
+    arrived = across(arrived)
+    half_up, h_all, n_all, *kept = call(
+        middle_kernel,
+        "second_forward_backward",
+        2 * LAYERS,
+        (ROWS,) + STATE_SHAPES,
+        (place, rows_in, arrived, up_in, seg_col, seg_row),
+        sources,
+        [WEIGHT_SCRATCH, ROWS_F32, WEIGHT_SEMS],
+    )
     with jax.named_scope("normed_slices"):
-        rows = states[1].reshape(LAYERS, LENGTH, 2, 2, CHUNK).transpose(0, 3, 2, 1, 4)
+        rows = n_all.reshape(LAYERS, LENGTH, 2, 2, CHUNK).transpose(0, 3, 2, 1, 4)
         rows = rows.reshape(4 * LAYERS, LENGTH, CHUNK)
         rows = lax.all_to_all(rows, PLANE, 0, 0, tiled=True).reshape(-1, CHUNK)
-        half_up, rows = lax.optimization_barrier((half_up, rows))
-    arrived = swap(half_up, "yh")
-    upstream = jnp.where(yh == 0, arrived, up_in)
-    grads = run_backward(place, upstream, states, weights, False)[1]
+    arrived = across(half_up)
+    (grads,) = call(
+        last_kernel,
+        "first_backward",
+        LAYERS,
+        (jax.ShapeDtypeStruct((LAYERS, LENGTH, 2 * HEAD), BF16),),
+        (place, up_in, arrived, h_all, *kept),
+        sources,
+        [pltpu.VMEM((LENGTH, WIDTH), BF16), WEIGHT_SCRATCH, ROWS_F32, WEIGHT_SEMS],
+    )
 
     with jax.named_scope("gather_grads"):
         cols = jnp.broadcast_to(grads[:, None], (LAYERS, 4, LENGTH, 2 * HEAD))

time: 425 us -> 422 us (level)
  starting transfers between devices: 54.4 us -> 76.3 us
  waiting for transfers between devices: 174 us -> 156 us
  Pallas kernels: 71.6 us -> 65.8 us
  blocking collectives: 82.4 us -> 87.8 us
  local copies, waits for them, and re-layouts: 18.1 us -> 13.1 us
    ppermute x7 -> x9, waiting for transfers between devices: 86.1 us -> 70.2 us  [turned(): return lax.ppermute(block, 'x', [(i, (i + distance) % 4) for i in range(4)])]
    all_gather x1, waiting for transfers between devices: 72.8 us -> 59.6 us  [gather_layers(): whole = lax.all_gather(pair, ('z', 'c'), axis=0).reshape(16, 2, 2, 64, COLS)]
    ppermute x0 -> x2, waiting for transfers between devices: none -> 12.1 us  [across(): return lax.ppermute(block, ('yh', 'yl'), [(i, 3 - i) for i in range(4)])]
    ppermute x0 -> x2, starting transfers between devices: none -> 9.14 us  [across(): return lax.ppermute(block, ('yh', 'yl'), [(i, 3 - i) for i in range(4)])]
    ppermute x7 -> x9, waiting for transfers between devices: 15.3 us -> 7.48 us  [swap(): return lax.ppermute(block, axis, [(0, 1), (1, 0)])]
    ppermute x7 -> x9, starting transfers between devices: 23.9 us -> 30.5 us  [turned(): return lax.ppermute(block, 'x', [(i, (i + distance) % 4) for i in range(4)])]
    all_to_all x1, waiting for transfers between devices: 0.01 us -> 6.26 us  [shards(): cols = lax.all_to_all(cols, PLANE, 0, 0, tiled=True).reshape(-1, 2 * HEAD)]
    pallas_call x4 -> x3, Pallas kernels: 71.6 us -> 65.8 us  [call(): pl.pallas_call(kernel, out_shape=out_shape, in_specs=[SM] + [VM] * (len(i...]
  transfers between devices with their start and end apart: 17 -> 23, of which waited for: 9 -> 13; matrix products, arithmetic and copies ran while one was open for 3% -> 2% of each run, Pallas kernels for 4% -> 0%
where the time goes in v4:
time: 422 us; the launch traced here: 421 us
  waiting for transfers between devices  156 us (37%)
  blocking collectives  87.8 us (21%)
  starting transfers between devices  76.3 us (18%)
  Pallas kernels  65.8 us (16%)
  between operations  15.2 us (4%)
  local copies, waits for them, and re-layouts  13.1 us (3%)
  other arithmetic  6.9 us (2%)
    ppermute x9, waiting for transfers between devices, turned(): return lax.ppermute(block, 'x', [(i, (i + distance) % 4) for i in range(4)])  70.2 us
    pallas_call x3, Pallas kernels, call(): pl.pallas_call(kernel, out_shape=out_shape, in_specs=[SM] + [VM] * (len(i...  65.8 us
    all_gather x1, waiting for transfers between devices, gather_layers(): whole = lax.all_gather(pair, ('z', 'c'), axis=0).reshape(16, 2, 2, 64, COLS)  59.6 us
    all_to_all x2, blocking collectives, sum_over(): return jnp.sum(lax.all_to_all(spread, axes, 0, 0, tiled=True), axis=0)  40.1 us
    ppermute x9, starting transfers between devices, turned(): return lax.ppermute(block, 'x', [(i, (i + distance) % 4) for i in range(4)])  30.5 us
    ppermute x9, starting transfers between devices, swap(): return lax.ppermute(block, axis, [(0, 1), (1, 0)])  30.2 us
    all_to_all x1, blocking collectives, shards(): parts = lax.all_to_all(partial, 'z', 0, 0, tiled=True)  29.6 us
    all_to_all x1, blocking collectives, shards(): rows = lax.all_to_all(rows, PLANE, 0, 0, tiled=True).reshape(-1, CHUNK)  18.1 us
  transfers between devices with their start and end apart: 23, of which 13 were waited for; matrix products, arithmetic and copies ran while one was open for 2% of the time, Pallas kernels for 0%

profile of v4, /device:TPU:1, one launch (start us, length us, event | category | flops | bytes accessed | tf_op | source)
XLA Modules:
  0.0 421.2 jit_solution(9927755750264971860)
XLA Ops:
  9.0 4.0 collective-permute-start
  30.2 4.8 %collective-permute-start.3 = (bf16[2,32,1280]{2,1,0:T(8,128)(2,1)S(1)}, bf16[2,32,1280]{2,1,0:T(8,128)(2,1)S(1)}, u32[]{:S(2)}, u32[]{:S(2)}) collective-permute-start(bf16[2,32,1280]{2,1,0:T(8,128)(2,1)S(1)} %fusion.1), channel_id=1, source_target_pairs={{0,64},{64,128},{128,192},{192,0},{1,65},{65,129},{129,193},{193,1... | collective-permute-start | bytes 491528 | tf_op jit(solution)/shard_map/gather_weights/ppermute | solution.py:281
  34.9 4.4 %collective-permute-start.4 = (bf16[2,32,1280]{2,1,0:T(8,128)(2,1)S(1)}, bf16[2,32,1280]{2,1,0:T(8,128)(2,1)S(1)}, u32[]{:S(2)}, u32[]{:S(2)}) collective-permute-start(bf16[2,32,1280]{2,1,0:T(8,128)(2,1)S(1)} %fusion.1), channel_id=1, source_target_pairs={{0,128},{64,192},{128,0},{192,64},{1,129},{65,193},{129,1},{193,65... | collective-permute-start | bytes 491528 | tf_op jit(solution)/shard_map/gather_weights/ppermute | solution.py:281
  46.6 59.6 %all-gather.5.cloned.1.call-done = bf16[64,64,1280]{2,1,0:T(8,128)(2,1)} async-done(((bf16[2,64,1280]{2,1,0:T(8,128)(2,1)}), bf16[64,64,1280]{2,1,0:T(8,128)(2,1)}) %all-gather.5.cloned.1.call-update) | async-done | bytes 10485776 | tf_op jit(solution)/shard_map/gather_weights/all_gather | solution.py:294
  114.7 26.8 %collective-permute-done.6.refs_2_ = bf16[8,2,32,1280]{3,2,1,0:T(8,128)(2,1)S(1)} collective-permute-done((bf16[8,2,32,1280]{3,2,1,0:T(8,128)(2,1)S(1)}, bf16[8,2,32,1280]{3,2,1,0:T(8,128)(2,1)S(1)}, u32[]{:S(2)}, u32[]{:S(2)}) %collective-permute-start.6) | collective-permute-done | bytes 1310752 | tf_op jit(solution)/shard_map/gather_weights/ppermute | solution.py:281
  149.2 3.8 collective-permute-start.13
  154.9 4.3 %collective-permute-start.17 = (bf16[8,2,32,1280]{3,2,1,0:T(8,128)(2,1)S(1)}, bf16[8,2,32,1280]{3,2,1,0:T(8,128)(2,1)S(1)}, u32[]{:S(2)}, u32[]{:S(2)}) collective-permute-start(bf16[8,2,32,1280]{3,2,1,0:T(8,128)(2,1)S(1)} %collective-permute-done.7.refs_12_), channel_id=1, source_target_pairs={{0,1},{1,0},{2,3},{3,2},{4,5},{5,4},{6,7},{7,6},{8,9},{9,8},{10,11... | collective-permute-start | bytes 3932168 | tf_op jit(solution)/shard_map/gather_weights/ppermute | solution.py:277
  159.2 16.2 %collective-permute-done.9.refs_4_ = bf16[8,2,32,1280]{3,2,1,0:T(8,128)(2,1)} collective-permute-done((bf16[8,2,32,1280]{3,2,1,0:T(8,128)(2,1)S(1)}, bf16[8,2,32,1280]{3,2,1,0:T(8,128)(2,1)}, u32[]{:S(2)}, u32[]{:S(2)}) %collective-permute-start.9) | collective-permute-done | bytes 1310752 | tf_op jit(solution)/shard_map/gather_weights/ppermute | solution.py:281
  175.4 5.8 %collective-permute-start.8 = (bf16[8,2,32,1280]{3,2,1,0:T(8,128)(2,1)S(1)}, bf16[8,2,32,1280]{3,2,1,0:T(8,128)(2,1)}, u32[]{:S(2)}, u32[]{:S(2)}) collective-permute-start(bf16[8,2,32,1280]{3,2,1,0:T(8,128)(2,1)S(1)} %collective-permute-done.6.refs_2_), channel_id=1, source_target_pairs={{0,1},{1,0},{2,3},{3,2},{4,5},{5,4},{6,7},{7,6},{8,9},{9,8},{10,11... | collective-permute-start | bytes 3932168 | tf_op jit(solution)/shard_map/gather_weights/ppermute | solution.py:277
  181.2 22.3 %collective-permute-done.11.refs_6_ = bf16[8,2,32,1280]{3,2,1,0:T(8,128)(2,1)} collective-permute-done((bf16[8,2,32,1280]{3,2,1,0:T(8,128)(2,1)S(1)}, bf16[8,2,32,1280]{3,2,1,0:T(8,128)(2,1)}, u32[]{:S(2)}, u32[]{:S(2)}) %collective-permute-start.11) | collective-permute-done | bytes 1310752 | tf_op jit(solution)/shard_map/gather_weights/ppermute | solution.py:281
  203.5 4.1 collective-permute-start.10
  218.8 18.0 %first_forward.1 = bf16[32,4096]{1,0:T(8,128)(2,1)} custom-call(s32[3]{0:T(128)} %pad_add_fusion.place, bf16[32,4096]{1,0:T(8,128)(2,1)} %reshape.103.h_ref, s32[32,1]{1,0:T(8,128)} %copy.31.seg_col, s32[1,32]{1,0:T(1,128)} %get-tuple-element.22.seg_row, bf16[16,2,2,64,1280]{4,3,2,1,0:T(8,128)(2,1)} %bitcast.64, bf16[16,2,3,2,32,1280]{5,4,3,2,1,0:T(8,128)(2,1)} %bitcast.60, ...), custom_call_target="tpu_custom_call" | custom-call | flops 1342177280 | bytes 41943040 | tf_op jit(solution)/shard_map/first_forward/pallas_call | solution.py:259
  236.8 4.6 %collective-permute-start.18 = (bf16[32,4096]{1,0:T(8,128)(2,1)}, bf16[32,4096]{1,0:T(8,128)(2,1)S(1)}, u32[]{:S(2)}, u32[]{:S(2)}) collective-permute-start(bf16[32,4096]{1,0:T(8,128)(2,1)} %first_forward.1), channel_id=1, source_target_pairs={{0,258},{2,256},{256,2},{258,0},{1,259},{3,257},{257,3},{259,1},{4... | collective-permute-start | bytes 786440 | tf_op jit(solution)/shard_map/ppermute | solution.py:285
  241.4 6.5 %collective-permute-done.18.arrived = bf16[32,4096]{1,0:T(8,128)(2,1)S(1)} collective-permute-done((bf16[32,4096]{1,0:T(8,128)(2,1)}, bf16[32,4096]{1,0:T(8,128)(2,1)S(1)}, u32[]{:S(2)}, u32[]{:S(2)}) %collective-permute-start.18) | collective-permute-done | bytes 262176 | tf_op jit(solution)/shard_map/ppermute | solution.py:285
  248.6 30.8 %second_forward_backward.1 = (bf16[32,4096]{1,0:T(8,128)(2,1)}, bf16[4,32,4096]{2,1,0:T(8,128)(2,1)}, bf16[4,32,4096]{2,1,0:T(8,128)(2,1)}, bf16[4,128,128]{2,1,...) custom-call(s32[3]{0:T(128)} %pad_add_fusion.place, ...), custom_call_target="tpu_custom_call" | custom-call | flops 2684354560 | bytes 41943040 | tf_op jit(solution)/shard_map/second_forward_backward/pallas_call | solution.py:259
  279.4 4.6 %collective-permute-start.19 = (bf16[32,4096]{1,0:T(8,128)(2,1)}, bf16[32,4096]{1,0:T(8,128)(2,1)S(1)}, u32[]{:S(2)}, u32[]{:S(2)}) collective-permute-start(bf16[32,4096]{1,0:T(8,128)(2,1)} %get-tuple-element.30), channel_id=1, source_target_pairs={{0,258},{2,256},{256,2},{258,0},{1,259},{3,257},{257,3},{259,1},{4... | collective-permute-start | bytes 786440 | tf_op jit(solution)/shard_map/ppermute | solution.py:285
  284.0 5.6 %collective-permute-done.19.arrived = bf16[32,4096]{1,0:T(8,128)(2,1)S(1)} collective-permute-done((bf16[32,4096]{1,0:T(8,128)(2,1)}, bf16[32,4096]{1,0:T(8,128)(2,1)S(1)}, u32[]{:S(2)}, u32[]{:S(2)}) %collective-permute-start.19) | collective-permute-done | bytes 262176 | tf_op jit(solution)/shard_map/ppermute | solution.py:285
  290.3 16.9 %first_backward.1 = bf16[4,32,256]{2,1,0:T(8,128)(2,1)} custom-call(s32[3]{0:T(128)} %pad_add_fusion.place, bf16[32,4096]{1,0:T(8,128)(2,1)} %copy-done.3, bf16[32,4096]{1,0:T(8,128)(2,1)} %copy-done.5, bf16[4,32,4096]{2,1,0:T(8,128)(2,1)} %get-tuple-element.31.h_all, bf16[4,128,128]{2,1,0:T(8,128)(2,1)} %get-tuple-element.32.q_all, ...), custom_call_target="tpu_custom_call" | custom-call | flops 1342177280 | bytes 41943040 | tf_op jit(solution)/shard_map/first_backward/pallas_call | solution.py:259
  308.8 6.5 %all-to-all-start.1 = ((bf16[16,32,256]{2,1,0:T(8,128)(2,1)}), bf16[16,32,256]{2,1,0:T(8,128)(2,1)S(1)}, u32[]{:S(2)}, u32[]{:S(2)}) async-start(bf16[16,32,256]{2,1,0:T(8,128)(2,1)} %bitcast.23), calls=%async_computation.1 | async-start | bytes 524288 | tf_op jit(solution)/shard_map/gather_grads/all_to_all | solution.py:379
  316.5 6.3 %all-to-all-done.1 = bf16[16,32,256]{2,1,0:T(8,128)(2,1)S(1)} async-done(((bf16[16,32,256]{2,1,0:T(8,128)(2,1)}), bf16[16,32,256]{2,1,0:T(8,128)(2,1)S(1)}, u32[]{:S(2)}, u32[]{:S(2)}) %all-to-all-start.1) | async-done | bytes 262176 | tf_op jit(solution)/shard_map/gather_grads/all_to_all | solution.py:379
  322.7 18.1 %all_to_all.25 = bf16[16,32,1024]{2,1,0:T(8,128)(2,1)S(1)} all-to-all(bf16[16,32,1024]{2,1,0:T(8,128)(2,1)S(1)} %bitcast.67), channel_id=1, replica_groups=mesh['yh'=2,'x'=4,'z'=16,'yl'=2,'c'=2] {'x','yl','c'}, dimensions={0} | all-to-all | bytes 2097152 | tf_op jit(solution)/shard_map/normed_slices/all_to_all | solution.py:364
  341.4 29.6 %all_to_all.26 = bf16[16,64,256]{2,1,0:T(8,128)(2,1)S(1)} all-to-all(bf16[16,64,256]{2,1,0:T(8,128)(2,1)S(1)} %bitcast.71), channel_id=1, replica_groups=mesh['yh'=2,'x'=4,'z'=16,'yl'=2,'c'=2] {'z'}, dimensions={0} | all-to-all | bytes 1048576 | tf_op jit(solution)/shard_map/sum_grads/all_to_all | solution.py:383
  372.3 23.5 %all_to_all.27 = f32[16,8,128]{2,1,0:T(8,128)S(1)} all-to-all(f32[16,8,128]{2,1,0:T(8,128)S(1)} %broadcast_in_dim.23), channel_id=1, replica_groups=mesh['yh'=2,'x'=4,'z'=16,'yl'=2,'c'=2] {'z'}, dimensions={0} | all-to-all | bytes 131072 | tf_op jit(solution)/shard_map/clip/all_to_all | solution.py:311
  395.9 16.6 %all_to_all.28 = f32[32,8,128]{2,1,0:T(8,128)S(1)} all-to-all(f32[32,8,128]{2,1,0:T(8,128)S(1)} %broadcast_in_dim.24), channel_id=1, replica_groups=mesh['yh'=2,'x'=4,'z'=16,'yl'=2,'c'=2] {'yh','x','yl','c'}, dimensions={0} | all-to-all | bytes 262144 | tf_op jit(solution)/shard_map/clip/all_to_all | solution.py:311
  (85 shorter events, 62.6 us)
Async XLA Ops:
  7.2 99.1 %all-gather.5.cloned.1.call-start = ((), (), s32[]{:S(2)}) async-start(), calls=%async_computation.5 | async-start | bytes 10813440 | tf_op jit(solution)/shard_map/gather_weights/all_gather | solution.py:294
  9.0 6.7 %collective-permute-start = (bf16[64,1280]{1,0:T(8,128)(2,1)S(1)}, bf16[64,1280]{1,0:T(8,128)(2,1)S(1)}, u32[]{:S(2)}, u32[]{:S(2)}) collective-permute-start(bf16[64,1280]{1,0:T(8,128)(2,1)S(1)} %pad_maximum_fusion.2), channel_id=1, source_target_pairs={{0,2},{2,0},{1,3},{3,1},{4,6},{6,4},{5,7},{7,5},{8,10},{10,8},{9,1... | collective-permute-start | bytes 491528 | tf_op jit(solution)/shard_map/gather_weights/ppermute | solution.py:277
  17.4 201.3 %all-gather.7.cloned.1.call-start = ((), (), s32[]{:S(2)}) async-start(), calls=%async_computation.6 | async-start | bytes 16220160 | tf_op jit(solution)/shard_map/gather_weights/all_gather | solution.py:296
  17.5 10.0 %collective-permute-start.2 = (s32[32]{0:T(128)S(1)}, s32[32]{0:T(128)S(1)}, u32[]{:S(2)}, u32[]{:S(2)}) collective-permute-start(s32[32]{0:T(128)S(1)} %fusion.7), channel_id=1, source_target_pairs={{0,2},{2,0},{1,3},{3,1},{4,6},{6,4},{5,7},{7,5},{8,10},{10,8},{9,1... | collective-permute-start | bytes 392 | tf_op jit(solution)/shard_map/ppermute | solution.py:277
  23.0 7.1 %collective-permute-start.1 = (bf16[32,4096]{1,0:T(8,128)(2,1)S(1)}, bf16[32,4096]{1,0:T(8,128)(2,1)S(1)}, u32[]{:S(2)}, u32[]{:S(2)}) collective-permute-start(bf16[32,4096]{1,0:T(8,128)(2,1)S(1)} %reshape.105), channel_id=1, source_target_pairs={{0,2},{2,0},{1,3},{3,1},{4,6},{6,4},{5,7},{7,5},{8,10},{10,8},{9,1... | collective-permute-start | bytes 786440 | tf_op jit(solution)/shard_map/ppermute | solution.py:277
  30.2 78.0 %copy-start.3 = (bf16[32,4096]{1,0:T(8,128)(2,1)}, bf16[32,4096]{1,0:T(8,128)(2,1)S(1)}, u32[]{:S(2)}) copy-start(bf16[32,4096]{1,0:T(8,128)(2,1)S(1)} %collective-permute-done.1.up_ref) | copy-start | bytes 786436
  30.2 12.2 %collective-permute-start.3 = (bf16[2,32,1280]{2,1,0:T(8,128)(2,1)S(1)}, bf16[2,32,1280]{2,1,0:T(8,128)(2,1)S(1)}, u32[]{:S(2)}, u32[]{:S(2)}) collective-permute-start(bf16[2,32,1280]{2,1,0:T(8,128)(2,1)S(1)} %fusion.1), channel_id=1, source_target_pairs={{0,64},{64,128},{128,192},{192,0},{1,65},{65,129},{129,193},{193,1... | collective-permute-start | bytes 491528 | tf_op jit(solution)/shard_map/gather_weights/ppermute | solution.py:281
  34.9 8.6 %collective-permute-start.4 = (bf16[2,32,1280]{2,1,0:T(8,128)(2,1)S(1)}, bf16[2,32,1280]{2,1,0:T(8,128)(2,1)S(1)}, u32[]{:S(2)}, u32[]{:S(2)}) collective-permute-start(bf16[2,32,1280]{2,1,0:T(8,128)(2,1)S(1)} %fusion.1), channel_id=1, source_target_pairs={{0,128},{64,192},{128,0},{192,64},{1,129},{65,193},{129,1},{193,65... | collective-permute-start | bytes 491528 | tf_op jit(solution)/shard_map/gather_weights/ppermute | solution.py:281
  39.3 6.5 %collective-permute-start.5 = (bf16[2,32,1280]{2,1,0:T(8,128)(2,1)S(1)}, bf16[2,32,1280]{2,1,0:T(8,128)(2,1)S(1)}, u32[]{:S(2)}, u32[]{:S(2)}) collective-permute-start(bf16[2,32,1280]{2,1,0:T(8,128)(2,1)S(1)} %fusion.1), channel_id=1, source_target_pairs={{0,192},{64,0},{128,64},{192,128},{1,193},{65,1},{129,65},{193,129... | collective-permute-start | bytes 491528 | tf_op jit(solution)/shard_map/gather_weights/ppermute | solution.py:281
  108.2 33.3 %collective-permute-start.6 = (bf16[8,2,32,1280]{3,2,1,0:T(8,128)(2,1)S(1)}, bf16[8,2,32,1280]{3,2,1,0:T(8,128)(2,1)S(1)}, u32[]{:S(2)}, u32[]{:S(2)}) collective-permute-start(bf16[8,2,32,1280]{3,2,1,0:T(8,128)(2,1)S(1)} %get-tuple-element.27), channel_id=1, source_target_pairs={{0,64},{64,128},{128,192},{192,0},{1,65},{65,129},{129,193},{193,1... | collective-permute-start | bytes 3932168 | tf_op jit(solution)/shard_map/gather_weights/ppermute | solution.py:281
  111.2 31.9 %collective-permute-start.7 = (bf16[8,2,32,1280]{3,2,1,0:T(8,128)(2,1)S(1)}, bf16[8,2,32,1280]{3,2,1,0:T(8,128)(2,1)S(1)}, u32[]{:S(2)}, u32[]{:S(2)}) collective-permute-start(bf16[8,2,32,1280]{3,2,1,0:T(8,128)(2,1)S(1)} %get-tuple-element.25), channel_id=1, source_target_pairs={{0,192},{64,0},{128,64},{192,128},{1,193},{65,1},{129,65},{193,129... | collective-permute-start | bytes 3932168 | tf_op jit(solution)/shard_map/gather_weights/ppermute | solution.py:281
  143.1 32.3 %collective-permute-start.9 = (bf16[8,2,32,1280]{3,2,1,0:T(8,128)(2,1)S(1)}, bf16[8,2,32,1280]{3,2,1,0:T(8,128)(2,1)}, u32[]{:S(2)}, u32[]{:S(2)}) collective-permute-start(bf16[8,2,32,1280]{3,2,1,0:T(8,128)(2,1)S(1)} %get-tuple-element.25), channel_id=1, source_target_pairs={{0,64},{64,128},{128,192},{192,0},{1,65},{65,129},{129,193},{193,1... | collective-permute-start | bytes 3932168 | tf_op jit(solution)/shard_map/gather_weights/ppermute | solution.py:281
  146.4 57.0 %collective-permute-start.11 = (bf16[8,2,32,1280]{3,2,1,0:T(8,128)(2,1)S(1)}, bf16[8,2,32,1280]{3,2,1,0:T(8,128)(2,1)}, u32[]{:S(2)}, u32[]{:S(2)}) collective-permute-start(bf16[8,2,32,1280]{3,2,1,0:T(8,128)(2,1)S(1)} %collective-permute-done.6.refs_2_), channel_id=1, source_target_pairs={{0,64},{64,128},{128,192},{192,0},{1,65},{65,129},{129,193},{193,1... | collective-permute-start | bytes 3932168 | tf_op jit(solution)/shard_map/gather_weights/ppermute | solution.py:281
  149.2 58.4 %collective-permute-start.13 = (bf16[8,2,32,1280]{3,2,1,0:T(8,128)(2,1)S(1)}, bf16[8,2,32,1280]{3,2,1,0:T(8,128)(2,1)}, u32[]{:S(2)}, u32[]{:S(2)}) collective-permute-start(bf16[8,2,32,1280]{3,2,1,0:T(8,128)(2,1)S(1)} %collective-permute-done.7.refs_12_), channel_id=1, source_target_pairs={{0,192},{64,0},{128,64},{192,128},{1,193},{65,1},{129,65},{193,129... | collective-permute-start | bytes 3932168 | tf_op jit(solution)/shard_map/gather_weights/ppermute | solution.py:281
  152.9 56.5 %collective-permute-start.15 = (bf16[8,2,32,1280]{3,2,1,0:T(8,128)(2,1)S(1)}, bf16[8,2,32,1280]{3,2,1,0:T(8,128)(2,1)}, u32[]{:S(2)}, u32[]{:S(2)}) collective-permute-start(bf16[8,2,32,1280]{3,2,1,0:T(8,128)(2,1)S(1)} %get-tuple-element.27), channel_id=1, source_target_pairs={{0,192},{64,0},{128,64},{192,128},{1,193},{65,1},{129,65},{193,129... | collective-permute-start | bytes 3932168 | tf_op jit(solution)/shard_map/gather_weights/ppermute | solution.py:281
  154.9 57.4 %collective-permute-start.17 = (bf16[8,2,32,1280]{3,2,1,0:T(8,128)(2,1)S(1)}, bf16[8,2,32,1280]{3,2,1,0:T(8,128)(2,1)S(1)}, u32[]{:S(2)}, u32[]{:S(2)}) collective-permute-start(bf16[8,2,32,1280]{3,2,1,0:T(8,128)(2,1)S(1)} %collective-permute-done.7.refs_12_), channel_id=1, source_target_pairs={{0,1},{1,0},{2,3},{3,2},{4,5},{5,4},{6,7},{7,6},{8,9},{9,8},{10,11... | collective-permute-start | bytes 3932168 | tf_op jit(solution)/shard_map/gather_weights/ppermute | solution.py:277
  175.4 40.7 %collective-permute-start.8 = (bf16[8,2,32,1280]{3,2,1,0:T(8,128)(2,1)S(1)}, bf16[8,2,32,1280]{3,2,1,0:T(8,128)(2,1)}, u32[]{:S(2)}, u32[]{:S(2)}) collective-permute-start(bf16[8,2,32,1280]{3,2,1,0:T(8,128)(2,1)S(1)} %collective-permute-done.6.refs_2_), channel_id=1, source_target_pairs={{0,1},{1,0},{2,3},{3,2},{4,5},{5,4},{6,7},{7,6},{8,9},{9,8},{10,11... | collective-permute-start | bytes 3932168 | tf_op jit(solution)/shard_map/gather_weights/ppermute | solution.py:277
  203.5 12.7 %collective-permute-start.10 = (bf16[8,2,32,1280]{3,2,1,0:T(8,128)(2,1)}, bf16[8,2,32,1280]{3,2,1,0:T(8,128)(2,1)}, u32[]{:S(2)}, u32[]{:S(2)}) collective-permute-start(bf16[8,2,32,1280]{3,2,1,0:T(8,128)(2,1)} %collective-permute-done.9.refs_4_), channel_id=1, source_target_pairs={{0,1},{1,0},{2,3},{3,2},{4,5},{5,4},{6,7},{7,6},{8,9},{9,8},{10,11... | collective-permute-start | bytes 3932168 | tf_op jit(solution)/shard_map/gather_weights/ppermute | solution.py:277
  207.5 8.6 %collective-permute-start.12 = (bf16[8,2,32,1280]{3,2,1,0:T(8,128)(2,1)}, bf16[8,2,32,1280]{3,2,1,0:T(8,128)(2,1)}, u32[]{:S(2)}, u32[]{:S(2)}) collective-permute-start(bf16[8,2,32,1280]{3,2,1,0:T(8,128)(2,1)} %collective-permute-done.11.refs_6_), channel_id=1, source_target_pairs={{0,1},{1,0},{2,3},{3,2},{4,5},{5,4},{6,7},{7,6},{8,9},{9,8},{10,11... | collective-permute-start | bytes 3932168 | tf_op jit(solution)/shard_map/gather_weights/ppermute | solution.py:277
  209.5 6.7 %collective-permute-start.14 = (bf16[8,2,32,1280]{3,2,1,0:T(8,128)(2,1)}, bf16[8,2,32,1280]{3,2,1,0:T(8,128)(2,1)}, u32[]{:S(2)}, u32[]{:S(2)}) collective-permute-start(bf16[8,2,32,1280]{3,2,1,0:T(8,128)(2,1)} %collective-permute-done.13.refs_8_), channel_id=1, source_target_pairs={{0,1},{1,0},{2,3},{3,2},{4,5},{5,4},{6,7},{7,6},{8,9},{9,8},{10,11... | collective-permute-start | bytes 3932168 | tf_op jit(solution)/shard_map/gather_weights/ppermute | solution.py:277
  213.5 5.3 %collective-permute-start.16 = (bf16[8,2,32,1280]{3,2,1,0:T(8,128)(2,1)}, bf16[8,2,32,1280]{3,2,1,0:T(8,128)(2,1)}, u32[]{:S(2)}, u32[]{:S(2)}) collective-permute-start(bf16[8,2,32,1280]{3,2,1,0:T(8,128)(2,1)} %collective-permute-done.15.refs_10_), channel_id=1, source_target_pairs={{0,1},{1,0},{2,3},{3,2},{4,5},{5,4},{6,7},{7,6},{8,9},{9,8},{10,11... | collective-permute-start | bytes 3932168 | tf_op jit(solution)/shard_map/gather_weights/ppermute | solution.py:277
  236.8 11.1 %collective-permute-start.18 = (bf16[32,4096]{1,0:T(8,128)(2,1)}, bf16[32,4096]{1,0:T(8,128)(2,1)S(1)}, u32[]{:S(2)}, u32[]{:S(2)}) collective-permute-start(bf16[32,4096]{1,0:T(8,128)(2,1)} %first_forward.1), channel_id=1, source_target_pairs={{0,258},{2,256},{256,2},{258,0},{1,259},{3,257},{257,3},{259,1},{4... | collective-permute-start | bytes 786440 | tf_op jit(solution)/shard_map/ppermute | solution.py:285
  279.4 10.2 %collective-permute-start.19 = (bf16[32,4096]{1,0:T(8,128)(2,1)}, bf16[32,4096]{1,0:T(8,128)(2,1)S(1)}, u32[]{:S(2)}, u32[]{:S(2)}) collective-permute-start(bf16[32,4096]{1,0:T(8,128)(2,1)} %get-tuple-element.30), channel_id=1, source_target_pairs={{0,258},{2,256},{256,2},{258,0},{1,259},{3,257},{257,3},{259,1},{4... | collective-permute-start | bytes 786440 | tf_op jit(solution)/shard_map/ppermute | solution.py:285
  308.8 13.9 %all-to-all-start.1 = ((bf16[16,32,256]{2,1,0:T(8,128)(2,1)}), bf16[16,32,256]{2,1,0:T(8,128)(2,1)S(1)}, u32[]{:S(2)}, u32[]{:S(2)}) async-start(bf16[16,32,256]{2,1,0:T(8,128)(2,1)} %bitcast.23), calls=%async_computation.1 | async-start | bytes 524288 | tf_op jit(solution)/shard_map/gather_grads/all_to_all | solution.py:379
  (10 other events, 407.7 us)
Sparse Core Ops, SparseCore 0:
  17.5 88.6 all-gather.4
  108.4 97.6 all-gather.6

commit v5 on v4

--- a/solution.py
+++ b/solution.py
@@ -27,8 +27,10 @@
 KVW = QW + 2 * HEAD
 COLS = KVW + QW
 CHUNK = 1024
-UPPER = 32
-SOURCES = 14
+UPPER = 48
+EARLY = 8
+REST_AT = {1: 0, 3: 64 - UPPER, 2: 2 * (64 - UPPER)}
+SOURCES = 10
 SCALE = 1.0 / math.sqrt(HEAD)
 VMEM_LIMIT = 60 * 1024 * 1024
 F32 = jnp.float32
@@ -47,37 +49,42 @@
     return lax.dot_general(a, b, (((0,), (0,)), ((), ())), preferred_element_type=F32)
 
 
-def start_copies(at, layer, distance, core, sources, w_vmem, sems):
+def start_copies(layer, distance, place, sources, w_vmem, sems):
     whole, rest, *moved = sources
-
-    def start(source, target):
-        pltpu.make_async_copy(source, target, sems.at[layer, at]).start()
-
-    c, yl = at // 2, at % 2
-    target = w_vmem.at[layer, at]
-    if distance == 0:
-        start(whole.at[:, c, yl], target)
-        return
-    start(rest.at[:, c, distance - 1, yl], target.at[:, UPPER:])
-    upper = target.at[:, :UPPER]
-    for own in range(2):
-
-        @pl.when((core == c) == (own == 0))
-        def _(own=own):
-            for half in range(2):
-                block = moved[(distance - 1) * 4 + half * 2 + own]
-                start(block.at[:, yl], upper.at[half * 8 : half * 8 + 8])
+    core, side = place[1], place[3]
+    for c in range(2):
+        for other in range(2):
+            at = c * 2 + (side if other == 0 else 1 - side)
+
+            def start(source, first, last, low=0, high=16, at=at):
+                target = w_vmem.at[layer, at, low:high, first:last]
+                pltpu.make_async_copy(source, target, sems.at[layer, at]).start()
+
+            if distance == 0:
+                start(whole.at[:, c, other], 0, 64)
+                continue
+            begin = REST_AT[distance]
+            first = 0 if distance == 2 else UPPER
+            start(rest.at[:, c, other, begin : begin + 64 - first], first, 64)
+            if distance == 2:
+                continue
+            for own in range(2):
+
+                @pl.when((core == c) == (own == 0))
+                def _(own=own, other=other, start=start):
+                    early, late = moved[(distance // 2) * 4 + own], moved[(distance // 2) * 4 + 2 + own]
+                    start(early.at[:, other], 0, UPPER, 0, EARLY)
+                    start(late.at[:, other], 0, UPPER, EARLY, 16)
 
 
 def start_layers(order, place, sources, w_vmem, sems):
-    x, core = place[0], place[1]
+    x = place[0]
     for layer in order:
         for distance in range(4):
 
             @pl.when(((x - layer + 4) & 3) == distance)
             def _(layer=layer, distance=distance):
-                for at in range(WIDTH // CHUNK):
-                    start_copies(at, layer, distance, core, sources, w_vmem, sems)
+                start_copies(layer, distance, place, sources, w_vmem, sems)
 
 
 def wait_rows(w_vmem, sems, layer, at):
@@ -285,23 +292,18 @@
     return lax.ppermute(block, ("yh", "yl"), [(i, 3 - i) for i in range(4)])
 
 
-def pair_rows(own, yl):
-    other = swap(own, "yl")
-    return jnp.stack([jnp.where(yl == 0, own, other), jnp.where(yl == 0, other, own)])
-
-
-def gather_layers(pair, lower, c):
+def gather_layers(pair, rest, c):
     whole = lax.all_gather(pair, ("z", "c"), axis=0).reshape(16, 2, 2, 64, COLS)
-    lower = jnp.stack([turned(lower, distance) for distance in range(1, 4)])
-    rest = lax.all_gather(lower, ("z", "c"), axis=0).reshape(16, 2, 3, 2, 64 - UPPER, COLS)
+    rest = [turned(rest[:, UPPER:], 1), turned(rest[:, UPPER:], 3), turned(rest, 2)]
+    rest = jnp.concatenate(rest, axis=1)
+    rest = lax.all_gather(rest, ("z", "c"), axis=0).reshape(16, 2, 2, -1, COLS)
     share = lax.dynamic_slice(whole, (0, c, 0, 0, 0), (16, 1, 2, UPPER, COLS))[:, 0]
-    low, high = share[:8], share[8:]
-    near_low, far_high = turned(low, 1), turned(high, 3)
-    near_low, far_high, low, high = lax.optimization_barrier((near_low, far_high, low, high))
-    twice_low, twice_high = turned(near_low, 1), turned(far_high, 3)
-    near_high, far_low = turned(high, 1), turned(low, 3)
+    early, late = share[:EARLY], share[EARLY:]
+    near, far = turned(early, 1), turned(early, 3)
+    near, far, late = lax.optimization_barrier((near, far, late))
+    near_late, far_late = turned(late, 1), turned(late, 3)
     moved = []
-    for block in (near_low, near_high, twice_low, twice_high, far_low, far_high):
+    for block in (near, near_late, far, far_late):
         moved += [block, swap(block, "c")]
     return [whole, rest] + moved
 
@@ -330,14 +332,12 @@
     up_in = swap(up_in, "yl")
     segment = jnp.where(yh == 1, swap(segment, "yl"), segment)
     seg_col, seg_row = segment[:, None], segment[None, :]
-    place = jnp.stack([x, c, yh]).astype(jnp.int32)
+    place = jnp.stack([x, c, yh, yl]).astype(jnp.int32)
     with jax.named_scope("gather_weights"):
-        pair = pair_rows(own, yl)
-        tied = lax.optimization_barrier(
-            (pair[:, UPPER:], place, rows_in, up_in, seg_col, seg_row)
-        )
-        lower, place, rows_in, up_in, seg_col, seg_row = tied
-        sources = gather_layers(pair, lower, c)
+        pair = jnp.stack([own, swap(own, "yl")])
+        tied = lax.optimization_barrier((pair, place, rows_in, up_in, seg_col, seg_row))
+        rest, place, rows_in, up_in, seg_col, seg_row = tied
+        sources = gather_layers(pair, rest, c)
 
     (arrived,) = call(
         first_kernel,
@@ -374,6 +374,7 @@
     )
 
     with jax.named_scope("gather_grads"):
+        grads, rows = lax.optimization_barrier((grads, rows))
         cols = jnp.broadcast_to(grads[:, None], (LAYERS, 4, LENGTH, 2 * HEAD))
         cols = cols.reshape(4 * LAYERS, LENGTH, 2 * HEAD)
         cols = lax.all_to_all(cols, PLANE, 0, 0, tiled=True).reshape(-1, 2 * HEAD)

time: 422 us -> 407 us (0.964)
  starting transfers between devices: 76.3 us -> 59.3 us
  waiting for transfers between devices: 156 us -> 162 us
  blocking collectives: 87.8 us -> 82.1 us
    ppermute x9 -> x7, waiting for transfers between devices: 70.2 us -> 86.1 us  [turned(): return lax.ppermute(block, 'x', [(i, (i + distance) % 4) for i in range(4)])]
    ppermute x9 -> x7, starting transfers between devices: 30.2 us -> 22.4 us  [swap(): return lax.ppermute(block, axis, [(0, 1), (1, 0)])]
    ppermute x9 -> x7, starting transfers between devices: 30.5 us -> 22.7 us  [turned(): return lax.ppermute(block, 'x', [(i, (i + distance) % 4) for i in range(4)])]
    all_to_all x1, waiting for transfers between devices: 6.26 us -> 0.01 us  [shards(): rows = lax.all_to_all(rows, PLANE, 0, 0, tiled=True).reshape(-1, CHUNK)]
    all_to_all x1, blocking collectives: 18.1 us -> 12.4 us  [shards(): cols = lax.all_to_all(cols, PLANE, 0, 0, tiled=True).reshape(-1, 2 * HEAD)]
  transfers between devices with their start and end apart: 23 -> 19, of which waited for: 13 -> 12; matrix products, arithmetic and copies ran while one was open for 2% -> 3% of each run, Pallas kernels for 0% -> 4%
where the time goes in v5:
time: 407 us; the launch traced here: 406 us
  waiting for transfers between devices  162 us (40%)
  blocking collectives  82.1 us (20%)
  Pallas kernels  65.7 us (16%)
  starting transfers between devices  59.3 us (15%)
  between operations  15.1 us (4%)
  local copies, waits for them, and re-layouts  14.4 us (4%)
  other arithmetic  6.65 us (2%)
    ppermute x7, waiting for transfers between devices, turned(): return lax.ppermute(block, 'x', [(i, (i + distance) % 4) for i in range(4)])  86.1 us
    pallas_call x3, Pallas kernels, call(): pl.pallas_call(kernel, out_shape=out_shape, in_specs=[SM] + [VM] * (len(i...  65.7 us
    all_gather x1, waiting for transfers between devices, gather_layers(): whole = lax.all_gather(pair, ('z', 'c'), axis=0).reshape(16, 2, 2, 64, COLS)  56.2 us
    all_to_all x2, blocking collectives, sum_over(): return jnp.sum(lax.all_to_all(spread, axes, 0, 0, tiled=True), axis=0)  40.2 us
    all_to_all x1, blocking collectives, shards(): parts = lax.all_to_all(partial, 'z', 0, 0, tiled=True)  29.6 us
    ppermute x7, starting transfers between devices, turned(): return lax.ppermute(block, 'x', [(i, (i + distance) % 4) for i in range(4)])  22.7 us
    ppermute x7, starting transfers between devices, swap(): return lax.ppermute(block, axis, [(0, 1), (1, 0)])  22.4 us
    ppermute x2, waiting for transfers between devices, across(): return lax.ppermute(block, ('yh', 'yl'), [(i, 3 - i) for i in range(4)])  12.7 us
  transfers between devices with their start and end apart: 19, of which 12 were waited for; matrix products, arithmetic and copies ran while one was open for 3% of the time, Pallas kernels for 4%

profile of v5, /device:TPU:1, one launch (start us, length us, event | category | flops | bytes accessed | tf_op | source)
XLA Modules:
  0.0 406.1 jit_solution(12700101039928917728)
XLA Ops:
  9.0 4.0 collective-permute-start
  17.2 3.4 collective-permute-start.2
  29.9 6.3 %collective-permute-start.5 = (bf16[2,64,1280]{2,1,0:T(8,128)(2,1)S(1)}, bf16[2,64,1280]{2,1,0:T(8,128)(2,1)S(1)}, u32[]{:S(2)}, u32[]{:S(2)}) collective-permute-start(bf16[2,64,1280]{2,1,0:T(8,128)(2,1)S(1)} %copy-done.1), channel_id=1, source_target_pairs={{0,128},{64,192},{128,0},{192,64},{1,129},{65,193},{129,1},{193,65... | collective-permute-start | bytes 983048 | tf_op jit(solution)/shard_map/gather_weights/ppermute | solution.py:288
  43.3 5.3 %collective-permute-done.3 = bf16[2,16,1280]{2,1,0:T(8,128)(2,1)S(1)} collective-permute-done((bf16[2,16,1280]{2,1,0:T(8,128)(2,1)S(1)}, bf16[2,16,1280]{2,1,0:T(8,128)(2,1)S(1)}, u32[]{:S(2)}, u32[]{:S(2)}) %collective-permute-start.3) | collective-permute-done | bytes 81952 | tf_op jit(solution)/shard_map/gather_weights/ppermute | solution.py:288
  49.5 56.2 %all-gather.5.cloned.1.call-done = bf16[64,64,1280]{2,1,0:T(8,128)(2,1)} async-done(((bf16[2,64,1280]{2,1,0:T(8,128)(2,1)}), bf16[64,64,1280]{2,1,0:T(8,128)(2,1)}) %all-gather.5.cloned.1.call-update) | async-done | bytes 10485776 | tf_op jit(solution)/shard_map/gather_weights/all_gather | solution.py:296
  108.1 4.0 collective-permute-start.7
  114.0 40.2 %collective-permute-done.7.refs_6_ = bf16[8,2,48,1280]{3,2,1,0:T(8,128)(2,1)S(1)} collective-permute-done((bf16[8,2,48,1280]{3,2,1,0:T(8,128)(2,1)S(1)}, bf16[8,2,48,1280]{3,2,1,0:T(8,128)(2,1)S(1)}, u32[]{:S(2)}, u32[]{:S(2)}) %collective-permute-start.7) | collective-permute-done | bytes 1966112 | tf_op jit(solution)/shard_map/gather_weights/ppermute | solution.py:288
  154.2 4.9 %collective-permute-done.6.refs_2_ = bf16[8,2,48,1280]{3,2,1,0:T(8,128)(2,1)} collective-permute-done((bf16[8,2,48,1280]{3,2,1,0:T(8,128)(2,1)S(1)}, bf16[8,2,48,1280]{3,2,1,0:T(8,128)(2,1)}, u32[]{:S(2)}, u32[]{:S(2)}) %collective-permute-start.6) | collective-permute-done | bytes 1966112 | tf_op jit(solution)/shard_map/gather_weights/ppermute | solution.py:288
  161.0 3.4 collective-permute-start.9
  164.4 3.9 collective-permute-start.8
  170.2 33.8 %collective-permute-done.12.refs_8_ = bf16[8,2,48,1280]{3,2,1,0:T(8,128)(2,1)} collective-permute-done((bf16[8,2,48,1280]{3,2,1,0:T(8,128)(2,1)S(1)}, bf16[8,2,48,1280]{3,2,1,0:T(8,128)(2,1)}, u32[]{:S(2)}, u32[]{:S(2)}) %collective-permute-start.12) | collective-permute-done | bytes 1966112 | tf_op jit(solution)/shard_map/gather_weights/ppermute | solution.py:288
  204.0 4.2 %collective-permute-start.13 = (bf16[8,2,48,1280]{3,2,1,0:T(8,128)(2,1)}, bf16[8,2,48,1280]{3,2,1,0:T(8,128)(2,1)}, u32[]{:S(2)}, u32[]{:S(2)}) collective-permute-start(bf16[8,2,48,1280]{3,2,1,0:T(8,128)(2,1)} %collective-permute-done.12.refs_8_), channel_id=1, source_target_pairs={{0,1},{1,0},{2,3},{3,2},{4,5},{5,4},{6,7},{7,6},{8,9},{9,8},{10,11... | collective-permute-start | bytes 5898248 | tf_op jit(solution)/shard_map/gather_weights/ppermute | solution.py:284
  215.3 18.0 %first_forward.1 = bf16[32,4096]{1,0:T(8,128)(2,1)} custom-call(s32[4]{0:T(128)} %pad_add_fusion.place, bf16[32,4096]{1,0:T(8,128)(2,1)} %reshape.107.h_ref, s32[32,1]{1,0:T(8,128)} %copy.30.seg_col, s32[1,32]{1,0:T(1,128)} %get-tuple-element.24.seg_row, bf16[16,2,2,64,1280]{4,3,2,1,0:T(8,128)(2,1)} %bitcast.60, bf16[16,2,2,96,1280]{4,3,2,1,0:T(8,128)(2,1)} %bitcast.56, ...), custom_call_target="tpu_custom_call" | custom-call | flops 1342177280 | bytes 41943040 | tf_op jit(solution)/shard_map/first_forward/pallas_call | solution.py:266
  233.4 4.5 %collective-permute-start.14 = (bf16[32,4096]{1,0:T(8,128)(2,1)}, bf16[32,4096]{1,0:T(8,128)(2,1)S(1)}, u32[]{:S(2)}, u32[]{:S(2)}) collective-permute-start(bf16[32,4096]{1,0:T(8,128)(2,1)} %first_forward.1), channel_id=1, source_target_pairs={{0,258},{2,256},{256,2},{258,0},{1,259},{3,257},{257,3},{259,1},{4... | collective-permute-start | bytes 786440 | tf_op jit(solution)/shard_map/ppermute | solution.py:292
  237.9 6.3 %collective-permute-done.14.arrived = bf16[32,4096]{1,0:T(8,128)(2,1)S(1)} collective-permute-done((bf16[32,4096]{1,0:T(8,128)(2,1)}, bf16[32,4096]{1,0:T(8,128)(2,1)S(1)}, u32[]{:S(2)}, u32[]{:S(2)}) %collective-permute-start.14) | collective-permute-done | bytes 262176 | tf_op jit(solution)/shard_map/ppermute | solution.py:292
  244.9 30.8 %second_forward_backward.1 = (bf16[32,4096]{1,0:T(8,128)(2,1)}, bf16[4,32,4096]{2,1,0:T(8,128)(2,1)}, bf16[4,32,4096]{2,1,0:T(8,128)(2,1)}, bf16[4,128,128]{2,1,...) custom-call(s32[4]{0:T(128)} %pad_add_fusion.place, ...), custom_call_target="tpu_custom_call" | custom-call | flops 2684354560 | bytes 41943040 | tf_op jit(solution)/shard_map/second_forward_backward/pallas_call | solution.py:266
  278.9 4.6 %all-to-all-start = ((bf16[16,32,1024]{2,1,0:T(8,128)(2,1)}), bf16[16,32,1024]{2,1,0:T(8,128)(2,1)S(1)}, u32[]{:S(2)}, u32[]{:S(2)}) async-start(bf16[16,32,1024]{2,1,0:T(8,128)(2,1)} %bitcast.20), calls=%async_computation | async-start | bytes 2097152 | tf_op jit(solution)/shard_map/normed_slices/all_to_all | solution.py:364
  283.6 4.9 %collective-permute-start.15 = (bf16[32,4096]{1,0:T(8,128)(2,1)S(1)}, bf16[32,4096]{1,0:T(8,128)(2,1)S(1)}, u32[]{:S(2)}, u32[]{:S(2)}) collective-permute-start(bf16[32,4096]{1,0:T(8,128)(2,1)S(1)} %copy-done.8), channel_id=1, source_target_pairs={{0,258},{2,256},{256,2},{258,0},{1,259},{3,257},{257,3},{259,1},{4... | collective-permute-start | bytes 786440 | tf_op jit(solution)/shard_map/ppermute | solution.py:292
  288.5 6.4 %collective-permute-done.15.arrived = bf16[32,4096]{1,0:T(8,128)(2,1)S(1)} collective-permute-done((bf16[32,4096]{1,0:T(8,128)(2,1)S(1)}, bf16[32,4096]{1,0:T(8,128)(2,1)S(1)}, u32[]{:S(2)}, u32[]{:S(2)}) %collective-permute-start.15) | collective-permute-done | bytes 262176 | tf_op jit(solution)/shard_map/ppermute | solution.py:292
  295.6 16.9 %first_backward.1 = bf16[4,32,256]{2,1,0:T(8,128)(2,1)} custom-call(s32[4]{0:T(128)} %pad_add_fusion.place, bf16[32,4096]{1,0:T(8,128)(2,1)} %copy-done.2, bf16[32,4096]{1,0:T(8,128)(2,1)} %copy-done.3, bf16[4,32,4096]{2,1,0:T(8,128)(2,1)} %get-tuple-element.30.h_all, bf16[4,128,128]{2,1,0:T(8,128)(2,1)} %get-tuple-element.31.q_all, ...), custom_call_target="tpu_custom_call" | custom-call | flops 1342177280 | bytes 41943040 | tf_op jit(solution)/shard_map/first_backward/pallas_call | solution.py:266
  313.3 12.4 %all_to_all.25 = bf16[16,32,256]{2,1,0:T(8,128)(2,1)S(1)} all-to-all(bf16[16,32,256]{2,1,0:T(8,128)(2,1)S(1)} %bitcast.65), channel_id=1, replica_groups=mesh['yh'=2,'x'=4,'z'=16,'yl'=2,'c'=2] {'x','yl','c'}, dimensions={0} | all-to-all | bytes 524288 | tf_op jit(solution)/shard_map/gather_grads/all_to_all | solution.py:380
  326.2 29.6 %all_to_all.26 = bf16[16,64,256]{2,1,0:T(8,128)(2,1)S(1)} all-to-all(bf16[16,64,256]{2,1,0:T(8,128)(2,1)S(1)} %bitcast.67), channel_id=1, replica_groups=mesh['yh'=2,'x'=4,'z'=16,'yl'=2,'c'=2] {'z'}, dimensions={0} | all-to-all | bytes 1048576 | tf_op jit(solution)/shard_map/sum_grads/all_to_all | solution.py:384
  357.1 24.2 %all_to_all.27 = f32[16,8,128]{2,1,0:T(8,128)S(1)} all-to-all(f32[16,8,128]{2,1,0:T(8,128)S(1)} %broadcast_in_dim.23), channel_id=1, replica_groups=mesh['yh'=2,'x'=4,'z'=16,'yl'=2,'c'=2] {'z'}, dimensions={0} | all-to-all | bytes 131072 | tf_op jit(solution)/shard_map/clip/all_to_all | solution.py:313
  381.4 16.0 %all_to_all.28 = f32[32,8,128]{2,1,0:T(8,128)S(1)} all-to-all(f32[32,8,128]{2,1,0:T(8,128)S(1)} %broadcast_in_dim.24), channel_id=1, replica_groups=mesh['yh'=2,'x'=4,'z'=16,'yl'=2,'c'=2] {'yh','x','yl','c'}, dimensions={0} | all-to-all | bytes 262144 | tf_op jit(solution)/shard_map/clip/all_to_all | solution.py:313
  (72 shorter events, 47.0 us)
Async XLA Ops:
  7.2 98.5 %all-gather.5.cloned.1.call-start = ((), (), s32[]{:S(2)}) async-start(), calls=%async_computation.5 | async-start | bytes 10813440 | tf_op jit(solution)/shard_map/gather_weights/all_gather | solution.py:296
  9.0 6.7 %collective-permute-start = (bf16[64,1280]{1,0:T(8,128)(2,1)S(1)}, bf16[64,1280]{1,0:T(8,128)(2,1)S(1)}, u32[]{:S(2)}, u32[]{:S(2)}) collective-permute-start(bf16[64,1280]{1,0:T(8,128)(2,1)S(1)} %get-tuple-element.43), channel_id=1, source_target_pairs={{0,2},{2,0},{1,3},{3,1},{4,6},{6,4},{5,7},{7,5},{8,10},{10,8},{9,1... | collective-permute-start | bytes 491528 | tf_op jit(solution)/shard_map/gather_weights/ppermute | solution.py:284
  16.5 198.8 %all-gather.7.cloned.1.call-start = ((), (), s32[]{:S(2)}) async-start(), calls=%async_computation.6 | async-start | bytes 16220160 | tf_op jit(solution)/shard_map/gather_weights/all_gather | solution.py:299
  17.2 9.9 %collective-permute-start.2 = (s32[32]{0:T(128)S(1)}, s32[32]{0:T(128)S(1)}, u32[]{:S(2)}, u32[]{:S(2)}) collective-permute-start(s32[32]{0:T(128)S(1)} %fusion.5), channel_id=1, source_target_pairs={{0,2},{2,0},{1,3},{3,1},{4,6},{6,4},{5,7},{7,5},{8,10},{10,8},{9,1... | collective-permute-start | bytes 392 | tf_op jit(solution)/shard_map/ppermute | solution.py:284
  22.8 7.1 %collective-permute-start.1 = (bf16[32,4096]{1,0:T(8,128)(2,1)S(1)}, bf16[32,4096]{1,0:T(8,128)(2,1)S(1)}, u32[]{:S(2)}, u32[]{:S(2)}) collective-permute-start(bf16[32,4096]{1,0:T(8,128)(2,1)S(1)} %reshape.109), channel_id=1, source_target_pairs={{0,2},{2,0},{1,3},{3,1},{4,6},{6,4},{5,7},{7,5},{8,10},{10,8},{9,1... | collective-permute-start | bytes 786440 | tf_op jit(solution)/shard_map/ppermute | solution.py:284
  29.9 78.2 %copy-start.2 = (bf16[32,4096]{1,0:T(8,128)(2,1)}, bf16[32,4096]{1,0:T(8,128)(2,1)S(1)}, u32[]{:S(2)}) copy-start(bf16[32,4096]{1,0:T(8,128)(2,1)S(1)} %collective-permute-done.1.up_ref) | copy-start | bytes 786436
  29.9 18.8 %collective-permute-start.5 = (bf16[2,64,1280]{2,1,0:T(8,128)(2,1)S(1)}, bf16[2,64,1280]{2,1,0:T(8,128)(2,1)S(1)}, u32[]{:S(2)}, u32[]{:S(2)}) collective-permute-start(bf16[2,64,1280]{2,1,0:T(8,128)(2,1)S(1)} %copy-done.1), channel_id=1, source_target_pairs={{0,128},{64,192},{128,0},{192,64},{1,129},{65,193},{129,1},{193,65... | collective-permute-start | bytes 983048 | tf_op jit(solution)/shard_map/gather_weights/ppermute | solution.py:288
  36.2 7.1 %collective-permute-start.4 = (bf16[2,16,1280]{2,1,0:T(8,128)(2,1)S(1)}, bf16[2,16,1280]{2,1,0:T(8,128)(2,1)S(1)}, u32[]{:S(2)}, u32[]{:S(2)}) collective-permute-start(bf16[2,16,1280]{2,1,0:T(8,128)(2,1)S(1)} %slice.35), channel_id=1, source_target_pairs={{0,192},{64,0},{128,64},{192,128},{1,193},{65,1},{129,65},{193,129... | collective-permute-start | bytes 245768 | tf_op jit(solution)/shard_map/gather_weights/ppermute | solution.py:288
  39.0 9.7 %collective-permute-start.3 = (bf16[2,16,1280]{2,1,0:T(8,128)(2,1)S(1)}, bf16[2,16,1280]{2,1,0:T(8,128)(2,1)S(1)}, u32[]{:S(2)}, u32[]{:S(2)}) collective-permute-start(bf16[2,16,1280]{2,1,0:T(8,128)(2,1)S(1)} %slice.35), channel_id=1, source_target_pairs={{0,64},{64,128},{128,192},{192,0},{1,65},{65,129},{129,193},{193,1... | collective-permute-start | bytes 245768 | tf_op jit(solution)/shard_map/gather_weights/ppermute | solution.py:288
  108.1 46.2 %collective-permute-start.7 = (bf16[8,2,48,1280]{3,2,1,0:T(8,128)(2,1)S(1)}, bf16[8,2,48,1280]{3,2,1,0:T(8,128)(2,1)S(1)}, u32[]{:S(2)}, u32[]{:S(2)}) collective-permute-start(bf16[8,2,48,1280]{3,2,1,0:T(8,128)(2,1)S(1)} %get-tuple-element.41), channel_id=1, source_target_pairs={{0,192},{64,0},{128,64},{192,128},{1,193},{65,1},{129,65},{193,129... | collective-permute-start | bytes 5898248 | tf_op jit(solution)/shard_map/gather_weights/ppermute | solution.py:288
  112.1 47.1 %collective-permute-start.6 = (bf16[8,2,48,1280]{3,2,1,0:T(8,128)(2,1)S(1)}, bf16[8,2,48,1280]{3,2,1,0:T(8,128)(2,1)}, u32[]{:S(2)}, u32[]{:S(2)}) collective-permute-start(bf16[8,2,48,1280]{3,2,1,0:T(8,128)(2,1)S(1)} %get-tuple-element.41), channel_id=1, source_target_pairs={{0,64},{64,128},{128,192},{192,0},{1,65},{65,129},{129,193},{193,1... | collective-permute-start | bytes 5898248 | tf_op jit(solution)/shard_map/gather_weights/ppermute | solution.py:288
  154.2 61.1 %copy-start = (bf16[8,2,48,1280]{3,2,1,0:T(8,128)(2,1)}, bf16[8,2,48,1280]{3,2,1,0:T(8,128)(2,1)S(1)}, u32[]{:S(2)}) copy-start(bf16[8,2,48,1280]{3,2,1,0:T(8,128)(2,1)S(1)} %collective-permute-done.7.refs_6_) | copy-start | bytes 5898244
  159.1 44.9 %collective-permute-start.12 = (bf16[8,2,48,1280]{3,2,1,0:T(8,128)(2,1)S(1)}, bf16[8,2,48,1280]{3,2,1,0:T(8,128)(2,1)}, u32[]{:S(2)}, u32[]{:S(2)}) collective-permute-start(bf16[8,2,48,1280]{3,2,1,0:T(8,128)(2,1)S(1)} %get-tuple-element.27), channel_id=1, source_target_pairs={{0,192},{64,0},{128,64},{192,128},{1,193},{65,1},{129,65},{193,129... | collective-permute-start | bytes 5898248 | tf_op jit(solution)/shard_map/gather_weights/ppermute | solution.py:288
  161.0 47.2 %collective-permute-start.9 = (bf16[8,2,48,1280]{3,2,1,0:T(8,128)(2,1)S(1)}, bf16[8,2,48,1280]{3,2,1,0:T(8,128)(2,1)}, u32[]{:S(2)}, u32[]{:S(2)}) collective-permute-start(bf16[8,2,48,1280]{3,2,1,0:T(8,128)(2,1)S(1)} %get-tuple-element.27), channel_id=1, source_target_pairs={{0,64},{64,128},{128,192},{192,0},{1,65},{65,129},{129,193},{193,1... | collective-permute-start | bytes 5898248 | tf_op jit(solution)/shard_map/gather_weights/ppermute | solution.py:288
  164.4 47.7 %collective-permute-start.8 = (bf16[8,2,48,1280]{3,2,1,0:T(8,128)(2,1)}, bf16[8,2,48,1280]{3,2,1,0:T(8,128)(2,1)}, u32[]{:S(2)}, u32[]{:S(2)}) collective-permute-start(bf16[8,2,48,1280]{3,2,1,0:T(8,128)(2,1)} %collective-permute-done.6.refs_2_), channel_id=1, source_target_pairs={{0,1},{1,0},{2,3},{3,2},{4,5},{5,4},{6,7},{7,6},{8,9},{9,8},{10,11... | collective-permute-start | bytes 5898248 | tf_op jit(solution)/shard_map/gather_weights/ppermute | solution.py:284
  168.3 43.8 %collective-permute-start.11 = (bf16[8,2,48,1280]{3,2,1,0:T(8,128)(2,1)S(1)}, bf16[8,2,48,1280]{3,2,1,0:T(8,128)(2,1)}, u32[]{:S(2)}, u32[]{:S(2)}) collective-permute-start(bf16[8,2,48,1280]{3,2,1,0:T(8,128)(2,1)S(1)} %collective-permute-done.7.refs_6_), channel_id=1, source_target_pairs={{0,1},{1,0},{2,3},{3,2},{4,5},{5,4},{6,7},{7,6},{8,9},{9,8},{10,11... | collective-permute-start | bytes 5898248 | tf_op jit(solution)/shard_map/gather_weights/ppermute | solution.py:284
  204.0 8.1 %collective-permute-start.13 = (bf16[8,2,48,1280]{3,2,1,0:T(8,128)(2,1)}, bf16[8,2,48,1280]{3,2,1,0:T(8,128)(2,1)}, u32[]{:S(2)}, u32[]{:S(2)}) collective-permute-start(bf16[8,2,48,1280]{3,2,1,0:T(8,128)(2,1)} %collective-permute-done.12.refs_8_), channel_id=1, source_target_pairs={{0,1},{1,0},{2,3},{3,2},{4,5},{5,4},{6,7},{7,6},{8,9},{9,8},{10,11... | collective-permute-start | bytes 5898248 | tf_op jit(solution)/shard_map/gather_weights/ppermute | solution.py:284
  208.3 7.0 %collective-permute-start.10 = (bf16[8,2,48,1280]{3,2,1,0:T(8,128)(2,1)}, bf16[8,2,48,1280]{3,2,1,0:T(8,128)(2,1)}, u32[]{:S(2)}, u32[]{:S(2)}) collective-permute-start(bf16[8,2,48,1280]{3,2,1,0:T(8,128)(2,1)} %collective-permute-done.9.refs_4_), channel_id=1, source_target_pairs={{0,1},{1,0},{2,3},{3,2},{4,5},{5,4},{6,7},{7,6},{8,9},{9,8},{10,11... | collective-permute-start | bytes 5898248 | tf_op jit(solution)/shard_map/gather_weights/ppermute | solution.py:284
  233.4 10.8 %collective-permute-start.14 = (bf16[32,4096]{1,0:T(8,128)(2,1)}, bf16[32,4096]{1,0:T(8,128)(2,1)S(1)}, u32[]{:S(2)}, u32[]{:S(2)}) collective-permute-start(bf16[32,4096]{1,0:T(8,128)(2,1)} %first_forward.1), channel_id=1, source_target_pairs={{0,258},{2,256},{256,2},{258,0},{1,259},{3,257},{257,3},{259,1},{4... | collective-permute-start | bytes 786440 | tf_op jit(solution)/shard_map/ppermute | solution.py:292
  278.9 33.5 %all-to-all-start = ((bf16[16,32,1024]{2,1,0:T(8,128)(2,1)}), bf16[16,32,1024]{2,1,0:T(8,128)(2,1)S(1)}, u32[]{:S(2)}, u32[]{:S(2)}) async-start(bf16[16,32,1024]{2,1,0:T(8,128)(2,1)} %bitcast.20), calls=%async_computation | async-start | bytes 2097152 | tf_op jit(solution)/shard_map/normed_slices/all_to_all | solution.py:364
  283.6 11.3 %collective-permute-start.15 = (bf16[32,4096]{1,0:T(8,128)(2,1)S(1)}, bf16[32,4096]{1,0:T(8,128)(2,1)S(1)}, u32[]{:S(2)}, u32[]{:S(2)}) collective-permute-start(bf16[32,4096]{1,0:T(8,128)(2,1)S(1)} %copy-done.8), channel_id=1, source_target_pairs={{0,258},{2,256},{256,2},{258,0},{1,259},{3,257},{257,3},{259,1},{4... | collective-permute-start | bytes 786440 | tf_op jit(solution)/shard_map/ppermute | solution.py:292
  325.7 72.9 %copy-start.5 = (f32[1,2,64,128]{3,2,1,0:T(8,128)S(1)}, f32[1,2,64,128]{3,2,1,0:T(8,128)}, u32[]{:S(2)}) copy-start(f32[1,2,64,128]{3,2,1,0:T(8,128)} %param.13) | copy-start | bytes 196612
  325.7 72.9 %copy-start.6 = (f32[1,2,64,128]{3,2,1,0:T(8,128)S(1)}, f32[1,2,64,128]{3,2,1,0:T(8,128)}, u32[]{:S(2)}) copy-start(f32[1,2,64,128]{3,2,1,0:T(8,128)} %param.15) | copy-start | bytes 196612
  325.7 72.9 %copy-start.7 = (f32[1,2,64,128]{3,2,1,0:T(8,128)S(1)}, f32[1,2,64,128]{3,2,1,0:T(8,128)}, u32[]{:S(2)}) copy-start(f32[1,2,64,128]{3,2,1,0:T(8,128)} %param.14) | copy-start | bytes 196612
  (4 other events, 15.0 us)
Sparse Core Ops, SparseCore 0:
  16.6 88.9 all-gather.4
  107.8 97.3 all-gather.6

commit v6 on v5

--- a/solution.py
+++ b/solution.py
@@ -32,7 +32,7 @@
 REST_AT = {1: 0, 3: 64 - UPPER, 2: 2 * (64 - UPPER)}
 SOURCES = 10
 SCALE = 1.0 / math.sqrt(HEAD)
-VMEM_LIMIT = 60 * 1024 * 1024
+VMEM_LIMIT = 12 * 1024 * 1024
 F32 = jnp.float32
 BF16 = jnp.bfloat16
 
@@ -49,7 +49,7 @@
     return lax.dot_general(a, b, (((0,), (0,)), ((), ())), preferred_element_type=F32)
 
 
-def start_copies(layer, distance, place, sources, w_vmem, sems):
+def start_copies(layer, distance, place, sources, weights, sems):
     whole, rest, *moved = sources
     core, side = place[1], place[3]
     for c in range(2):
@@ -57,7 +57,7 @@
             at = c * 2 + (side if other == 0 else 1 - side)
 
             def start(source, first, last, low=0, high=16, at=at):
-                target = w_vmem.at[layer, at, low:high, first:last]
+                target = weights[layer].at[at, low:high, first:last]
                 pltpu.make_async_copy(source, target, sems.at[layer, at]).start()
 
             if distance == 0:
@@ -77,18 +77,18 @@
                     start(late.at[:, other], 0, UPPER, EARLY, 16)
 
 
-def start_layers(order, place, sources, w_vmem, sems):
+def start_layers(order, place, sources, weights, sems):
     x = place[0]
     for layer in order:
         for distance in range(4):
 
             @pl.when(((x - layer + 4) & 3) == distance)
             def _(layer=layer, distance=distance):
-                start_copies(layer, distance, place, sources, w_vmem, sems)
-
-
-def wait_rows(w_vmem, sems, layer, at):
-    block = w_vmem.at[layer, at // CHUNK]
+                start_copies(layer, distance, place, sources, weights, sems)
+
+
+def wait_rows(weights, sems, layer, at):
+    block = weights[layer].at[at // CHUNK]
     pltpu.make_async_copy(block, block, sems.at[layer, at // CHUNK]).wait()
 
 
@@ -100,16 +100,9 @@
     return jnp.concatenate([rows[h * LENGTH : (h + 1) * LENGTH] for h in range(HEADS)], axis=1)
 
 
-def inverse_norm(h_ref, layer):
-    total = jnp.zeros((LENGTH, 1), F32)
-    for at in range(0, WIDTH, CHUNK):
-        signal = h_ref[layer, :, at : at + CHUNK].astype(F32)
-        total = total + jnp.sum(signal * signal, axis=-1, keepdims=True)
-    return lax.rsqrt(total * (1.0 / WIDTH) + NORM_EPS)
-
-
-def weight_rows(w_vmem, layer, at, first, last):
-    return w_vmem[layer, at // CHUNK, :, :, first:last].reshape(CHUNK, last - first)
+def weight_rows(weights, layer, at, first, last):
+    block = weights[layer][at // CHUNK, :, :, first:last]
+    return block.reshape(CHUNK, last - first)
 
 
 def attention_mask(seg_col, seg_row):
@@ -119,49 +112,61 @@
     return jnp.concatenate([allowed] * HEADS, axis=0) > 0.0
 
 
-def forward_layers(mask, h_all, n_all, kept, out_ref, w_vmem, sems):
+def forward_layers(mask, h_all, kept, out_ref, weights, sems):
+    def project(layer, at, rows, acc, squares):
+        if sems is not None:
+            wait_rows(weights, sems, layer, at)
+        wide = rows.astype(F32)
+        acc = acc + dot_nn(rows, weight_rows(weights, layer, at, 0, KVW))
+        return acc, squares + jnp.sum(wide * wide, axis=-1, keepdims=True)
+
+    start = (jnp.zeros((LENGTH, KVW), F32), jnp.zeros((LENGTH, 1), F32))
+    acc, squares = start
+    for at in range(0, WIDTH, CHUNK):
+        acc, squares = project(0, at, h_all[0, :, at : at + CHUNK], acc, squares)
     for layer in range(LAYERS):
-        inverse = inverse_norm(h_all, layer)
-        for at in range(0, WIDTH, CHUNK):
-            signal = h_all[layer, :, at : at + CHUNK].astype(F32)
-            n_all[layer, :, at : at + CHUNK] = (signal * inverse).astype(BF16)
-        acc = jnp.zeros((LENGTH, KVW), F32)
-        for at in range(0, WIDTH, CHUNK):
-            wait_rows(w_vmem, sems, layer, at)
-            acc = acc + dot_nn(
-                n_all[layer, :, at : at + CHUNK], weight_rows(w_vmem, layer, at, 0, KVW)
-            )
-        rows = acc.astype(BF16)
+        inverse = lax.rsqrt(squares * (1.0 / WIDTH) + NORM_EPS)
+        rows = (acc * inverse).astype(BF16)
         query = stack_heads(rows[:, :QW])
         keys = rows[:, QW : QW + HEAD]
         values = rows[:, QW + HEAD :]
         scores = dot_nt(query, keys) * SCALE
         exp_scores = jnp.where(mask, jnp.exp(scores), 0.0)
         probs = exp_scores / jnp.sum(exp_scores, axis=-1, keepdims=True)
-        context = unstack_heads(dot_nn(probs.astype(BF16), values).astype(BF16))
         if kept is not None:
-            for ref, value in zip(kept, (query, keys, values, probs)):
+            n_all, i_all, q_all, k_all, v_all, p_all = kept
+            for ref, value in zip(kept[2:], (query, keys, values, probs)):
                 ref[layer] = value
+            i_all[layer] = jnp.broadcast_to(inverse, (LENGTH, HEAD))
+            for at in range(0, WIDTH, CHUNK):
+                signal = h_all[layer, :, at : at + CHUNK].astype(F32)
+                core, side = divmod(at // CHUNK, 2)
+                n_all[layer * 4 + side * 2 + core] = (signal * inverse).astype(BF16)
         if out_ref is None and layer + 1 == LAYERS:
             return
+        context = unstack_heads(dot_nn(probs.astype(BF16), values).astype(BF16))
+        acc, squares = start
         for at in range(0, WIDTH, CHUNK):
             signal = h_all[layer, :, at : at + CHUNK].astype(F32)
-            branch = dot_nt(context, weight_rows(w_vmem, layer, at, KVW, COLS))
+            branch = dot_nt(context, weight_rows(weights, layer, at, KVW, COLS))
             result = (signal + branch).astype(BF16)
             if layer + 1 < LAYERS:
                 h_all[layer + 1, :, at : at + CHUNK] = result
+                acc, squares = project(layer + 1, at, result, acc, squares)
             else:
                 out_ref[:, at : at + CHUNK] = result
 
 
-def backward_layers(need_up, h_all, kept, up, g_all, w_vmem, gn, sems):
-    q_all, k_all, v_all, p_all = kept
+def backward_layers(need_up, h_all, kept, up, g_all, weights):
+    i_all, q_all, k_all, v_all, p_all = kept
+
+    def project(layer, at, rows, acc):
+        return acc + dot_nn(rows, weight_rows(weights, layer, at, KVW, COLS))
+
+    acc = jnp.zeros((LENGTH, QW), F32)
+    for at in range(0, WIDTH, CHUNK):
+        acc = project(LAYERS - 1, at, up[:, at : at + CHUNK], acc)
     for layer in reversed(range(LAYERS)):
-        acc = jnp.zeros((LENGTH, QW), F32)
-        for at in range(0, WIDTH, CHUNK):
-            if sems is not None:
-                wait_rows(w_vmem, sems, layer, at)
-            acc = acc + dot_nn(up[:, at : at + CHUNK], weight_rows(w_vmem, layer, at, KVW, COLS))
         grad_context = stack_heads(acc.astype(BF16))
         query, keys, values, probs = q_all[layer], k_all[layer], v_all[layer], p_all[layer]
         grad_probs = dot_nt(grad_context, values)
@@ -170,40 +175,44 @@
         grad_keys = dot_tn(grad_scores, query).astype(BF16)
         grad_values = dot_tn(probs.astype(BF16), grad_context).astype(BF16)
         if g_all is not None:
-            g_all[layer, :, :HEAD] = grad_keys
-            g_all[layer, :, HEAD:] = grad_values
+            for copy in range(4):
+                g_all[layer * 4 + copy, :, :HEAD] = grad_keys
+                g_all[layer * 4 + copy, :, HEAD:] = grad_values
         if layer == 0 and not need_up:
             return
-        grad_query = unstack_heads(dot_nn(grad_scores, keys).astype(BF16))
-        grads = jnp.concatenate([grad_query, grad_keys, grad_values], axis=1)
-        inverse = inverse_norm(h_all, layer)
-        total = jnp.zeros((LENGTH, 1), F32)
+        grad_query = dot_nn(grad_scores, keys).astype(BF16)
+        grads = jnp.concatenate([unstack_heads(grad_query), grad_keys, grad_values], axis=1)
+        by_head = jnp.sum(grad_query.astype(F32) * query.astype(F32), axis=-1, keepdims=True)
+        total = sum(by_head[h * LENGTH : (h + 1) * LENGTH] for h in range(HEADS))
+        for grad, value in ((grad_keys, keys), (grad_values, values)):
+            product = grad.astype(F32) * value.astype(F32)
+            total = total + jnp.sum(product, axis=-1, keepdims=True)
+        inverse = i_all[layer][:, :1]
+        pull = inverse * inverse * (total * (1.0 / WIDTH))
+        acc = jnp.zeros((LENGTH, QW), F32)
         for at in range(0, WIDTH, CHUNK):
-            part = dot_nt(grads, weight_rows(w_vmem, layer, at, 0, KVW))
-            gn[:, at : at + CHUNK] = part
-            signal = h_all[layer, :, at : at + CHUNK].astype(F32)
-            total = total + jnp.sum(part * signal, axis=-1, keepdims=True)
-        pull = inverse * inverse * inverse * (total * (1.0 / WIDTH))
-        for at in range(0, WIDTH, CHUNK):
+            part = dot_nt(grads, weight_rows(weights, layer, at, 0, KVW))
             signal = h_all[layer, :, at : at + CHUNK].astype(F32)
             upstream = up[:, at : at + CHUNK].astype(F32)
-            up[:, at : at + CHUNK] = (
-                upstream + inverse * gn[:, at : at + CHUNK] - signal * pull
-            ).astype(BF16)
+            result = (upstream + inverse * part - signal * pull).astype(BF16)
+            up[:, at : at + CHUNK] = result
+            if layer > 0:
+                acc = project(layer - 1, at, result, acc)
 
 
 def first_kernel(place, h_ref, seg_col, seg_row, *refs):
     sources, refs = refs[:SOURCES], refs[SOURCES:]
-    out_ref, h_all, n_all, w_vmem, sems = refs
-    start_layers(range(LAYERS), place, sources, w_vmem, sems)
+    out_ref, *weights = refs[: LAYERS + 1]
+    h_all, sems = refs[LAYERS + 1 :]
+    start_layers(range(LAYERS), place, sources, weights, sems)
     h_all[0] = h_ref[...]
-    forward_layers(attention_mask(seg_col, seg_row), h_all, n_all, None, out_ref, w_vmem, sems)
+    mask = attention_mask(seg_col, seg_row)
+    forward_layers(mask, h_all, None, out_ref, weights, sems)
 
 
 def middle_kernel(place, h_ref, arrived, up_ref, seg_col, seg_row, *refs):
-    sources, refs = refs[:SOURCES], refs[SOURCES:]
-    out_ref, h_all, n_all, q_all, k_all, v_all, p_all, w_vmem, gn, sems = refs
-    start_layers(range(LAYERS), place, sources, w_vmem, sems)
+    weights, refs = refs[:LAYERS], refs[LAYERS:]
+    out_ref, h_all, *kept = refs
 
     @pl.when(place[2] == 1)
     def _():
@@ -214,15 +223,14 @@
         h_all[0] = h_ref[...]
 
     out_ref[...] = up_ref[...]
-    kept = (q_all, k_all, v_all, p_all)
-    forward_layers(attention_mask(seg_col, seg_row), h_all, n_all, kept, None, w_vmem, sems)
-    backward_layers(True, h_all, kept, out_ref, None, w_vmem, gn, None)
-
-
-def last_kernel(place, up_ref, arrived, h_all, q_all, k_all, v_all, p_all, *refs):
-    sources, refs = refs[:SOURCES], refs[SOURCES:]
-    g_all, up, w_vmem, gn, sems = refs
-    start_layers(reversed(range(LAYERS)), place, sources, w_vmem, sems)
+    mask = attention_mask(seg_col, seg_row)
+    forward_layers(mask, h_all, kept, None, weights, None)
+    backward_layers(True, h_all, kept[1:], out_ref, None, weights)
+
+
+def last_kernel(place, up_ref, arrived, h_all, i_all, q_all, k_all, v_all, p_all, *refs):
+    weights, refs = refs[:LAYERS], refs[LAYERS:]
+    g_all, up = refs
 
     @pl.when(place[2] == 0)
     def _():
@@ -232,21 +240,21 @@
     def _():
         up[...] = up_ref[...]
 
-    kept = (q_all, k_all, v_all, p_all)
-    backward_layers(False, h_all, kept, up, g_all, w_vmem, gn, sems)
+    kept = (i_all, q_all, k_all, v_all, p_all)
+    backward_layers(False, h_all, kept, up, g_all, weights)
 
 
 VM = pl.BlockSpec(memory_space=pltpu.VMEM)
 SM = pl.BlockSpec(memory_space=pltpu.SMEM)
 ANY = pl.BlockSpec(memory_space=pl.ANY)
-WEIGHT_SCRATCH = pltpu.VMEM((LAYERS, WIDTH // CHUNK, 16, 64, COLS), BF16)
+WEIGHTS = (pltpu.VMEM((WIDTH // CHUNK, 16, 64, COLS), BF16),) * LAYERS
 WEIGHT_SEMS = pltpu.SemaphoreType.DMA((LAYERS, WIDTH // CHUNK))
 ROWS = jax.ShapeDtypeStruct((LENGTH, WIDTH), BF16)
-ROWS_F32 = pltpu.VMEM((LENGTH, WIDTH), F32)
 ROWS_ALL = pltpu.VMEM((LAYERS, LENGTH, WIDTH), BF16)
 STATE_SHAPES = (
     jax.ShapeDtypeStruct((LAYERS, LENGTH, WIDTH), BF16),
-    jax.ShapeDtypeStruct((LAYERS, LENGTH, WIDTH), BF16),
+    jax.ShapeDtypeStruct((LAYERS * 4, LENGTH, CHUNK), BF16),
+    jax.ShapeDtypeStruct((LAYERS, LENGTH, HEAD), F32),
     jax.ShapeDtypeStruct((LAYERS, LENGTH * HEADS, HEAD), BF16),
     jax.ShapeDtypeStruct((LAYERS, LENGTH, HEAD), BF16),
     jax.ShapeDtypeStruct((LAYERS, LENGTH, HEAD), BF16),
@@ -266,7 +274,7 @@
     return pl.pallas_call(
         kernel,
         out_shape=out_shape,
-        in_specs=[SM] + [VM] * (len(inputs) - 1) + [ANY] * SOURCES,
+        in_specs=[SM] + [VM] * (len(inputs) - 1) + [ANY] * len(sources),
         out_specs=(VM,) * len(out_shape),
         scratch_shapes=scratch,
         compiler_params=pltpu.CompilerParams(vmem_limit_bytes=VMEM_LIMIT),
@@ -339,45 +347,42 @@
         rest, place, rows_in, up_in, seg_col, seg_row = tied
         sources = gather_layers(pair, rest, c)
 
-    (arrived,) = call(
+    arrived, *weights = call(
         first_kernel,
         "first_forward",
         LAYERS,
-        (ROWS,),
+        (ROWS,) + WEIGHTS,
         (place, rows_in, seg_col, seg_row),
         sources,
-        [ROWS_ALL, ROWS_ALL, WEIGHT_SCRATCH, WEIGHT_SEMS],
-    )
+        [ROWS_ALL, WEIGHT_SEMS],
+    )
+    weights = [pltpu.with_memory_space_constraint(block, pltpu.VMEM) for block in weights]
     arrived = across(arrived)
     half_up, h_all, n_all, *kept = call(
         middle_kernel,
         "second_forward_backward",
         2 * LAYERS,
         (ROWS,) + STATE_SHAPES,
-        (place, rows_in, arrived, up_in, seg_col, seg_row),
-        sources,
-        [WEIGHT_SCRATCH, ROWS_F32, WEIGHT_SEMS],
+        (place, rows_in, arrived, up_in, seg_col, seg_row, *weights),
+        (),
+        [],
     )
     with jax.named_scope("normed_slices"):
-        rows = n_all.reshape(LAYERS, LENGTH, 2, 2, CHUNK).transpose(0, 3, 2, 1, 4)
-        rows = rows.reshape(4 * LAYERS, LENGTH, CHUNK)
-        rows = lax.all_to_all(rows, PLANE, 0, 0, tiled=True).reshape(-1, CHUNK)
+        rows = lax.all_to_all(n_all, PLANE, 0, 0, tiled=True).reshape(-1, CHUNK)
     arrived = across(half_up)
     (grads,) = call(
         last_kernel,
         "first_backward",
         LAYERS,
-        (jax.ShapeDtypeStruct((LAYERS, LENGTH, 2 * HEAD), BF16),),
-        (place, up_in, arrived, h_all, *kept),
-        sources,
-        [pltpu.VMEM((LENGTH, WIDTH), BF16), WEIGHT_SCRATCH, ROWS_F32, WEIGHT_SEMS],
+        (jax.ShapeDtypeStruct((LAYERS * 4, LENGTH, 2 * HEAD), BF16),),
+        (place, up_in, arrived, h_all, *kept, *weights),
+        (),
+        [pltpu.VMEM((LENGTH, WIDTH), BF16)],
     )
 
     with jax.named_scope("gather_grads"):
         grads, rows = lax.optimization_barrier((grads, rows))
-        cols = jnp.broadcast_to(grads[:, None], (LAYERS, 4, LENGTH, 2 * HEAD))
-        cols = cols.reshape(4 * LAYERS, LENGTH, 2 * HEAD)
-        cols = lax.all_to_all(cols, PLANE, 0, 0, tiled=True).reshape(-1, 2 * HEAD)
+        cols = lax.all_to_all(grads, PLANE, 0, 0, tiled=True).reshape(-1, 2 * HEAD)
 
     with jax.named_scope("sum_grads"):
         partial = dot_tn(rows, cols).astype(BF16).reshape(16, 64, 2 * HEAD)

time: 407 us -> 407 us (level)
  Pallas kernels: 65.7 us -> 51.7 us
  local copies, waits for them, and re-layouts: 14.4 us -> 26.8 us
    unnamed x18 -> x52, local copies, waits for them, and re-layouts: 1.44 us -> 19.2 us
    pallas_call x3, Pallas kernels: 65.7 us -> 51.7 us  [call(): pl.pallas_call(kernel, out_shape=out_shape, in_specs=[SM] + [VM] * (len(i...]
  transfers between devices with their start and end apart: 19 -> 19, of which waited for: 12 -> 12; matrix products, arithmetic and copies ran while one was open for 3% -> 2% of each run, Pallas kernels for 4% -> 3%
where the time goes in v6:
time: 407 us; the launch traced here: 405 us
  waiting for transfers between devices  164 us (40%)
  blocking collectives  81.9 us (20%)
  starting transfers between devices  59.6 us (15%)
  Pallas kernels  51.7 us (13%)
  local copies, waits for them, and re-layouts  26.8 us (7%)
  between operations  15.2 us (4%)
  other arithmetic  5.55 us (1%)
    ppermute x7, waiting for transfers between devices, turned(): return lax.ppermute(block, 'x', [(i, (i + distance) % 4) for i in range(4)])  86.1 us
    all_gather x1, waiting for transfers between devices, gather_layers(): whole = lax.all_gather(pair, ('z', 'c'), axis=0).reshape(16, 2, 2, 64, COLS)  55.6 us
    pallas_call x3, Pallas kernels, call(): pl.pallas_call(kernel, out_shape=out_shape, in_specs=[SM] + [VM] * (len(i...  51.7 us
    all_to_all x2, blocking collectives, sum_over(): return jnp.sum(lax.all_to_all(spread, axes, 0, 0, tiled=True), axis=0)  39.8 us
    all_to_all x1, blocking collectives, shards(): parts = lax.all_to_all(partial, 'z', 0, 0, tiled=True)  29.5 us
    ppermute x7, starting transfers between devices, turned(): return lax.ppermute(block, 'x', [(i, (i + distance) % 4) for i in range(4)])  23.1 us
    ppermute x7, starting transfers between devices, swap(): return lax.ppermute(block, axis, [(0, 1), (1, 0)])  22.4 us
    unnamed x52, local copies, waits for them, and re-layouts  19.2 us
  transfers between devices with their start and end apart: 19, of which 12 were waited for; matrix products, arithmetic and copies ran while one was open for 2% of the time, Pallas kernels for 3%

profile of v6, /device:TPU:1, one launch (start us, length us, event | category | flops | bytes accessed | tf_op | source)
XLA Modules:
  0.0 405.4 jit_solution(16043829165514073130)
XLA Ops:
  9.0 4.0 collective-permute-start
  29.9 6.3 %collective-permute-start.5 = (bf16[2,64,1280]{2,1,0:T(8,128)(2,1)S(1)}, bf16[2,64,1280]{2,1,0:T(8,128)(2,1)S(1)}, u32[]{:S(2)}, u32[]{:S(2)}) collective-permute-start(bf16[2,64,1280]{2,1,0:T(8,128)(2,1)S(1)} %copy-done.22), channel_id=1, source_target_pairs={{0,128},{64,192},{128,0},{192,64},{1,129},{65,193},{129,1},{193,65... | collective-permute-start | bytes 983048 | tf_op jit(solution)/shard_map/gather_weights/ppermute | solution.py:296
  43.3 5.3 %collective-permute-done.3 = bf16[2,16,1280]{2,1,0:T(8,128)(2,1)S(1)} collective-permute-done((bf16[2,16,1280]{2,1,0:T(8,128)(2,1)S(1)}, bf16[2,16,1280]{2,1,0:T(8,128)(2,1)S(1)}, u32[]{:S(2)}, u32[]{:S(2)}) %collective-permute-start.3) | collective-permute-done | bytes 81952 | tf_op jit(solution)/shard_map/gather_weights/ppermute | solution.py:296
  49.5 55.6 %all-gather.5.cloned.1.call-done = bf16[64,64,1280]{2,1,0:T(8,128)(2,1)} async-done(((bf16[2,64,1280]{2,1,0:T(8,128)(2,1)}), bf16[64,64,1280]{2,1,0:T(8,128)(2,1)}) %all-gather.5.cloned.1.call-update) | async-done | bytes 10485776 | tf_op jit(solution)/shard_map/gather_weights/all_gather | solution.py:304
  107.5 4.3 %collective-permute-start.7 = (bf16[8,2,48,1280]{3,2,1,0:T(8,128)(2,1)S(1)}, bf16[8,2,48,1280]{3,2,1,0:T(8,128)(2,1)S(1)}, u32[]{:S(2)}, u32[]{:S(2)}) collective-permute-start(bf16[8,2,48,1280]{3,2,1,0:T(8,128)(2,1)S(1)} %get-tuple-element.53), channel_id=1, source_target_pairs={{0,192},{64,0},{128,64},{192,128},{1,193},{65,1},{129,65},{193,129... | collective-permute-start | bytes 5898248 | tf_op jit(solution)/shard_map/gather_weights/ppermute | solution.py:296
  113.8 40.0 %collective-permute-done.7.refs_6_ = bf16[8,2,48,1280]{3,2,1,0:T(8,128)(2,1)S(1)} collective-permute-done((bf16[8,2,48,1280]{3,2,1,0:T(8,128)(2,1)S(1)}, bf16[8,2,48,1280]{3,2,1,0:T(8,128)(2,1)S(1)}, u32[]{:S(2)}, u32[]{:S(2)}) %collective-permute-start.7) | collective-permute-done | bytes 1966112 | tf_op jit(solution)/shard_map/gather_weights/ppermute | solution.py:296
  153.8 5.1 %collective-permute-done.6.refs_2_ = bf16[8,2,48,1280]{3,2,1,0:T(8,128)(2,1)} collective-permute-done((bf16[8,2,48,1280]{3,2,1,0:T(8,128)(2,1)S(1)}, bf16[8,2,48,1280]{3,2,1,0:T(8,128)(2,1)}, u32[]{:S(2)}, u32[]{:S(2)}) %collective-permute-start.6) | collective-permute-done | bytes 1966112 | tf_op jit(solution)/shard_map/gather_weights/ppermute | solution.py:296
  170.0 33.8 %collective-permute-done.12.refs_8_ = bf16[8,2,48,1280]{3,2,1,0:T(8,128)(2,1)} collective-permute-done((bf16[8,2,48,1280]{3,2,1,0:T(8,128)(2,1)S(1)}, bf16[8,2,48,1280]{3,2,1,0:T(8,128)(2,1)}, u32[]{:S(2)}, u32[]{:S(2)}) %collective-permute-start.12) | collective-permute-done | bytes 1966112 | tf_op jit(solution)/shard_map/gather_weights/ppermute | solution.py:296
  203.8 4.2 %collective-permute-start.13 = (bf16[8,2,48,1280]{3,2,1,0:T(8,128)(2,1)}, bf16[8,2,48,1280]{3,2,1,0:T(8,128)(2,1)}, u32[]{:S(2)}, u32[]{:S(2)}) collective-permute-start(bf16[8,2,48,1280]{3,2,1,0:T(8,128)(2,1)} %collective-permute-done.12.refs_8_), channel_id=1, source_target_pairs={{0,1},{1,0},{2,3},{3,2},{4,5},{5,4},{6,7},{7,6},{8,9},{9,8},{10,11... | collective-permute-start | bytes 5898248 | tf_op jit(solution)/shard_map/gather_weights/ppermute | solution.py:292
  215.1 17.1 %first_forward.1 = (bf16[32,4096]{1,0:T(8,128)(2,1)S(1)}, bf16[4,16,64,1280]{3,2,1,0:T(8,128)(2,1)S(1)}, bf16[4,16,64,1280]{3,2,1,0:T(8,128)(2,1)S(1)}, bf16[4,1...) custom-call(s32[4]{0:T(128)S(1)} %pad_add_fusion.place, bf16[32,4096]{1,0:T(8,128)(2,1)S(1)} %reshape.97.h_ref, ...), custom_call_target="tpu_custom_call" | custom-call | flops 1342177280 | bytes 41943040 | tf_op jit(solution)/shard_map/first_forward/pallas_call | solution.py:274
  232.3 4.8 %collective-permute-start.14 = (bf16[32,4096]{1,0:T(8,128)(2,1)S(1)}, bf16[32,4096]{1,0:T(8,128)(2,1)S(1)}, u32[]{:S(2)}, u32[]{:S(2)}) collective-permute-start(bf16[32,4096]{1,0:T(8,128)(2,1)S(1)} %get-tuple-element.35), channel_id=1, source_target_pairs={{0,258},{2,256},{256,2},{258,0},{1,259},{3,257},{257,3},{259,1},{4... | collective-permute-start | bytes 786440 | tf_op jit(solution)/shard_map/ppermute | solution.py:300
  237.1 6.3 %collective-permute-done.14.arrived = bf16[32,4096]{1,0:T(8,128)(2,1)S(1)} collective-permute-done((bf16[32,4096]{1,0:T(8,128)(2,1)S(1)}, bf16[32,4096]{1,0:T(8,128)(2,1)S(1)}, u32[]{:S(2)}, u32[]{:S(2)}) %collective-permute-start.14) | collective-permute-done | bytes 262176 | tf_op jit(solution)/shard_map/ppermute | solution.py:300
  243.4 22.9 %second_forward_backward.1 = (bf16[32,4096]{1,0:T(8,128)(2,1)S(1)}, bf16[4,32,4096]{2,1,0:T(8,128)(2,1)}, bf16[16,32,1024]{2,1,0:T(8,128)(2,1)}, f32[4,32,128]{2...) custom-call(s32[4]{0:T(128)S(1)} %pad_add_fusion.place, ...), custom_call_target="tpu_custom_call" | custom-call | flops 2684354560 | bytes 41943040 | tf_op jit(solution)/shard_map/second_forward_backward/pallas_call | solution.py:274
  269.6 4.5 %all-to-all-start = ((bf16[16,32,1024]{2,1,0:T(8,128)(2,1)}), bf16[16,32,1024]{2,1,0:T(8,128)(2,1)S(1)}, u32[]{:S(2)}, u32[]{:S(2)}) async-start(bf16[16,32,1024]{2,1,0:T(8,128)(2,1)} %get-tuple-element.47), calls=%async_computation | async-start | bytes 2097152 | tf_op jit(solution)/shard_map/normed_slices/all_to_all | solution.py:371
  274.1 4.7 %collective-permute-start.15 = (bf16[32,4096]{1,0:T(8,128)(2,1)S(1)}, bf16[32,4096]{1,0:T(8,128)(2,1)S(1)}, u32[]{:S(2)}, u32[]{:S(2)}) collective-permute-start(bf16[32,4096]{1,0:T(8,128)(2,1)S(1)} %copy-done.20), channel_id=1, source_target_pairs={{0,258},{2,256},{256,2},{258,0},{1,259},{3,257},{257,3},{259,1},{4... | collective-permute-start | bytes 786440 | tf_op jit(solution)/shard_map/ppermute | solution.py:300
  278.8 6.3 %collective-permute-done.15.arrived = bf16[32,4096]{1,0:T(8,128)(2,1)S(1)} collective-permute-done((bf16[32,4096]{1,0:T(8,128)(2,1)S(1)}, bf16[32,4096]{1,0:T(8,128)(2,1)S(1)}, u32[]{:S(2)}, u32[]{:S(2)}) %collective-permute-start.15) | collective-permute-done | bytes 262176 | tf_op jit(solution)/shard_map/ppermute | solution.py:300
  289.2 4.0 copy-done.3
  293.1 4.0 copy-done.5
  297.1 4.0 copy-done.7
  301.1 11.7 %first_backward.1 = bf16[16,32,256]{2,1,0:T(8,128)(2,1)S(1)} custom-call(s32[4]{0:T(128)S(1)} %pad_add_fusion.place, bf16[32,4096]{1,0:T(8,128)(2,1)S(1)} %copy-done.10, bf16[32,4096]{1,0:T(8,128)(2,1)S(1)} %collective-permute-done.15.arrived, bf16[4,32,4096]{2,1,0:T(8,128)(2,1)} %get-tuple-element.41.h_all, f32[4,32,128]{2,1,0:T(8,128)S(1)} %copy-done.14, ...), custom_call_target="tpu_custom_call" | custom-call | flops 1342177280 | bytes 41943040 | tf_op jit(solution)/shard_map/first_backward/pallas_call | solution.py:274
  312.8 12.5 %all_to_all.25 = bf16[16,32,256]{2,1,0:T(8,128)(2,1)S(1)} all-to-all(bf16[16,32,256]{2,1,0:T(8,128)(2,1)S(1)} %first_backward.1), channel_id=1, replica_groups=mesh['yh'=2,'x'=4,'z'=16,'yl'=2,'c'=2] {'x','yl','c'}, dimensions={0} | all-to-all | bytes 524288 | tf_op jit(solution)/shard_map/gather_grads/all_to_all | solution.py:385
  325.8 29.5 %all_to_all.26 = bf16[16,64,256]{2,1,0:T(8,128)(2,1)S(1)} all-to-all(bf16[16,64,256]{2,1,0:T(8,128)(2,1)S(1)} %bitcast.58), channel_id=1, replica_groups=mesh['yh'=2,'x'=4,'z'=16,'yl'=2,'c'=2] {'z'}, dimensions={0} | all-to-all | bytes 1048576 | tf_op jit(solution)/shard_map/sum_grads/all_to_all | solution.py:389
  356.7 24.2 %all_to_all.27 = f32[16,8,128]{2,1,0:T(8,128)S(1)} all-to-all(f32[16,8,128]{2,1,0:T(8,128)S(1)} %broadcast_in_dim.16), channel_id=1, replica_groups=mesh['yh'=2,'x'=4,'z'=16,'yl'=2,'c'=2] {'z'}, dimensions={0} | all-to-all | bytes 131072 | tf_op jit(solution)/shard_map/clip/all_to_all | solution.py:321
  381.0 15.6 %all_to_all.28 = f32[32,8,128]{2,1,0:T(8,128)S(1)} all-to-all(f32[32,8,128]{2,1,0:T(8,128)S(1)} %broadcast_in_dim.17), channel_id=1, replica_groups=mesh['yh'=2,'x'=4,'z'=16,'yl'=2,'c'=2] {'yh','x','yl','c'}, dimensions={0} | all-to-all | bytes 262144 | tf_op jit(solution)/shard_map/clip/all_to_all | solution.py:321
  (103 shorter events, 59.3 us)
Async XLA Ops:
  7.2 98.0 %all-gather.5.cloned.1.call-start = ((), (), s32[]{:S(2)}) async-start(), calls=%async_computation.5 | async-start | bytes 10813440 | tf_op jit(solution)/shard_map/gather_weights/all_gather | solution.py:304
  9.0 6.7 %collective-permute-start = (bf16[64,1280]{1,0:T(8,128)(2,1)S(1)}, bf16[64,1280]{1,0:T(8,128)(2,1)S(1)}, u32[]{:S(2)}, u32[]{:S(2)}) collective-permute-start(bf16[64,1280]{1,0:T(8,128)(2,1)S(1)} %get-tuple-element.55), channel_id=1, source_target_pairs={{0,2},{2,0},{1,3},{3,1},{4,6},{6,4},{5,7},{7,5},{8,10},{10,8},{9,1... | collective-permute-start | bytes 491528 | tf_op jit(solution)/shard_map/gather_weights/ppermute | solution.py:292
  16.5 198.6 %all-gather.7.cloned.1.call-start = ((), (), s32[]{:S(2)}) async-start(), calls=%async_computation.6 | async-start | bytes 16220160 | tf_op jit(solution)/shard_map/gather_weights/all_gather | solution.py:307
  17.2 8.7 %collective-permute-start.2 = (s32[32]{0:T(128)S(1)}, s32[32]{0:T(128)S(1)}, u32[]{:S(2)}, u32[]{:S(2)}) collective-permute-start(s32[32]{0:T(128)S(1)} %fusion.5), channel_id=1, source_target_pairs={{0,2},{2,0},{1,3},{3,1},{4,6},{6,4},{5,7},{7,5},{8,10},{10,8},{9,1... | collective-permute-start | bytes 392 | tf_op jit(solution)/shard_map/ppermute | solution.py:292
  22.8 7.1 %collective-permute-start.1 = (bf16[32,4096]{1,0:T(8,128)(2,1)S(1)}, bf16[32,4096]{1,0:T(8,128)(2,1)S(1)}, u32[]{:S(2)}, u32[]{:S(2)}) collective-permute-start(bf16[32,4096]{1,0:T(8,128)(2,1)S(1)} %reshape.99), channel_id=1, source_target_pairs={{0,2},{2,0},{1,3},{3,1},{4,6},{6,4},{5,7},{7,5},{8,10},{10,8},{9,1... | collective-permute-start | bytes 786440 | tf_op jit(solution)/shard_map/ppermute | solution.py:292
  29.9 77.6 %copy-start.8 = (bf16[32,4096]{1,0:T(8,128)(2,1)}, bf16[32,4096]{1,0:T(8,128)(2,1)S(1)}, u32[]{:S(2)}) copy-start(bf16[32,4096]{1,0:T(8,128)(2,1)S(1)} %collective-permute-done.1.up_ref) | copy-start | bytes 786436
  29.9 18.8 %collective-permute-start.5 = (bf16[2,64,1280]{2,1,0:T(8,128)(2,1)S(1)}, bf16[2,64,1280]{2,1,0:T(8,128)(2,1)S(1)}, u32[]{:S(2)}, u32[]{:S(2)}) collective-permute-start(bf16[2,64,1280]{2,1,0:T(8,128)(2,1)S(1)} %copy-done.22), channel_id=1, source_target_pairs={{0,128},{64,192},{128,0},{192,64},{1,129},{65,193},{129,1},{193,65... | collective-permute-start | bytes 983048 | tf_op jit(solution)/shard_map/gather_weights/ppermute | solution.py:296
  36.2 7.1 %collective-permute-start.4 = (bf16[2,16,1280]{2,1,0:T(8,128)(2,1)S(1)}, bf16[2,16,1280]{2,1,0:T(8,128)(2,1)S(1)}, u32[]{:S(2)}, u32[]{:S(2)}) collective-permute-start(bf16[2,16,1280]{2,1,0:T(8,128)(2,1)S(1)} %slice.35), channel_id=1, source_target_pairs={{0,192},{64,0},{128,64},{192,128},{1,193},{65,1},{129,65},{193,129... | collective-permute-start | bytes 245768 | tf_op jit(solution)/shard_map/gather_weights/ppermute | solution.py:296
  39.0 9.7 %collective-permute-start.3 = (bf16[2,16,1280]{2,1,0:T(8,128)(2,1)S(1)}, bf16[2,16,1280]{2,1,0:T(8,128)(2,1)S(1)}, u32[]{:S(2)}, u32[]{:S(2)}) collective-permute-start(bf16[2,16,1280]{2,1,0:T(8,128)(2,1)S(1)} %slice.35), channel_id=1, source_target_pairs={{0,64},{64,128},{128,192},{192,0},{1,65},{65,129},{129,193},{193,1... | collective-permute-start | bytes 245768 | tf_op jit(solution)/shard_map/gather_weights/ppermute | solution.py:296
  107.5 46.3 %collective-permute-start.7 = (bf16[8,2,48,1280]{3,2,1,0:T(8,128)(2,1)S(1)}, bf16[8,2,48,1280]{3,2,1,0:T(8,128)(2,1)S(1)}, u32[]{:S(2)}, u32[]{:S(2)}) collective-permute-start(bf16[8,2,48,1280]{3,2,1,0:T(8,128)(2,1)S(1)} %get-tuple-element.53), channel_id=1, source_target_pairs={{0,192},{64,0},{128,64},{192,128},{1,193},{65,1},{129,65},{193,129... | collective-permute-start | bytes 5898248 | tf_op jit(solution)/shard_map/gather_weights/ppermute | solution.py:296
  111.9 47.1 %collective-permute-start.6 = (bf16[8,2,48,1280]{3,2,1,0:T(8,128)(2,1)S(1)}, bf16[8,2,48,1280]{3,2,1,0:T(8,128)(2,1)}, u32[]{:S(2)}, u32[]{:S(2)}) collective-permute-start(bf16[8,2,48,1280]{3,2,1,0:T(8,128)(2,1)S(1)} %get-tuple-element.53), channel_id=1, source_target_pairs={{0,64},{64,128},{128,192},{192,0},{1,65},{65,129},{129,193},{193,1... | collective-permute-start | bytes 5898248 | tf_op jit(solution)/shard_map/gather_weights/ppermute | solution.py:296
  153.8 61.3 %copy-start.21 = (bf16[8,2,48,1280]{3,2,1,0:T(8,128)(2,1)}, bf16[8,2,48,1280]{3,2,1,0:T(8,128)(2,1)S(1)}, u32[]{:S(2)}) copy-start(bf16[8,2,48,1280]{3,2,1,0:T(8,128)(2,1)S(1)} %collective-permute-done.7.refs_6_) | copy-start | bytes 5898244
  158.9 44.9 %collective-permute-start.12 = (bf16[8,2,48,1280]{3,2,1,0:T(8,128)(2,1)S(1)}, bf16[8,2,48,1280]{3,2,1,0:T(8,128)(2,1)}, u32[]{:S(2)}, u32[]{:S(2)}) collective-permute-start(bf16[8,2,48,1280]{3,2,1,0:T(8,128)(2,1)S(1)} %get-tuple-element.33), channel_id=1, source_target_pairs={{0,192},{64,0},{128,64},{192,128},{1,193},{65,1},{129,65},{193,129... | collective-permute-start | bytes 5898248 | tf_op jit(solution)/shard_map/gather_weights/ppermute | solution.py:296
  160.8 47.2 %collective-permute-start.9 = (bf16[8,2,48,1280]{3,2,1,0:T(8,128)(2,1)S(1)}, bf16[8,2,48,1280]{3,2,1,0:T(8,128)(2,1)}, u32[]{:S(2)}, u32[]{:S(2)}) collective-permute-start(bf16[8,2,48,1280]{3,2,1,0:T(8,128)(2,1)S(1)} %get-tuple-element.33), channel_id=1, source_target_pairs={{0,64},{64,128},{128,192},{192,0},{1,65},{65,129},{129,193},{193,1... | collective-permute-start | bytes 5898248 | tf_op jit(solution)/shard_map/gather_weights/ppermute | solution.py:296
  164.2 47.1 %collective-permute-start.8 = (bf16[8,2,48,1280]{3,2,1,0:T(8,128)(2,1)}, bf16[8,2,48,1280]{3,2,1,0:T(8,128)(2,1)}, u32[]{:S(2)}, u32[]{:S(2)}) collective-permute-start(bf16[8,2,48,1280]{3,2,1,0:T(8,128)(2,1)} %collective-permute-done.6.refs_2_), channel_id=1, source_target_pairs={{0,1},{1,0},{2,3},{3,2},{4,5},{5,4},{6,7},{7,6},{8,9},{9,8},{10,11... | collective-permute-start | bytes 5898248 | tf_op jit(solution)/shard_map/gather_weights/ppermute | solution.py:292
  168.1 43.2 %collective-permute-start.11 = (bf16[8,2,48,1280]{3,2,1,0:T(8,128)(2,1)S(1)}, bf16[8,2,48,1280]{3,2,1,0:T(8,128)(2,1)}, u32[]{:S(2)}, u32[]{:S(2)}) collective-permute-start(bf16[8,2,48,1280]{3,2,1,0:T(8,128)(2,1)S(1)} %collective-permute-done.7.refs_6_), channel_id=1, source_target_pairs={{0,1},{1,0},{2,3},{3,2},{4,5},{5,4},{6,7},{7,6},{8,9},{9,8},{10,11... | collective-permute-start | bytes 5898248 | tf_op jit(solution)/shard_map/gather_weights/ppermute | solution.py:292
  203.8 8.1 %collective-permute-start.13 = (bf16[8,2,48,1280]{3,2,1,0:T(8,128)(2,1)}, bf16[8,2,48,1280]{3,2,1,0:T(8,128)(2,1)}, u32[]{:S(2)}, u32[]{:S(2)}) collective-permute-start(bf16[8,2,48,1280]{3,2,1,0:T(8,128)(2,1)} %collective-permute-done.12.refs_8_), channel_id=1, source_target_pairs={{0,1},{1,0},{2,3},{3,2},{4,5},{5,4},{6,7},{7,6},{8,9},{9,8},{10,11... | collective-permute-start | bytes 5898248 | tf_op jit(solution)/shard_map/gather_weights/ppermute | solution.py:292
  208.1 7.0 %collective-permute-start.10 = (bf16[8,2,48,1280]{3,2,1,0:T(8,128)(2,1)}, bf16[8,2,48,1280]{3,2,1,0:T(8,128)(2,1)}, u32[]{:S(2)}, u32[]{:S(2)}) collective-permute-start(bf16[8,2,48,1280]{3,2,1,0:T(8,128)(2,1)} %collective-permute-done.9.refs_4_), channel_id=1, source_target_pairs={{0,1},{1,0},{2,3},{3,2},{4,5},{5,4},{6,7},{7,6},{8,9},{9,8},{10,11... | collective-permute-start | bytes 5898248 | tf_op jit(solution)/shard_map/gather_weights/ppermute | solution.py:292
  232.3 11.1 %collective-permute-start.14 = (bf16[32,4096]{1,0:T(8,128)(2,1)S(1)}, bf16[32,4096]{1,0:T(8,128)(2,1)S(1)}, u32[]{:S(2)}, u32[]{:S(2)}) collective-permute-start(bf16[32,4096]{1,0:T(8,128)(2,1)S(1)} %get-tuple-element.35), channel_id=1, source_target_pairs={{0,258},{2,256},{256,2},{258,0},{1,259},{3,257},{257,3},{259,1},{4... | collective-permute-start | bytes 786440 | tf_op jit(solution)/shard_map/ppermute | solution.py:300
  269.6 43.2 %all-to-all-start = ((bf16[16,32,1024]{2,1,0:T(8,128)(2,1)}), bf16[16,32,1024]{2,1,0:T(8,128)(2,1)S(1)}, u32[]{:S(2)}, u32[]{:S(2)}) async-start(bf16[16,32,1024]{2,1,0:T(8,128)(2,1)} %get-tuple-element.47), calls=%async_computation | async-start | bytes 2097152 | tf_op jit(solution)/shard_map/normed_slices/all_to_all | solution.py:371
  274.1 11.0 %collective-permute-start.15 = (bf16[32,4096]{1,0:T(8,128)(2,1)S(1)}, bf16[32,4096]{1,0:T(8,128)(2,1)S(1)}, u32[]{:S(2)}, u32[]{:S(2)}) collective-permute-start(bf16[32,4096]{1,0:T(8,128)(2,1)S(1)} %copy-done.20), channel_id=1, source_target_pairs={{0,258},{2,256},{256,2},{258,0},{1,259},{3,257},{257,3},{259,1},{4... | collective-permute-start | bytes 786440 | tf_op jit(solution)/shard_map/ppermute | solution.py:300
  325.3 72.5 %copy-start.23 = (f32[1,2,64,128]{3,2,1,0:T(8,128)S(1)}, f32[1,2,64,128]{3,2,1,0:T(8,128)}, u32[]{:S(2)}) copy-start(f32[1,2,64,128]{3,2,1,0:T(8,128)} %param.13) | copy-start | bytes 196612
  325.3 72.5 %copy-start.24 = (f32[1,2,64,128]{3,2,1,0:T(8,128)S(1)}, f32[1,2,64,128]{3,2,1,0:T(8,128)}, u32[]{:S(2)}) copy-start(f32[1,2,64,128]{3,2,1,0:T(8,128)} %param.15) | copy-start | bytes 196612
  325.4 72.5 %copy-start.25 = (f32[1,2,64,128]{3,2,1,0:T(8,128)S(1)}, f32[1,2,64,128]{3,2,1,0:T(8,128)}, u32[]{:S(2)}) copy-start(f32[1,2,64,128]{3,2,1,0:T(8,128)} %param.14) | copy-start | bytes 196612
  (21 other events, 273.7 us)
Sparse Core Ops, SparseCore 0:
  16.6 88.4 all-gather.4
  107.2 97.8 all-gather.6

commit v7 on v6

--- a/solution.py
+++ b/solution.py
@@ -27,12 +27,13 @@
 KVW = QW + 2 * HEAD
 COLS = KVW + QW
 CHUNK = 1024
-UPPER = 48
-EARLY = 8
-REST_AT = {1: 0, 3: 64 - UPPER, 2: 2 * (64 - UPPER)}
+ALONG_X = 896
+EARLY = 10
+REST_AT = {1: 0, 3: COLS - ALONG_X, 2: 2 * (COLS - ALONG_X)}
 SOURCES = 10
 SCALE = 1.0 / math.sqrt(HEAD)
 VMEM_LIMIT = 12 * 1024 * 1024
+VMEM_LAST = 56 * 1024 * 1024
 F32 = jnp.float32
 BF16 = jnp.bfloat16
 
@@ -57,15 +58,15 @@
             at = c * 2 + (side if other == 0 else 1 - side)
 
             def start(source, first, last, low=0, high=16, at=at):
-                target = weights[layer].at[at, low:high, first:last]
+                target = weights[layer].at[at, low:high, :, first:last]
                 pltpu.make_async_copy(source, target, sems.at[layer, at]).start()
 
             if distance == 0:
-                start(whole.at[:, c, other], 0, 64)
+                start(whole.at[:, c, other], 0, COLS)
                 continue
             begin = REST_AT[distance]
-            first = 0 if distance == 2 else UPPER
-            start(rest.at[:, c, other, begin : begin + 64 - first], first, 64)
+            first = 0 if distance == 2 else ALONG_X
+            start(rest.at[:, c, other, :, begin : begin + COLS - first], first, COLS)
             if distance == 2:
                 continue
             for own in range(2):
@@ -73,8 +74,8 @@
                 @pl.when((core == c) == (own == 0))
                 def _(own=own, other=other, start=start):
                     early, late = moved[(distance // 2) * 4 + own], moved[(distance // 2) * 4 + 2 + own]
-                    start(early.at[:, other], 0, UPPER, 0, EARLY)
-                    start(late.at[:, other], 0, UPPER, EARLY, 16)
+                    start(early.at[:, other], 0, ALONG_X, 0, EARLY)
+                    start(late.at[:, other], 0, ALONG_X, EARLY, 16)
 
 
 def start_layers(order, place, sources, weights, sems):
@@ -157,10 +158,12 @@
                 out_ref[:, at : at + CHUNK] = result
 
 
-def backward_layers(need_up, h_all, kept, up, g_all, weights):
+def backward_layers(need_up, h_all, kept, up, g_all, weights, sems):
     i_all, q_all, k_all, v_all, p_all = kept
 
     def project(layer, at, rows, acc):
+        if sems is not None:
+            wait_rows(weights, sems, layer, at)
         return acc + dot_nn(rows, weight_rows(weights, layer, at, KVW, COLS))
 
     acc = jnp.zeros((LENGTH, QW), F32)
@@ -225,12 +228,13 @@
     out_ref[...] = up_ref[...]
     mask = attention_mask(seg_col, seg_row)
     forward_layers(mask, h_all, kept, None, weights, None)
-    backward_layers(True, h_all, kept[1:], out_ref, None, weights)
+    backward_layers(True, h_all, kept[1:], out_ref, None, weights, None)
 
 
 def last_kernel(place, up_ref, arrived, h_all, i_all, q_all, k_all, v_all, p_all, *refs):
-    weights, refs = refs[:LAYERS], refs[LAYERS:]
-    g_all, up = refs
+    sources, refs = refs[:SOURCES], refs[SOURCES:]
+    g_all, up, sems, *weights = refs
+    start_layers(reversed(range(LAYERS)), place, sources, weights, sems)
 
     @pl.when(place[2] == 0)
     def _():
@@ -241,7 +245,7 @@
         up[...] = up_ref[...]
 
     kept = (i_all, q_all, k_all, v_all, p_all)
-    backward_layers(False, h_all, kept, up, g_all, weights)
+    backward_layers(False, h_all, kept, up, g_all, weights, sems)
 
 
 VM = pl.BlockSpec(memory_space=pltpu.VMEM)
@@ -252,13 +256,13 @@
 ROWS = jax.ShapeDtypeStruct((LENGTH, WIDTH), BF16)
 ROWS_ALL = pltpu.VMEM((LAYERS, LENGTH, WIDTH), BF16)
 STATE_SHAPES = (
-    jax.ShapeDtypeStruct((LAYERS, LENGTH, WIDTH), BF16),
-    jax.ShapeDtypeStruct((LAYERS * 4, LENGTH, CHUNK), BF16),
-    jax.ShapeDtypeStruct((LAYERS, LENGTH, HEAD), F32),
-    jax.ShapeDtypeStruct((LAYERS, LENGTH * HEADS, HEAD), BF16),
-    jax.ShapeDtypeStruct((LAYERS, LENGTH, HEAD), BF16),
-    jax.ShapeDtypeStruct((LAYERS, LENGTH, HEAD), BF16),
-    jax.ShapeDtypeStruct((LAYERS, LENGTH * HEADS, LENGTH), F32),
+    pltpu.HBM((LAYERS, LENGTH, WIDTH), BF16),
+    pltpu.HBM((LAYERS * 4, LENGTH, CHUNK), BF16),
+    pltpu.HBM((LAYERS, LENGTH, HEAD), F32),
+    pltpu.HBM((LAYERS, LENGTH * HEADS, HEAD), BF16),
+    pltpu.HBM((LAYERS, LENGTH, HEAD), BF16),
+    pltpu.HBM((LAYERS, LENGTH, HEAD), BF16),
+    pltpu.HBM((LAYERS, LENGTH * HEADS, LENGTH), F32),
 )
 
 
@@ -270,14 +274,16 @@
     )
 
 
-def call(kernel, name, products, out_shape, inputs, sources, scratch):
+def call(
+    kernel, name, products, out_shape, inputs, sources, scratch, limit=VMEM_LIMIT
+):
     return pl.pallas_call(
         kernel,
         out_shape=out_shape,
         in_specs=[SM] + [VM] * (len(inputs) - 1) + [ANY] * len(sources),
         out_specs=(VM,) * len(out_shape),
         scratch_shapes=scratch,
-        compiler_params=pltpu.CompilerParams(vmem_limit_bytes=VMEM_LIMIT),
+        compiler_params=pltpu.CompilerParams(vmem_limit_bytes=limit),
         cost_estimate=cost(products),
         name=name,
     )(*inputs, *sources)
@@ -302,14 +308,15 @@
 
 def gather_layers(pair, rest, c):
     whole = lax.all_gather(pair, ("z", "c"), axis=0).reshape(16, 2, 2, 64, COLS)
-    rest = [turned(rest[:, UPPER:], 1), turned(rest[:, UPPER:], 3), turned(rest, 2)]
-    rest = jnp.concatenate(rest, axis=1)
-    rest = lax.all_gather(rest, ("z", "c"), axis=0).reshape(16, 2, 2, -1, COLS)
-    share = lax.dynamic_slice(whole, (0, c, 0, 0, 0), (16, 1, 2, UPPER, COLS))[:, 0]
+    edge = rest[:, :, ALONG_X:]
+    rest = jnp.concatenate([turned(edge, 1), turned(edge, 3), turned(rest, 2)], axis=2)
+    rest = lax.all_gather(rest, ("z", "c"), axis=0).reshape(16, 2, 2, 64, -1)
+    share = lax.dynamic_slice(whole, (0, c, 0, 0, 0), (16, 1, 2, 64, ALONG_X))[:, 0]
     early, late = share[:EARLY], share[EARLY:]
     near, far = turned(early, 1), turned(early, 3)
-    near, far, late = lax.optimization_barrier((near, far, late))
-    near_late, far_late = turned(late, 1), turned(late, 3)
+    near, late_near = lax.optimization_barrier((near, late))
+    far, late_far = lax.optimization_barrier((far, late))
+    near_late, far_late = turned(late_near, 1), turned(late_far, 3)
     moved = []
     for block in (near, near_late, far, far_late):
         moved += [block, swap(block, "c")]
@@ -375,9 +382,10 @@
         "first_backward",
         LAYERS,
         (jax.ShapeDtypeStruct((LAYERS * 4, LENGTH, 2 * HEAD), BF16),),
-        (place, up_in, arrived, h_all, *kept, *weights),
-        (),
-        [pltpu.VMEM((LENGTH, WIDTH), BF16)],
+        (place, up_in, arrived, h_all, *kept),
+        sources,
+        [pltpu.VMEM((LENGTH, WIDTH), BF16), WEIGHT_SEMS, *WEIGHTS],
+        VMEM_LAST,
     )
 
     with jax.named_scope("gather_grads"):

time: 407 us -> 396 us (0.973)
  local copies, waits for them, and re-layouts: 26.8 us -> 15.5 us
  waiting for transfers between devices: 164 us -> 154 us
  Pallas kernels: 51.7 us -> 57.7 us
    unnamed x52 -> x28, local copies, waits for them, and re-layouts: 19.2 us -> 4.81 us
    ppermute x7, waiting for transfers between devices: 86.1 us -> 76.1 us  [turned(): return lax.ppermute(block, 'x', [(i, (i + distance) % 4) for i in range(4)])]
    pallas_call x3, Pallas kernels: 51.7 us -> 57.7 us  [call(): pl.pallas_call(kernel, out_shape=out_shape, in_specs=[SM] + [VM] * (len(i...]
  transfers between devices with their start and end apart: 19 -> 19, of which waited for: 12 -> 12; matrix products, arithmetic and copies ran while one was open for 2% -> 3% of each run, Pallas kernels for 3% -> 4%
where the time goes in v7:
time: 396 us; the launch traced here: 395 us
  waiting for transfers between devices  154 us (39%)
  blocking collectives  84 us (21%)
  starting transfers between devices  62.8 us (16%)
  Pallas kernels  57.7 us (15%)
  local copies, waits for them, and re-layouts  15.5 us (4%)
  between operations  15.1 us (4%)
  other arithmetic  5.57 us (1%)
    ppermute x7, waiting for transfers between devices, turned(): return lax.ppermute(block, 'x', [(i, (i + distance) % 4) for i in range(4)])  76.1 us
    pallas_call x3, Pallas kernels, call(): pl.pallas_call(kernel, out_shape=out_shape, in_specs=[SM] + [VM] * (len(i...  57.7 us
    all_gather x1, waiting for transfers between devices, gather_layers(): whole = lax.all_gather(pair, ('z', 'c'), axis=0).reshape(16, 2, 2, 64, COLS)  55.4 us
    all_to_all x2, blocking collectives, sum_over(): return jnp.sum(lax.all_to_all(spread, axes, 0, 0, tiled=True), axis=0)  40.4 us
    all_to_all x1, blocking collectives, shards(): parts = lax.all_to_all(partial, 'z', 0, 0, tiled=True)  31.1 us
    ppermute x7, starting transfers between devices, turned(): return lax.ppermute(block, 'x', [(i, (i + distance) % 4) for i in range(4)])  25 us
    ppermute x7, starting transfers between devices, swap(): return lax.ppermute(block, axis, [(0, 1), (1, 0)])  22.1 us
    ppermute x2, waiting for transfers between devices, across(): return lax.ppermute(block, ('yh', 'yl'), [(i, 3 - i) for i in range(4)])  12.9 us
  transfers between devices with their start and end apart: 19, of which 12 were waited for; matrix products, arithmetic and copies ran while one was open for 3% of the time, Pallas kernels for 4%

profile of v7, /device:TPU:1, one launch (start us, length us, event | category | flops | bytes accessed | tf_op | source)
XLA Modules:
  0.0 395.1 jit_solution(7819861235892212875)
XLA Ops:
  9.0 4.0 %collective-permute-start = (bf16[64,1280]{1,0:T(8,128)(2,1)S(1)}, bf16[64,1280]{1,0:T(8,128)(2,1)S(1)}, u32[]{:S(2)}, u32[]{:S(2)}) collective-permute-start(bf16[64,1280]{1,0:T(8,128)(2,1)S(1)} %get-tuple-element.55), channel_id=1, source_target_pairs={{0,2},{2,0},{1,3},{3,1},{4,6},{6,4},{5,7},{7,5},{8,10},{10,8},{9,1... | collective-permute-start | bytes 491528 | tf_op jit(solution)/shard_map/gather_weights/ppermute | solution.py:298
  17.2 3.4 collective-permute-start.2
  29.9 6.3 %collective-permute-start.5 = (bf16[2,64,1280]{2,1,0:T(8,128)(2,1)S(1)}, bf16[2,64,1280]{2,1,0:T(8,128)(2,1)S(1)}, u32[]{:S(2)}, u32[]{:S(2)}) collective-permute-start(bf16[2,64,1280]{2,1,0:T(8,128)(2,1)S(1)} %copy-done.9), channel_id=1, source_target_pairs={{0,128},{64,192},{128,0},{192,64},{1,129},{65,193},{129,1},{193,65... | collective-permute-start | bytes 983048 | tf_op jit(solution)/shard_map/gather_weights/ppermute | solution.py:302
  43.7 5.2 %collective-permute-done.3 = bf16[2,64,384]{2,1,0:T(8,128)(2,1)S(1)} collective-permute-done((bf16[2,64,384]{2,1,0:T(8,128)(2,1)S(1)}, bf16[2,64,384]{2,1,0:T(8,128)(2,1)S(1)}, u32[]{:S(2)}, u32[]{:S(2)}) %collective-permute-start.3) | collective-permute-done | bytes 98336 | tf_op jit(solution)/shard_map/gather_weights/ppermute | solution.py:302
  49.8 55.4 %all-gather.5.cloned.1.call-done = bf16[64,64,1280]{2,1,0:T(8,128)(2,1)} async-done(((bf16[2,64,1280]{2,1,0:T(8,128)(2,1)}), bf16[64,64,1280]{2,1,0:T(8,128)(2,1)}) %all-gather.5.cloned.1.call-update) | async-done | bytes 10485776 | tf_op jit(solution)/shard_map/gather_weights/all_gather | solution.py:310
  105.2 3.2 dynamic-slice_bitcast_fusion
  108.4 4.3 %collective-permute-start.10 = (bf16[10,2,64,896]{3,2,1,0:T(8,128)(2,1)}, bf16[10,2,64,896]{3,2,1,0:T(8,128)(2,1)S(1)}, u32[]{:S(2)}, u32[]{:S(2)}) collective-permute-start(bf16[10,2,64,896]{3,2,1,0:T(8,128)(2,1)} %dynamic-slice_bitcast_fusion), channel_id=1, source_target_pairs={{0,192},{64,0},{128,64},{192,128},{1,193},{65,1},{129,65},{193,129... | collective-permute-start | bytes 6881288 | tf_op jit(solution)/shard_map/gather_weights/ppermute | solution.py:302
  116.2 45.8 %collective-permute-done.10.refs_6_ = bf16[10,2,64,896]{3,2,1,0:T(8,128)(2,1)S(1)} collective-permute-done((bf16[10,2,64,896]{3,2,1,0:T(8,128)(2,1)}, bf16[10,2,64,896]{3,2,1,0:T(8,128)(2,1)S(1)}, u32[]{:S(2)}, u32[]{:S(2)}) %collective-permute-start.10) | collective-permute-done | bytes 2293792 | tf_op jit(solution)/shard_map/gather_weights/ppermute | solution.py:302
  162.0 5.3 %collective-permute-start.12 = (bf16[6,2,64,896]{3,2,1,0:T(8,128)(2,1)S(1)}, bf16[6,2,64,896]{3,2,1,0:T(8,128)(2,1)}, u32[]{:S(2)}, u32[]{:S(2)}) collective-permute-start(bf16[6,2,64,896]{3,2,1,0:T(8,128)(2,1)S(1)} %dynamic-slice_bitcast_fusion.1), channel_id=1, source_target_pairs={{0,192},{64,0},{128,64},{192,128},{1,193},{65,1},{129,65},{193,129... | collective-permute-start | bytes 4128776 | tf_op jit(solution)/shard_map/gather_weights/ppermute | solution.py:302
  174.4 21.5 %collective-permute-done.12.refs_8_ = bf16[6,2,64,896]{3,2,1,0:T(8,128)(2,1)} collective-permute-done((bf16[6,2,64,896]{3,2,1,0:T(8,128)(2,1)S(1)}, bf16[6,2,64,896]{3,2,1,0:T(8,128)(2,1)}, u32[]{:S(2)}, u32[]{:S(2)}) %collective-permute-start.12) | collective-permute-done | bytes 1376288 | tf_op jit(solution)/shard_map/gather_weights/ppermute | solution.py:302
  195.8 3.8 collective-permute-start.13
  201.0 4.0 %collective-permute-start.9 = (bf16[6,2,64,896]{3,2,1,0:T(8,128)(2,1)S(1)}, bf16[6,2,64,896]{3,2,1,0:T(8,128)(2,1)}, u32[]{:S(2)}, u32[]{:S(2)}) collective-permute-start(bf16[6,2,64,896]{3,2,1,0:T(8,128)(2,1)S(1)} %collective-permute-done.8.refs_4_), channel_id=1, source_target_pairs={{0,1},{1,0},{2,3},{3,2},{4,5},{5,4},{6,7},{7,6},{8,9},{9,8},{10,11... | collective-permute-start | bytes 4128776 | tf_op jit(solution)/shard_map/gather_weights/ppermute | solution.py:298
  212.7 17.1 %first_forward.1 = (bf16[32,4096]{1,0:T(8,128)(2,1)S(1)}, bf16[4,16,64,1280]{3,2,1,0:T(8,128)(2,1)S(1)}, bf16[4,16,64,1280]{3,2,1,0:T(8,128)(2,1)S(1)}, bf16[4,1...) custom-call(s32[4]{0:T(128)S(1)} %pad_add_fusion.place, bf16[32,4096]{1,0:T(8,128)(2,1)S(1)} %copy-done.2, ...), custom_call_target="tpu_custom_call" | custom-call | flops 1342177280 | bytes 41943040 | tf_op jit(solution)/shard_map/first_forward/pallas_call | solution.py:280
  229.8 4.7 %collective-permute-start.14 = (bf16[32,4096]{1,0:T(8,128)(2,1)S(1)}, bf16[32,4096]{1,0:T(8,128)(2,1)S(1)}, u32[]{:S(2)}, u32[]{:S(2)}) collective-permute-start(bf16[32,4096]{1,0:T(8,128)(2,1)S(1)} %get-tuple-element.37), channel_id=1, source_target_pairs={{0,258},{2,256},{256,2},{258,0},{1,259},{3,257},{257,3},{259,1},{4... | collective-permute-start | bytes 786440 | tf_op jit(solution)/shard_map/ppermute | solution.py:306
  234.5 6.3 %collective-permute-done.14.arrived = bf16[32,4096]{1,0:T(8,128)(2,1)S(1)} collective-permute-done((bf16[32,4096]{1,0:T(8,128)(2,1)S(1)}, bf16[32,4096]{1,0:T(8,128)(2,1)S(1)}, u32[]{:S(2)}, u32[]{:S(2)}) %collective-permute-start.14) | collective-permute-done | bytes 262176 | tf_op jit(solution)/shard_map/ppermute | solution.py:306
  240.8 23.0 %second_forward_backward.1 = (bf16[32,4096]{1,0:T(8,128)(2,1)S(1)}, bf16[4,32,4096]{2,1,0:T(8,128)(2,1)}, bf16[16,32,1024]{2,1,0:T(8,128)(2,1)}, f32[4,32,128]{2...) custom-call(s32[4]{0:T(128)S(1)} %pad_add_fusion.place, ...), custom_call_target="tpu_custom_call" | custom-call | flops 2684354560 | bytes 41943040 | tf_op jit(solution)/shard_map/second_forward_backward/pallas_call | solution.py:280
  264.5 5.3 %all-to-all-start = ((bf16[16,32,1024]{2,1,0:T(8,128)(2,1)}), bf16[16,32,1024]{2,1,0:T(8,128)(2,1)S(1)}, u32[]{:S(2)}, u32[]{:S(2)}) async-start(bf16[16,32,1024]{2,1,0:T(8,128)(2,1)} %get-tuple-element.49), calls=%async_computation | async-start | bytes 2097152 | tf_op jit(solution)/shard_map/normed_slices/all_to_all | solution.py:378
  269.8 5.7 %collective-permute-start.15 = (bf16[32,4096]{1,0:T(8,128)(2,1)}, bf16[32,4096]{1,0:T(8,128)(2,1)S(1)}, u32[]{:S(2)}, u32[]{:S(2)}) collective-permute-start(bf16[32,4096]{1,0:T(8,128)(2,1)} %copy-done.6), channel_id=1, source_target_pairs={{0,258},{2,256},{256,2},{258,0},{1,259},{3,257},{257,3},{259,1},{4... | collective-permute-start | bytes 786440 | tf_op jit(solution)/shard_map/ppermute | solution.py:306
  275.4 6.6 %collective-permute-done.15.arrived = bf16[32,4096]{1,0:T(8,128)(2,1)S(1)} collective-permute-done((bf16[32,4096]{1,0:T(8,128)(2,1)}, bf16[32,4096]{1,0:T(8,128)(2,1)S(1)}, u32[]{:S(2)}, u32[]{:S(2)}) %collective-permute-start.15) | collective-permute-done | bytes 262176 | tf_op jit(solution)/shard_map/ppermute | solution.py:306
  282.7 17.7 %first_backward.1 = bf16[16,32,256]{2,1,0:T(8,128)(2,1)} custom-call(s32[4]{0:T(128)} %copy-done.5, bf16[32,4096]{1,0:T(8,128)(2,1)} %copy-done.3, bf16[32,4096]{1,0:T(8,128)(2,1)} %copy-done.10, bf16[4,32,4096]{2,1,0:T(8,128)(2,1)} %get-tuple-element.43.h_all, f32[4,32,128]{2,1,0:T(8,128)} %get-tuple-element.44.i_all, ...), custom_call_target="tpu_custom_call" | custom-call | flops 1342177280 | bytes 41943040 | tf_op jit(solution)/shard_map/first_backward/pallas_call | solution.py:280
  300.4 12.6 %all_to_all.25 = bf16[16,32,256]{2,1,0:T(8,128)(2,1)S(1)} all-to-all(bf16[16,32,256]{2,1,0:T(8,128)(2,1)} %first_backward.1), channel_id=1, replica_groups=mesh['yh'=2,'x'=4,'z'=16,'yl'=2,'c'=2] {'x','yl','c'}, dimensions={0} | all-to-all | bytes 524288 | tf_op jit(solution)/shard_map/gather_grads/all_to_all | solution.py:393
  313.5 31.1 %all_to_all.26 = bf16[16,64,256]{2,1,0:T(8,128)(2,1)S(1)} all-to-all(bf16[16,64,256]{2,1,0:T(8,128)(2,1)S(1)} %bitcast.61), channel_id=1, replica_groups=mesh['yh'=2,'x'=4,'z'=16,'yl'=2,'c'=2] {'z'}, dimensions={0} | all-to-all | bytes 1048576 | tf_op jit(solution)/shard_map/sum_grads/all_to_all | solution.py:397
  345.9 24.2 %all_to_all.27 = f32[16,8,128]{2,1,0:T(8,128)S(1)} all-to-all(f32[16,8,128]{2,1,0:T(8,128)S(1)} %broadcast_in_dim.16), channel_id=1, replica_groups=mesh['yh'=2,'x'=4,'z'=16,'yl'=2,'c'=2] {'z'}, dimensions={0} | all-to-all | bytes 131072 | tf_op jit(solution)/shard_map/clip/all_to_all | solution.py:328
  370.2 16.2 %all_to_all.28 = f32[32,8,128]{2,1,0:T(8,128)S(1)} all-to-all(f32[32,8,128]{2,1,0:T(8,128)S(1)} %broadcast_in_dim.17), channel_id=1, replica_groups=mesh['yh'=2,'x'=4,'z'=16,'yl'=2,'c'=2] {'yh','x','yl','c'}, dimensions={0} | all-to-all | bytes 262144 | tf_op jit(solution)/shard_map/clip/all_to_all | solution.py:328
  (80 shorter events, 47.7 us)
Async XLA Ops:
  7.2 98.0 %all-gather.5.cloned.1.call-start = ((), (), s32[]{:S(2)}) async-start(), calls=%async_computation.5 | async-start | bytes 10813440 | tf_op jit(solution)/shard_map/gather_weights/all_gather | solution.py:310
  9.0 6.7 %collective-permute-start = (bf16[64,1280]{1,0:T(8,128)(2,1)S(1)}, bf16[64,1280]{1,0:T(8,128)(2,1)S(1)}, u32[]{:S(2)}, u32[]{:S(2)}) collective-permute-start(bf16[64,1280]{1,0:T(8,128)(2,1)S(1)} %get-tuple-element.55), channel_id=1, source_target_pairs={{0,2},{2,0},{1,3},{3,1},{4,6},{6,4},{5,7},{7,5},{8,10},{10,8},{9,1... | collective-permute-start | bytes 491528 | tf_op jit(solution)/shard_map/gather_weights/ppermute | solution.py:298
  16.5 193.9 %all-gather.7.cloned.1.call-start = ((), (), s32[]{:S(2)}) async-start(), calls=%async_computation.6 | async-start | bytes 17301504 | tf_op jit(solution)/shard_map/gather_weights/all_gather | solution.py:313
  17.2 9.4 %collective-permute-start.2 = (s32[32]{0:T(128)S(1)}, s32[32]{0:T(128)S(1)}, u32[]{:S(2)}, u32[]{:S(2)}) collective-permute-start(s32[32]{0:T(128)S(1)} %fusion.5), channel_id=1, source_target_pairs={{0,2},{2,0},{1,3},{3,1},{4,6},{6,4},{5,7},{7,5},{8,10},{10,8},{9,1... | collective-permute-start | bytes 392 | tf_op jit(solution)/shard_map/ppermute | solution.py:298
  22.8 7.1 %collective-permute-start.1 = (bf16[32,4096]{1,0:T(8,128)(2,1)S(1)}, bf16[32,4096]{1,0:T(8,128)(2,1)S(1)}, u32[]{:S(2)}, u32[]{:S(2)}) collective-permute-start(bf16[32,4096]{1,0:T(8,128)(2,1)S(1)} %reshape.99), channel_id=1, source_target_pairs={{0,2},{2,0},{1,3},{3,1},{4,6},{6,4},{5,7},{7,5},{8,10},{10,8},{9,1... | collective-permute-start | bytes 786440 | tf_op jit(solution)/shard_map/ppermute | solution.py:298
  24.8 216.0 %copy-start.5 = (s32[4]{0:T(128)}, s32[4]{0:T(128)S(1)}, u32[]{:S(2)}) copy-start(s32[4]{0:T(128)S(1)} %pad_add_fusion.place) | copy-start | bytes 52
  29.9 78.5 %copy-start.3 = (bf16[32,4096]{1,0:T(8,128)(2,1)}, bf16[32,4096]{1,0:T(8,128)(2,1)S(1)}, u32[]{:S(2)}) copy-start(bf16[32,4096]{1,0:T(8,128)(2,1)S(1)} %collective-permute-done.1.up_ref) | copy-start | bytes 786436
  29.9 19.0 %collective-permute-start.5 = (bf16[2,64,1280]{2,1,0:T(8,128)(2,1)S(1)}, bf16[2,64,1280]{2,1,0:T(8,128)(2,1)S(1)}, u32[]{:S(2)}, u32[]{:S(2)}) collective-permute-start(bf16[2,64,1280]{2,1,0:T(8,128)(2,1)S(1)} %copy-done.9), channel_id=1, source_target_pairs={{0,128},{64,192},{128,0},{192,64},{1,129},{65,193},{129,1},{193,65... | collective-permute-start | bytes 983048 | tf_op jit(solution)/shard_map/gather_weights/ppermute | solution.py:302
  36.2 7.5 %collective-permute-start.4 = (bf16[2,64,384]{2,1,0:T(8,128)(2,1)S(1)}, bf16[2,64,384]{2,1,0:T(8,128)(2,1)S(1)}, u32[]{:S(2)}, u32[]{:S(2)}) collective-permute-start(bf16[2,64,384]{2,1,0:T(8,128)(2,1)S(1)} %slice.34), channel_id=1, source_target_pairs={{0,192},{64,0},{128,64},{192,128},{1,193},{65,1},{129,65},{193,129... | collective-permute-start | bytes 294920 | tf_op jit(solution)/shard_map/gather_weights/ppermute | solution.py:302
  39.0 9.9 %collective-permute-start.3 = (bf16[2,64,384]{2,1,0:T(8,128)(2,1)S(1)}, bf16[2,64,384]{2,1,0:T(8,128)(2,1)S(1)}, u32[]{:S(2)}, u32[]{:S(2)}) collective-permute-start(bf16[2,64,384]{2,1,0:T(8,128)(2,1)S(1)} %slice.34), channel_id=1, source_target_pairs={{0,64},{64,128},{128,192},{192,0},{1,65},{65,129},{129,193},{193,1... | collective-permute-start | bytes 294920 | tf_op jit(solution)/shard_map/gather_weights/ppermute | solution.py:302
  108.4 53.6 %collective-permute-start.10 = (bf16[10,2,64,896]{3,2,1,0:T(8,128)(2,1)}, bf16[10,2,64,896]{3,2,1,0:T(8,128)(2,1)S(1)}, u32[]{:S(2)}, u32[]{:S(2)}) collective-permute-start(bf16[10,2,64,896]{3,2,1,0:T(8,128)(2,1)} %dynamic-slice_bitcast_fusion), channel_id=1, source_target_pairs={{0,192},{64,0},{128,64},{192,128},{1,193},{65,1},{129,65},{193,129... | collective-permute-start | bytes 6881288 | tf_op jit(solution)/shard_map/gather_weights/ppermute | solution.py:302
  112.7 54.6 %collective-permute-start.6 = (bf16[10,2,64,896]{3,2,1,0:T(8,128)(2,1)}, bf16[10,2,64,896]{3,2,1,0:T(8,128)(2,1)}, u32[]{:S(2)}, u32[]{:S(2)}) collective-permute-start(bf16[10,2,64,896]{3,2,1,0:T(8,128)(2,1)} %dynamic-slice_bitcast_fusion), channel_id=1, source_target_pairs={{0,64},{64,128},{128,192},{192,0},{1,65},{65,129},{129,193},{193,1... | collective-permute-start | bytes 6881288 | tf_op jit(solution)/shard_map/gather_weights/ppermute | solution.py:302
  162.0 33.8 %collective-permute-start.12 = (bf16[6,2,64,896]{3,2,1,0:T(8,128)(2,1)S(1)}, bf16[6,2,64,896]{3,2,1,0:T(8,128)(2,1)}, u32[]{:S(2)}, u32[]{:S(2)}) collective-permute-start(bf16[6,2,64,896]{3,2,1,0:T(8,128)(2,1)S(1)} %dynamic-slice_bitcast_fusion.1), channel_id=1, source_target_pairs={{0,192},{64,0},{128,64},{192,128},{1,193},{65,1},{129,65},{193,129... | collective-permute-start | bytes 4128776 | tf_op jit(solution)/shard_map/gather_weights/ppermute | solution.py:302
  167.3 33.6 %collective-permute-start.8 = (bf16[6,2,64,896]{3,2,1,0:T(8,128)(2,1)S(1)}, bf16[6,2,64,896]{3,2,1,0:T(8,128)(2,1)S(1)}, u32[]{:S(2)}, u32[]{:S(2)}) collective-permute-start(bf16[6,2,64,896]{3,2,1,0:T(8,128)(2,1)S(1)} %dynamic-slice_bitcast_fusion.1), channel_id=1, source_target_pairs={{0,64},{64,128},{128,192},{192,0},{1,65},{65,129},{129,193},{193,1... | collective-permute-start | bytes 4128776 | tf_op jit(solution)/shard_map/gather_weights/ppermute | solution.py:302
  169.3 36.9 %collective-permute-start.11 = (bf16[10,2,64,896]{3,2,1,0:T(8,128)(2,1)}, bf16[10,2,64,896]{3,2,1,0:T(8,128)(2,1)}, u32[]{:S(2)}, u32[]{:S(2)}) collective-permute-start(bf16[10,2,64,896]{3,2,1,0:T(8,128)(2,1)} %copy-done.7), channel_id=1, source_target_pairs={{0,1},{1,0},{2,3},{3,2},{4,5},{5,4},{6,7},{7,6},{8,9},{9,8},{10,11... | collective-permute-start | bytes 6881288 | tf_op jit(solution)/shard_map/gather_weights/ppermute | solution.py:298
  172.4 33.7 %collective-permute-start.7 = (bf16[10,2,64,896]{3,2,1,0:T(8,128)(2,1)}, bf16[10,2,64,896]{3,2,1,0:T(8,128)(2,1)}, u32[]{:S(2)}, u32[]{:S(2)}) collective-permute-start(bf16[10,2,64,896]{3,2,1,0:T(8,128)(2,1)} %collective-permute-done.6.refs_2_), channel_id=1, source_target_pairs={{0,1},{1,0},{2,3},{3,2},{4,5},{5,4},{6,7},{7,6},{8,9},{9,8},{10,11... | collective-permute-start | bytes 6881288 | tf_op jit(solution)/shard_map/gather_weights/ppermute | solution.py:298
  195.8 10.3 %collective-permute-start.13 = (bf16[6,2,64,896]{3,2,1,0:T(8,128)(2,1)}, bf16[6,2,64,896]{3,2,1,0:T(8,128)(2,1)S(1)}, u32[]{:S(2)}, u32[]{:S(2)}) collective-permute-start(bf16[6,2,64,896]{3,2,1,0:T(8,128)(2,1)} %collective-permute-done.12.refs_8_), channel_id=1, source_target_pairs={{0,1},{1,0},{2,3},{3,2},{4,5},{5,4},{6,7},{7,6},{8,9},{9,8},{10,11... | collective-permute-start | bytes 4128776 | tf_op jit(solution)/shard_map/gather_weights/ppermute | solution.py:298
  201.0 6.8 %collective-permute-start.9 = (bf16[6,2,64,896]{3,2,1,0:T(8,128)(2,1)S(1)}, bf16[6,2,64,896]{3,2,1,0:T(8,128)(2,1)}, u32[]{:S(2)}, u32[]{:S(2)}) collective-permute-start(bf16[6,2,64,896]{3,2,1,0:T(8,128)(2,1)S(1)} %collective-permute-done.8.refs_4_), channel_id=1, source_target_pairs={{0,1},{1,0},{2,3},{3,2},{4,5},{5,4},{6,7},{7,6},{8,9},{9,8},{10,11... | collective-permute-start | bytes 4128776 | tf_op jit(solution)/shard_map/gather_weights/ppermute | solution.py:298
  229.8 11.0 %collective-permute-start.14 = (bf16[32,4096]{1,0:T(8,128)(2,1)S(1)}, bf16[32,4096]{1,0:T(8,128)(2,1)S(1)}, u32[]{:S(2)}, u32[]{:S(2)}) collective-permute-start(bf16[32,4096]{1,0:T(8,128)(2,1)S(1)} %get-tuple-element.37), channel_id=1, source_target_pairs={{0,258},{2,256},{256,2},{258,0},{1,259},{3,257},{257,3},{259,1},{4... | collective-permute-start | bytes 786440 | tf_op jit(solution)/shard_map/ppermute | solution.py:306
  264.5 35.9 %all-to-all-start = ((bf16[16,32,1024]{2,1,0:T(8,128)(2,1)}), bf16[16,32,1024]{2,1,0:T(8,128)(2,1)S(1)}, u32[]{:S(2)}, u32[]{:S(2)}) async-start(bf16[16,32,1024]{2,1,0:T(8,128)(2,1)} %get-tuple-element.49), calls=%async_computation | async-start | bytes 2097152 | tf_op jit(solution)/shard_map/normed_slices/all_to_all | solution.py:378
  269.8 12.2 %collective-permute-start.15 = (bf16[32,4096]{1,0:T(8,128)(2,1)}, bf16[32,4096]{1,0:T(8,128)(2,1)S(1)}, u32[]{:S(2)}, u32[]{:S(2)}) collective-permute-start(bf16[32,4096]{1,0:T(8,128)(2,1)} %copy-done.6), channel_id=1, source_target_pairs={{0,258},{2,256},{256,2},{258,0},{1,259},{3,257},{257,3},{259,1},{4... | collective-permute-start | bytes 786440 | tf_op jit(solution)/shard_map/ppermute | solution.py:306
  313.0 74.6 %copy-start.11 = (f32[1,2,64,128]{3,2,1,0:T(8,128)S(1)}, f32[1,2,64,128]{3,2,1,0:T(8,128)}, u32[]{:S(2)}) copy-start(f32[1,2,64,128]{3,2,1,0:T(8,128)} %param.13) | copy-start | bytes 196612
  313.0 74.6 %copy-start.12 = (f32[1,2,64,128]{3,2,1,0:T(8,128)S(1)}, f32[1,2,64,128]{3,2,1,0:T(8,128)}, u32[]{:S(2)}) copy-start(f32[1,2,64,128]{3,2,1,0:T(8,128)} %param.15) | copy-start | bytes 196612
  313.0 74.6 %copy-start.13 = (f32[1,2,64,128]{3,2,1,0:T(8,128)S(1)}, f32[1,2,64,128]{3,2,1,0:T(8,128)}, u32[]{:S(2)}) copy-start(f32[1,2,64,128]{3,2,1,0:T(8,128)} %param.14) | copy-start | bytes 196612
  (9 other events, 50.2 us)
Sparse Core Ops, SparseCore 0:
  16.6 88.5 all-gather.4
  107.3 103.0 all-gather.6

commit v8 on v7

--- a/solution.py
+++ b/solution.py
@@ -27,13 +27,14 @@
 KVW = QW + 2 * HEAD
 COLS = KVW + QW
 CHUNK = 1024
+LOADED = 1
 ALONG_X = 896
 EARLY = 10
 REST_AT = {1: 0, 3: COLS - ALONG_X, 2: 2 * (COLS - ALONG_X)}
 SOURCES = 10
 SCALE = 1.0 / math.sqrt(HEAD)
-VMEM_LIMIT = 12 * 1024 * 1024
-VMEM_LAST = 56 * 1024 * 1024
+VMEM_LIMIT = 7 * 1024 * 1024
+VMEM_LAST = 37 * 1024 * 1024
 F32 = jnp.float32
 BF16 = jnp.bfloat16
 
@@ -162,7 +163,7 @@
     i_all, q_all, k_all, v_all, p_all = kept
 
     def project(layer, at, rows, acc):
-        if sems is not None:
+        if sems is not None and layer < LAYERS - LOADED:
             wait_rows(weights, sems, layer, at)
         return acc + dot_nn(rows, weight_rows(weights, layer, at, KVW, COLS))
 
@@ -231,10 +232,23 @@
     backward_layers(True, h_all, kept[1:], out_ref, None, weights, None)
 
 
+def load_kernel(place, *refs):
+    sources, refs = refs[:SOURCES], refs[SOURCES:]
+    *late, sems = refs
+    weights = [None] * (LAYERS - LOADED) + late
+    layers = range(LAYERS - 1, LAYERS - 1 - LOADED, -1)
+    start_layers(layers, place, sources, weights, sems)
+    for layer in layers:
+        for at in range(0, WIDTH, CHUNK):
+            wait_rows(weights, sems, layer, at)
+
+
 def last_kernel(place, up_ref, arrived, h_all, i_all, q_all, k_all, v_all, p_all, *refs):
+    late, refs = refs[:LOADED], refs[LOADED:]
     sources, refs = refs[:SOURCES], refs[SOURCES:]
     g_all, up, sems, *weights = refs
-    start_layers(reversed(range(LAYERS)), place, sources, weights, sems)
+    weights += late
+    start_layers(reversed(range(LAYERS - LOADED)), place, sources, weights, sems)
 
     @pl.when(place[2] == 0)
     def _():
@@ -377,14 +391,25 @@
     with jax.named_scope("normed_slices"):
         rows = lax.all_to_all(n_all, PLANE, 0, 0, tiled=True).reshape(-1, CHUNK)
     arrived = across(half_up)
+    place, _ = lax.optimization_barrier((place, half_up))
+    late = call(
+        load_kernel,
+        "load_weights",
+        LOADED,
+        WEIGHTS[:LOADED],
+        (place,),
+        sources,
+        [WEIGHT_SEMS],
+    )
+    late = [pltpu.with_memory_space_constraint(block, pltpu.VMEM) for block in late]
     (grads,) = call(
         last_kernel,
         "first_backward",
         LAYERS,
         (jax.ShapeDtypeStruct((LAYERS * 4, LENGTH, 2 * HEAD), BF16),),
-        (place, up_in, arrived, h_all, *kept),
+        (place, up_in, arrived, h_all, *kept, *late),
         sources,
-        [pltpu.VMEM((LENGTH, WIDTH), BF16), WEIGHT_SEMS, *WEIGHTS],
+        [pltpu.VMEM((LENGTH, WIDTH), BF16), WEIGHT_SEMS, *WEIGHTS[LOADED:]],
         VMEM_LAST,
     )
 

time: 396 us -> 388 us (0.980)
  waiting for transfers between devices: 154 us -> 149 us
    ppermute x2, waiting for transfers between devices: 12.9 us -> 6.29 us  [across(): return lax.ppermute(block, ('yh', 'yl'), [(i, 3 - i) for i in range(4)])]
    pallas_call x3 -> x4, Pallas kernels: 57.7 us -> 57.4 us  [call(): pl.pallas_call(kernel, out_shape=out_shape, in_specs=[SM] + [VM] * (len(i...]
  transfers between devices with their start and end apart: 19 -> 19, of which waited for: 12 -> 11; matrix products, arithmetic and copies ran while one was open for 3% -> 3% of each run, Pallas kernels for 4% -> 5%
where the time goes in v8:
time: 388 us; the launch traced here: 386 us
  waiting for transfers between devices  149 us (38%)
  blocking collectives  80.2 us (21%)
  starting transfers between devices  62.8 us (16%)
  Pallas kernels  57.4 us (15%)
  local copies, waits for them, and re-layouts  15.6 us (4%)
  between operations  15.1 us (4%)
  other arithmetic  5.58 us (1%)
    ppermute x7, waiting for transfers between devices, turned(): return lax.ppermute(block, 'x', [(i, (i + distance) % 4) for i in range(4)])  76.1 us
    pallas_call x4, Pallas kernels, call(): pl.pallas_call(kernel, out_shape=out_shape, in_specs=[SM] + [VM] * (len(i...  57.4 us
    all_gather x1, waiting for transfers between devices, gather_layers(): whole = lax.all_gather(pair, ('z', 'c'), axis=0).reshape(16, 2, 2, 64, COLS)  55.5 us
    all_to_all x2, blocking collectives, sum_over(): return jnp.sum(lax.all_to_all(spread, axes, 0, 0, tiled=True), axis=0)  37.6 us
    all_to_all x1, blocking collectives, shards(): parts = lax.all_to_all(partial, 'z', 0, 0, tiled=True)  31.1 us
    ppermute x7, starting transfers between devices, turned(): return lax.ppermute(block, 'x', [(i, (i + distance) % 4) for i in range(4)])  24.9 us
    ppermute x7, starting transfers between devices, swap(): return lax.ppermute(block, axis, [(0, 1), (1, 0)])  22.2 us
    all_to_all x1, blocking collectives, shards(): cols = lax.all_to_all(grads, PLANE, 0, 0, tiled=True).reshape(-1, 2 * HEAD)  11.5 us
  transfers between devices with their start and end apart: 19, of which 11 were waited for; matrix products, arithmetic and copies ran while one was open for 3% of the time, Pallas kernels for 5%

profile of v8, /device:TPU:1, one launch (start us, length us, event | category | flops | bytes accessed | tf_op | source)
XLA Modules:
  0.0 386.5 jit_solution(4267294382258737827)
XLA Ops:
  9.0 4.0 %collective-permute-start = (bf16[64,1280]{1,0:T(8,128)(2,1)S(1)}, bf16[64,1280]{1,0:T(8,128)(2,1)S(1)}, u32[]{:S(2)}, u32[]{:S(2)}) collective-permute-start(bf16[64,1280]{1,0:T(8,128)(2,1)S(1)} %get-tuple-element.57), channel_id=1, source_target_pairs={{0,2},{2,0},{1,3},{3,1},{4,6},{6,4},{5,7},{7,5},{8,10},{10,8},{9,1... | collective-permute-start | bytes 491528 | tf_op jit(solution)/shard_map/gather_weights/ppermute | solution.py:312
  17.2 3.4 collective-permute-start.2
  29.9 6.3 %collective-permute-start.5 = (bf16[2,64,1280]{2,1,0:T(8,128)(2,1)S(1)}, bf16[2,64,1280]{2,1,0:T(8,128)(2,1)S(1)}, u32[]{:S(2)}, u32[]{:S(2)}) collective-permute-start(bf16[2,64,1280]{2,1,0:T(8,128)(2,1)S(1)} %copy-done.9), channel_id=1, source_target_pairs={{0,128},{64,192},{128,0},{192,64},{1,129},{65,193},{129,1},{193,65... | collective-permute-start | bytes 983048 | tf_op jit(solution)/shard_map/gather_weights/ppermute | solution.py:316
  43.7 5.2 %collective-permute-done.3 = bf16[2,64,384]{2,1,0:T(8,128)(2,1)S(1)} collective-permute-done((bf16[2,64,384]{2,1,0:T(8,128)(2,1)S(1)}, bf16[2,64,384]{2,1,0:T(8,128)(2,1)S(1)}, u32[]{:S(2)}, u32[]{:S(2)}) %collective-permute-start.3) | collective-permute-done | bytes 98336 | tf_op jit(solution)/shard_map/gather_weights/ppermute | solution.py:316
  49.8 55.5 %all-gather.5.cloned.1.call-done = bf16[64,64,1280]{2,1,0:T(8,128)(2,1)} async-done(((bf16[2,64,1280]{2,1,0:T(8,128)(2,1)}), bf16[64,64,1280]{2,1,0:T(8,128)(2,1)}) %all-gather.5.cloned.1.call-update) | async-done | bytes 10485776 | tf_op jit(solution)/shard_map/gather_weights/all_gather | solution.py:324
  108.5 4.2 %collective-permute-start.10 = (bf16[10,2,64,896]{3,2,1,0:T(8,128)(2,1)}, bf16[10,2,64,896]{3,2,1,0:T(8,128)(2,1)S(1)}, u32[]{:S(2)}, u32[]{:S(2)}) collective-permute-start(bf16[10,2,64,896]{3,2,1,0:T(8,128)(2,1)} %dynamic-slice_bitcast_fusion), channel_id=1, source_target_pairs={{0,192},{64,0},{128,64},{192,128},{1,193},{65,1},{129,65},{193,129... | collective-permute-start | bytes 6881288 | tf_op jit(solution)/shard_map/gather_weights/ppermute | solution.py:316
  116.2 45.8 %collective-permute-done.10.refs_6_.refs_7_ = bf16[10,2,64,896]{3,2,1,0:T(8,128)(2,1)S(1)} collective-permute-done((bf16[10,2,64,896]{3,2,1,0:T(8,128)(2,1)}, bf16[10,2,64,896]{3,2,1,0:T(8,128)(2,1)S(1)}, u32[]{:S(2)}, u32[]{:S(2)}) %collective-permute-start.10) | collective-permute-done | bytes 2293792 | tf_op jit(solution)/shard_map/gather_weights/ppermute | solution.py:316
  162.0 5.3 %collective-permute-start.12 = (bf16[6,2,64,896]{3,2,1,0:T(8,128)(2,1)S(1)}, bf16[6,2,64,896]{3,2,1,0:T(8,128)(2,1)}, u32[]{:S(2)}, u32[]{:S(2)}) collective-permute-start(bf16[6,2,64,896]{3,2,1,0:T(8,128)(2,1)S(1)} %dynamic-slice_bitcast_fusion.1), channel_id=1, source_target_pairs={{0,192},{64,0},{128,64},{192,128},{1,193},{65,1},{129,65},{193,129... | collective-permute-start | bytes 4128776 | tf_op jit(solution)/shard_map/gather_weights/ppermute | solution.py:316
  174.4 21.5 %collective-permute-done.12.refs_8_.refs_9_ = bf16[6,2,64,896]{3,2,1,0:T(8,128)(2,1)} collective-permute-done((bf16[6,2,64,896]{3,2,1,0:T(8,128)(2,1)S(1)}, bf16[6,2,64,896]{3,2,1,0:T(8,128)(2,1)}, u32[]{:S(2)}, u32[]{:S(2)}) %collective-permute-start.12) | collective-permute-done | bytes 1376288 | tf_op jit(solution)/shard_map/gather_weights/ppermute | solution.py:316
  195.8 3.8 collective-permute-start.13
  201.0 4.1 %collective-permute-start.9 = (bf16[6,2,64,896]{3,2,1,0:T(8,128)(2,1)}, bf16[6,2,64,896]{3,2,1,0:T(8,128)(2,1)}, u32[]{:S(2)}, u32[]{:S(2)}) collective-permute-start(bf16[6,2,64,896]{3,2,1,0:T(8,128)(2,1)} %collective-permute-done.8.refs_4_.refs_5_), channel_id=1, source_target_pairs={{0,1},{1,0},{2,3},{3,2},{4,5},{5,4},{6,7},{7,6},{8,9},{9,8},{10,11... | collective-permute-start | bytes 4128776 | tf_op jit(solution)/shard_map/gather_weights/ppermute | solution.py:312
  210.4 17.1 %first_forward.1 = (bf16[32,4096]{1,0:T(8,128)(2,1)S(1)}, bf16[4,16,64,1280]{3,2,1,0:T(8,128)(2,1)S(1)}, bf16[4,16,64,1280]{3,2,1,0:T(8,128)(2,1)S(1)}, bf16[4,1...) custom-call(s32[4]{0:T(128)S(1)} %pad_add_fusion.place, bf16[32,4096]{1,0:T(8,128)(2,1)S(1)} %reshape.97.h_ref, ...), custom_call_target="tpu_custom_call" | custom-call | flops 1342177280 | bytes 41943040 | tf_op jit(solution)/shard_map/first_forward/pallas_call | solution.py:294
  227.5 4.7 %collective-permute-start.14 = (bf16[32,4096]{1,0:T(8,128)(2,1)S(1)}, bf16[32,4096]{1,0:T(8,128)(2,1)S(1)}, u32[]{:S(2)}, u32[]{:S(2)}) collective-permute-start(bf16[32,4096]{1,0:T(8,128)(2,1)S(1)} %get-tuple-element.37), channel_id=1, source_target_pairs={{0,258},{2,256},{256,2},{258,0},{1,259},{3,257},{257,3},{259,1},{4... | collective-permute-start | bytes 786440 | tf_op jit(solution)/shard_map/ppermute | solution.py:320
  232.2 6.3 %collective-permute-done.14.arrived = bf16[32,4096]{1,0:T(8,128)(2,1)S(1)} collective-permute-done((bf16[32,4096]{1,0:T(8,128)(2,1)S(1)}, bf16[32,4096]{1,0:T(8,128)(2,1)S(1)}, u32[]{:S(2)}, u32[]{:S(2)}) %collective-permute-start.14) | collective-permute-done | bytes 262176 | tf_op jit(solution)/shard_map/ppermute | solution.py:320
  238.5 22.9 %second_forward_backward.1 = (bf16[32,4096]{1,0:T(8,128)(2,1)S(1)}, bf16[4,32,4096]{2,1,0:T(8,128)(2,1)}, bf16[16,32,1024]{2,1,0:T(8,128)(2,1)}, f32[4,32,128]{2...) custom-call(s32[4]{0:T(128)S(1)} %pad_add_fusion.place, ...), custom_call_target="tpu_custom_call" | custom-call | flops 2684354560 | bytes 41943040 | tf_op jit(solution)/shard_map/second_forward_backward/pallas_call | solution.py:294
  261.4 5.3 %all-to-all-start = ((bf16[16,32,1024]{2,1,0:T(8,128)(2,1)}), bf16[16,32,1024]{2,1,0:T(8,128)(2,1)S(1)}, u32[]{:S(2)}, u32[]{:S(2)}) async-start(bf16[16,32,1024]{2,1,0:T(8,128)(2,1)} %get-tuple-element.51), calls=%async_computation | async-start | bytes 2097152 | tf_op jit(solution)/shard_map/normed_slices/all_to_all | solution.py:392
  266.7 5.7 %collective-permute-start.15 = (bf16[32,4096]{1,0:T(8,128)(2,1)S(1)}, bf16[32,4096]{1,0:T(8,128)(2,1)S(1)}, u32[]{:S(2)}, u32[]{:S(2)}) collective-permute-start(bf16[32,4096]{1,0:T(8,128)(2,1)S(1)} %get-tuple-element.43), channel_id=1, source_target_pairs={{0,258},{2,256},{256,2},{258,0},{1,259},{3,257},{257,3},{259,1},{4... | collective-permute-start | bytes 786440 | tf_op jit(solution)/shard_map/ppermute | solution.py:320
  272.4 4.0 %copy-done = bf16[64,64,1280]{2,1,0:T(8,128)(2,1)S(1)} copy-done((bf16[64,64,1280]{2,1,0:T(8,128)(2,1)S(1)}, bf16[64,64,1280]{2,1,0:T(8,128)(2,1)}, u32[]{:S(2)}) %copy-start) | copy-done | bytes 10485784
  278.1 4.7 %load_weights.1.refs_0_ = bf16[4,16,64,1280]{3,2,1,0:T(8,128)(2,1)S(1)} custom-call(s32[4]{0:T(128)S(1)} %pad_add_fusion.place, bf16[16,2,2,64,1280]{4,3,2,1,0:T(8,128)(2,1)S(1)} %bitcast.56, bf16[16,2,2,64,2048]{4,3,2,1,0:T(8,128)(2,1)} %bitcast.58, bf16[10,2,64,896]{3,2,1,0:T(8,128)(2,1)} %collective-permute-done.6.refs_2_.refs_3_, ...), custom_call_target="tpu_custom_call" | custom-call | flops 335544320 | bytes 41943040 | tf_op jit(solution)/shard_map/load_weights/pallas_call | solution.py:294
  282.9 12.7 %first_backward.1 = bf16[16,32,256]{2,1,0:T(8,128)(2,1)S(1)} custom-call(s32[4]{0:T(128)S(1)} %pad_add_fusion.place, bf16[32,4096]{1,0:T(8,128)(2,1)S(1)} %collective-permute-done.1.up_ref, bf16[32,4096]{1,0:T(8,128)(2,1)S(1)} %collective-permute-done.15.arrived, bf16[4,32,4096]{2,1,0:T(8,128)(2,1)S(1)} %copy-done.3, f32[4,32,128]{2,1,0:T(8,128)S(1)} %copy-done.6, ...), custom_call_target="tpu_custom_call" | custom-call | flops 1342177280 | bytes 41943040 | tf_op jit(solution)/shard_map/first_backward/pallas_call | solution.py:294
  295.6 11.5 %all_to_all.25 = bf16[16,32,256]{2,1,0:T(8,128)(2,1)S(1)} all-to-all(bf16[16,32,256]{2,1,0:T(8,128)(2,1)S(1)} %first_backward.1), channel_id=1, replica_groups=mesh['yh'=2,'x'=4,'z'=16,'yl'=2,'c'=2] {'x','yl','c'}, dimensions={0} | all-to-all | bytes 524288 | tf_op jit(solution)/shard_map/gather_grads/all_to_all | solution.py:418
  307.6 31.1 %all_to_all.26 = bf16[16,64,256]{2,1,0:T(8,128)(2,1)S(1)} all-to-all(bf16[16,64,256]{2,1,0:T(8,128)(2,1)S(1)} %bitcast.63), channel_id=1, replica_groups=mesh['yh'=2,'x'=4,'z'=16,'yl'=2,'c'=2] {'z'}, dimensions={0} | all-to-all | bytes 1048576 | tf_op jit(solution)/shard_map/sum_grads/all_to_all | solution.py:422
  340.1 24.2 %all_to_all.27 = f32[16,8,128]{2,1,0:T(8,128)S(1)} all-to-all(f32[16,8,128]{2,1,0:T(8,128)S(1)} %broadcast_in_dim.16), channel_id=1, replica_groups=mesh['yh'=2,'x'=4,'z'=16,'yl'=2,'c'=2] {'z'}, dimensions={0} | all-to-all | bytes 131072 | tf_op jit(solution)/shard_map/clip/all_to_all | solution.py:342
  364.3 13.4 %all_to_all.28 = f32[32,8,128]{2,1,0:T(8,128)S(1)} all-to-all(f32[32,8,128]{2,1,0:T(8,128)S(1)} %broadcast_in_dim.17), channel_id=1, replica_groups=mesh['yh'=2,'x'=4,'z'=16,'yl'=2,'c'=2] {'yh','x','yl','c'}, dimensions={0} | all-to-all | bytes 262144 | tf_op jit(solution)/shard_map/clip/all_to_all | solution.py:342
  (79 shorter events, 48.8 us)
Async XLA Ops:
  7.2 98.1 %all-gather.5.cloned.1.call-start = ((), (), s32[]{:S(2)}) async-start(), calls=%async_computation.5 | async-start | bytes 10813440 | tf_op jit(solution)/shard_map/gather_weights/all_gather | solution.py:324
  9.0 6.7 %collective-permute-start = (bf16[64,1280]{1,0:T(8,128)(2,1)S(1)}, bf16[64,1280]{1,0:T(8,128)(2,1)S(1)}, u32[]{:S(2)}, u32[]{:S(2)}) collective-permute-start(bf16[64,1280]{1,0:T(8,128)(2,1)S(1)} %get-tuple-element.57), channel_id=1, source_target_pairs={{0,2},{2,0},{1,3},{3,1},{4,6},{6,4},{5,7},{7,5},{8,10},{10,8},{9,1... | collective-permute-start | bytes 491528 | tf_op jit(solution)/shard_map/gather_weights/ppermute | solution.py:312
  16.5 193.9 %all-gather.7.cloned.1.call-start = ((), (), s32[]{:S(2)}) async-start(), calls=%async_computation.6 | async-start | bytes 17301504 | tf_op jit(solution)/shard_map/gather_weights/all_gather | solution.py:327
  17.2 8.7 %collective-permute-start.2 = (s32[32]{0:T(128)S(1)}, s32[32]{0:T(128)S(1)}, u32[]{:S(2)}, u32[]{:S(2)}) collective-permute-start(s32[32]{0:T(128)S(1)} %fusion.5), channel_id=1, source_target_pairs={{0,2},{2,0},{1,3},{3,1},{4,6},{6,4},{5,7},{7,5},{8,10},{10,8},{9,1... | collective-permute-start | bytes 392 | tf_op jit(solution)/shard_map/ppermute | solution.py:312
  22.2 7.7 %copy-start.9 = (bf16[2,64,1280]{2,1,0:T(8,128)(2,1)S(1)}, bf16[2,64,1280]{2,1,0:T(8,128)(2,1)}, u32[]{:S(2)}) copy-start(bf16[2,64,1280]{2,1,0:T(8,128)(2,1)} %pad_maximum_fusion.1) | copy-start | bytes 983044
  22.8 7.1 %collective-permute-start.1 = (bf16[32,4096]{1,0:T(8,128)(2,1)S(1)}, bf16[32,4096]{1,0:T(8,128)(2,1)S(1)}, u32[]{:S(2)}, u32[]{:S(2)}) collective-permute-start(bf16[32,4096]{1,0:T(8,128)(2,1)S(1)} %reshape.99), channel_id=1, source_target_pairs={{0,2},{2,0},{1,3},{3,1},{4,6},{6,4},{5,7},{7,5},{8,10},{10,8},{9,1... | collective-permute-start | bytes 786440 | tf_op jit(solution)/shard_map/ppermute | solution.py:312
  29.9 19.0 %collective-permute-start.5 = (bf16[2,64,1280]{2,1,0:T(8,128)(2,1)S(1)}, bf16[2,64,1280]{2,1,0:T(8,128)(2,1)S(1)}, u32[]{:S(2)}, u32[]{:S(2)}) collective-permute-start(bf16[2,64,1280]{2,1,0:T(8,128)(2,1)S(1)} %copy-done.9), channel_id=1, source_target_pairs={{0,128},{64,192},{128,0},{192,64},{1,129},{65,193},{129,1},{193,65... | collective-permute-start | bytes 983048 | tf_op jit(solution)/shard_map/gather_weights/ppermute | solution.py:316
  36.2 7.5 %collective-permute-start.4 = (bf16[2,64,384]{2,1,0:T(8,128)(2,1)S(1)}, bf16[2,64,384]{2,1,0:T(8,128)(2,1)S(1)}, u32[]{:S(2)}, u32[]{:S(2)}) collective-permute-start(bf16[2,64,384]{2,1,0:T(8,128)(2,1)S(1)} %slice.34), channel_id=1, source_target_pairs={{0,192},{64,0},{128,64},{192,128},{1,193},{65,1},{129,65},{193,129... | collective-permute-start | bytes 294920 | tf_op jit(solution)/shard_map/gather_weights/ppermute | solution.py:316
  39.0 9.9 %collective-permute-start.3 = (bf16[2,64,384]{2,1,0:T(8,128)(2,1)S(1)}, bf16[2,64,384]{2,1,0:T(8,128)(2,1)S(1)}, u32[]{:S(2)}, u32[]{:S(2)}) collective-permute-start(bf16[2,64,384]{2,1,0:T(8,128)(2,1)S(1)} %slice.34), channel_id=1, source_target_pairs={{0,64},{64,128},{128,192},{192,0},{1,65},{65,129},{129,193},{193,1... | collective-permute-start | bytes 294920 | tf_op jit(solution)/shard_map/gather_weights/ppermute | solution.py:316
  108.5 53.5 %collective-permute-start.10 = (bf16[10,2,64,896]{3,2,1,0:T(8,128)(2,1)}, bf16[10,2,64,896]{3,2,1,0:T(8,128)(2,1)S(1)}, u32[]{:S(2)}, u32[]{:S(2)}) collective-permute-start(bf16[10,2,64,896]{3,2,1,0:T(8,128)(2,1)} %dynamic-slice_bitcast_fusion), channel_id=1, source_target_pairs={{0,192},{64,0},{128,64},{192,128},{1,193},{65,1},{129,65},{193,129... | collective-permute-start | bytes 6881288 | tf_op jit(solution)/shard_map/gather_weights/ppermute | solution.py:316
  112.7 54.6 %collective-permute-start.6 = (bf16[10,2,64,896]{3,2,1,0:T(8,128)(2,1)}, bf16[10,2,64,896]{3,2,1,0:T(8,128)(2,1)}, u32[]{:S(2)}, u32[]{:S(2)}) collective-permute-start(bf16[10,2,64,896]{3,2,1,0:T(8,128)(2,1)} %dynamic-slice_bitcast_fusion), channel_id=1, source_target_pairs={{0,64},{64,128},{128,192},{192,0},{1,65},{65,129},{129,193},{193,1... | collective-permute-start | bytes 6881288 | tf_op jit(solution)/shard_map/gather_weights/ppermute | solution.py:316
  162.0 48.4 %copy-start.1 = (bf16[10,2,64,896]{3,2,1,0:T(8,128)(2,1)}, bf16[10,2,64,896]{3,2,1,0:T(8,128)(2,1)S(1)}, u32[]{:S(2)}) copy-start(bf16[10,2,64,896]{3,2,1,0:T(8,128)(2,1)S(1)} %collective-permute-done.10.refs_6_.refs_7_) | copy-start | bytes 6881284
  162.0 33.8 %collective-permute-start.12 = (bf16[6,2,64,896]{3,2,1,0:T(8,128)(2,1)S(1)}, bf16[6,2,64,896]{3,2,1,0:T(8,128)(2,1)}, u32[]{:S(2)}, u32[]{:S(2)}) collective-permute-start(bf16[6,2,64,896]{3,2,1,0:T(8,128)(2,1)S(1)} %dynamic-slice_bitcast_fusion.1), channel_id=1, source_target_pairs={{0,192},{64,0},{128,64},{192,128},{1,193},{65,1},{129,65},{193,129... | collective-permute-start | bytes 4128776 | tf_op jit(solution)/shard_map/gather_weights/ppermute | solution.py:316
  167.3 33.6 %collective-permute-start.8 = (bf16[6,2,64,896]{3,2,1,0:T(8,128)(2,1)S(1)}, bf16[6,2,64,896]{3,2,1,0:T(8,128)(2,1)}, u32[]{:S(2)}, u32[]{:S(2)}) collective-permute-start(bf16[6,2,64,896]{3,2,1,0:T(8,128)(2,1)S(1)} %dynamic-slice_bitcast_fusion.1), channel_id=1, source_target_pairs={{0,64},{64,128},{128,192},{192,0},{1,65},{65,129},{129,193},{193,1... | collective-permute-start | bytes 4128776 | tf_op jit(solution)/shard_map/gather_weights/ppermute | solution.py:316
  169.3 35.9 %collective-permute-start.11 = (bf16[10,2,64,896]{3,2,1,0:T(8,128)(2,1)S(1)}, bf16[10,2,64,896]{3,2,1,0:T(8,128)(2,1)}, u32[]{:S(2)}, u32[]{:S(2)}) collective-permute-start(bf16[10,2,64,896]{3,2,1,0:T(8,128)(2,1)S(1)} %collective-permute-done.10.refs_6_.refs_7_), channel_id=1, source_target_pairs={{0,1},{1,0},{2,3},{3,2},{4,5},{5,4},{6,7},{7,6},{8,9},{9,8},{10,11... | collective-permute-start | bytes 6881288 | tf_op jit(solution)/shard_map/gather_weights/ppermute | solution.py:312
  172.4 32.7 %collective-permute-start.7 = (bf16[10,2,64,896]{3,2,1,0:T(8,128)(2,1)}, bf16[10,2,64,896]{3,2,1,0:T(8,128)(2,1)}, u32[]{:S(2)}, u32[]{:S(2)}) collective-permute-start(bf16[10,2,64,896]{3,2,1,0:T(8,128)(2,1)} %collective-permute-done.6.refs_2_.refs_3_), channel_id=1, source_target_pairs={{0,1},{1,0},{2,3},{3,2},{4,5},{5,4},{6,7},{7,6},{8,9},{9,8},{10,11... | collective-permute-start | bytes 6881288 | tf_op jit(solution)/shard_map/gather_weights/ppermute | solution.py:312
  195.8 9.3 %collective-permute-start.13 = (bf16[6,2,64,896]{3,2,1,0:T(8,128)(2,1)}, bf16[6,2,64,896]{3,2,1,0:T(8,128)(2,1)}, u32[]{:S(2)}, u32[]{:S(2)}) collective-permute-start(bf16[6,2,64,896]{3,2,1,0:T(8,128)(2,1)} %collective-permute-done.12.refs_8_.refs_9_), channel_id=1, source_target_pairs={{0,1},{1,0},{2,3},{3,2},{4,5},{5,4},{6,7},{7,6},{8,9},{9,8},{10,11... | collective-permute-start | bytes 4128776 | tf_op jit(solution)/shard_map/gather_weights/ppermute | solution.py:312
  201.0 7.1 %collective-permute-start.9 = (bf16[6,2,64,896]{3,2,1,0:T(8,128)(2,1)}, bf16[6,2,64,896]{3,2,1,0:T(8,128)(2,1)}, u32[]{:S(2)}, u32[]{:S(2)}) collective-permute-start(bf16[6,2,64,896]{3,2,1,0:T(8,128)(2,1)} %collective-permute-done.8.refs_4_.refs_5_), channel_id=1, source_target_pairs={{0,1},{1,0},{2,3},{3,2},{4,5},{5,4},{6,7},{7,6},{8,9},{9,8},{10,11... | collective-permute-start | bytes 4128776 | tf_op jit(solution)/shard_map/gather_weights/ppermute | solution.py:312
  227.5 11.0 %collective-permute-start.14 = (bf16[32,4096]{1,0:T(8,128)(2,1)S(1)}, bf16[32,4096]{1,0:T(8,128)(2,1)S(1)}, u32[]{:S(2)}, u32[]{:S(2)}) collective-permute-start(bf16[32,4096]{1,0:T(8,128)(2,1)S(1)} %get-tuple-element.37), channel_id=1, source_target_pairs={{0,258},{2,256},{256,2},{258,0},{1,259},{3,257},{257,3},{259,1},{4... | collective-permute-start | bytes 786440 | tf_op jit(solution)/shard_map/ppermute | solution.py:320
  261.4 34.1 %all-to-all-start = ((bf16[16,32,1024]{2,1,0:T(8,128)(2,1)}), bf16[16,32,1024]{2,1,0:T(8,128)(2,1)S(1)}, u32[]{:S(2)}, u32[]{:S(2)}) async-start(bf16[16,32,1024]{2,1,0:T(8,128)(2,1)} %get-tuple-element.51), calls=%async_computation | async-start | bytes 2097152 | tf_op jit(solution)/shard_map/normed_slices/all_to_all | solution.py:392
  266.7 16.1 %collective-permute-start.15 = (bf16[32,4096]{1,0:T(8,128)(2,1)S(1)}, bf16[32,4096]{1,0:T(8,128)(2,1)S(1)}, u32[]{:S(2)}, u32[]{:S(2)}) collective-permute-start(bf16[32,4096]{1,0:T(8,128)(2,1)S(1)} %get-tuple-element.43), channel_id=1, source_target_pairs={{0,258},{2,256},{256,2},{258,0},{1,259},{3,257},{257,3},{259,1},{4... | collective-permute-start | bytes 786440 | tf_op jit(solution)/shard_map/ppermute | solution.py:320
  307.1 71.8 %copy-start.10 = (f32[1,2,64,128]{3,2,1,0:T(8,128)S(1)}, f32[1,2,64,128]{3,2,1,0:T(8,128)}, u32[]{:S(2)}) copy-start(f32[1,2,64,128]{3,2,1,0:T(8,128)} %param.13) | copy-start | bytes 196612
  307.1 71.8 %copy-start.11 = (f32[1,2,64,128]{3,2,1,0:T(8,128)S(1)}, f32[1,2,64,128]{3,2,1,0:T(8,128)}, u32[]{:S(2)}) copy-start(f32[1,2,64,128]{3,2,1,0:T(8,128)} %param.15) | copy-start | bytes 196612
  307.1 71.8 %copy-start.12 = (f32[1,2,64,128]{3,2,1,0:T(8,128)S(1)}, f32[1,2,64,128]{3,2,1,0:T(8,128)}, u32[]{:S(2)}) copy-start(f32[1,2,64,128]{3,2,1,0:T(8,128)} %param.14) | copy-start | bytes 196612
  (8 other events, 34.5 us)
Sparse Core Ops, SparseCore 0:
  16.6 88.6 all-gather.4
  107.4 102.9 all-gather.6

commit v9 on v8

--- a/solution.py
+++ b/solution.py
@@ -15,9 +15,10 @@
 LEARN_RATE = 0.001
 CLIP_NORM = 1.0
 
-FINE = {"yh": 2, "x": 4, "z": 16, "yl": 2, "c": 2}
-DP = ("z", "yl", "c")
-PLANE = ("x", "yl", "c")
+FINE = {"yh": 2, "x": 4, "zh": 8, "zl": 2, "yl": 2, "c": 2}
+Z = ("zh", "zl")
+DP = Z + ("yl", "c")
+NEAR = ("x", "zl", "yl", "c")
 LAYERS = 4
 LENGTH = 32
 WIDTH = 4096
@@ -143,7 +144,9 @@
             for at in range(0, WIDTH, CHUNK):
                 signal = h_all[layer, :, at : at + CHUNK].astype(F32)
                 core, side = divmod(at // CHUNK, 2)
-                n_all[layer * 4 + side * 2 + core] = (signal * inverse).astype(BF16)
+                normed = (signal * inverse).astype(BF16)
+                for pair in range(2):
+                    n_all[layer * 8 + pair * 4 + side * 2 + core] = normed
         if out_ref is None and layer + 1 == LAYERS:
             return
         context = unstack_heads(dot_nn(probs.astype(BF16), values).astype(BF16))
@@ -180,8 +183,8 @@
         grad_values = dot_tn(probs.astype(BF16), grad_context).astype(BF16)
         if g_all is not None:
             for copy in range(4):
-                g_all[layer * 4 + copy, :, :HEAD] = grad_keys
-                g_all[layer * 4 + copy, :, HEAD:] = grad_values
+                g_all[layer * 8 + copy] = grad_keys
+                g_all[layer * 8 + 4 + copy] = grad_values
         if layer == 0 and not need_up:
             return
         grad_query = dot_nn(grad_scores, keys).astype(BF16)
@@ -271,7 +274,7 @@
 ROWS_ALL = pltpu.VMEM((LAYERS, LENGTH, WIDTH), BF16)
 STATE_SHAPES = (
     pltpu.HBM((LAYERS, LENGTH, WIDTH), BF16),
-    pltpu.HBM((LAYERS * 4, LENGTH, CHUNK), BF16),
+    pltpu.HBM((LAYERS * 8, LENGTH, CHUNK), BF16),
     pltpu.HBM((LAYERS, LENGTH, HEAD), F32),
     pltpu.HBM((LAYERS, LENGTH * HEADS, HEAD), BF16),
     pltpu.HBM((LAYERS, LENGTH, HEAD), BF16),
@@ -321,10 +324,10 @@
 
 
 def gather_layers(pair, rest, c):
-    whole = lax.all_gather(pair, ("z", "c"), axis=0).reshape(16, 2, 2, 64, COLS)
+    whole = lax.all_gather(pair, Z + ("c",), axis=0).reshape(16, 2, 2, 64, COLS)
     edge = rest[:, :, ALONG_X:]
     rest = jnp.concatenate([turned(edge, 1), turned(edge, 3), turned(rest, 2)], axis=2)
-    rest = lax.all_gather(rest, ("z", "c"), axis=0).reshape(16, 2, 2, 64, -1)
+    rest = lax.all_gather(rest, Z + ("c",), axis=0).reshape(16, 2, 2, 64, -1)
     share = lax.dynamic_slice(whole, (0, c, 0, 0, 0), (16, 1, 2, 64, ALONG_X))[:, 0]
     early, late = share[:EARLY], share[EARLY:]
     near, far = turned(early, 1), turned(early, 3)
@@ -345,7 +348,7 @@
 def shards(
     inputs, out_grad, doc_ids, query_weight, out_weight, master, first_moment, second_moment
 ):
-    yh, x, yl, c = (lax.axis_index(name) for name in ("yh", "x", "yl", "c"))
+    yh, x, zl, yl, c = (lax.axis_index(name) for name in ("yh", "x", "zl", "yl", "c"))
     own = jnp.concatenate(
         [
             query_weight[0],
@@ -389,7 +392,7 @@
         [],
     )
     with jax.named_scope("normed_slices"):
-        rows = lax.all_to_all(n_all, PLANE, 0, 0, tiled=True).reshape(-1, CHUNK)
+        rows = lax.all_to_all(n_all, NEAR, 0, 0, tiled=True).reshape(-1, CHUNK)
     arrived = across(half_up)
     place, _ = lax.optimization_barrier((place, half_up))
     late = call(
@@ -406,7 +409,7 @@
         last_kernel,
         "first_backward",
         LAYERS,
-        (jax.ShapeDtypeStruct((LAYERS * 4, LENGTH, 2 * HEAD), BF16),),
+        (jax.ShapeDtypeStruct((LAYERS * 8, LENGTH, HEAD), BF16),),
         (place, up_in, arrived, h_all, *kept, *late),
         sources,
         [pltpu.VMEM((LENGTH, WIDTH), BF16), WEIGHT_SEMS, *WEIGHTS[LOADED:]],
@@ -415,17 +418,19 @@
 
     with jax.named_scope("gather_grads"):
         grads, rows = lax.optimization_barrier((grads, rows))
-        cols = lax.all_to_all(grads, PLANE, 0, 0, tiled=True).reshape(-1, 2 * HEAD)
+        cols = lax.all_to_all(grads, NEAR, 0, 0, tiled=True).reshape(-1, HEAD)
 
     with jax.named_scope("sum_grads"):
-        partial = dot_tn(rows, cols).astype(BF16).reshape(16, 64, 2 * HEAD)
-        parts = lax.all_to_all(partial, "z", 0, 0, tiled=True)
-        grad = jnp.sum(parts.astype(F32), axis=0)
-        grad = jnp.stack([grad[:, :HEAD], grad[:, HEAD:]])
+        partial = dot_tn(rows, cols).astype(BF16).reshape(8, 128, HEAD)
+        parts = lax.all_to_all(partial, "zh", 0, 0, tiled=True)
+        both = jnp.sum(parts.astype(F32), axis=0)
+        mine = lax.dynamic_slice_in_dim(both, zl * 64, 64, 0)
+        other = swap(lax.dynamic_slice_in_dim(both, (1 - zl) * 64, 64, 0), "zl")
+        grad = jnp.stack([jnp.where(zl == 0, mine, other), jnp.where(zl == 0, other, mine)])
 
     with jax.named_scope("clip"):
-        total_sq = sum_over(jnp.sum(grad * grad), "z", 16)
-        total_sq = sum_over(total_sq, ("yh",) + PLANE, 32)
+        total_sq = sum_over(jnp.sum(both * both), Z, 16)
+        total_sq = sum_over(total_sq, ("yh", "x", "yl", "c"), 32)
         factor = jnp.minimum(1.0, CLIP_NORM / jnp.sqrt(total_sq[0, 0]))
     clipped = grad * factor
     first_new = BETA_FIRST * first_moment[0] + (1.0 - BETA_FIRST) * clipped

time: 388 us -> 384 us (0.990)
  blocking collectives: 80.2 us -> 43.1 us
  starting transfers between devices: 62.8 us -> 78.5 us
  waiting for transfers between devices: 149 us -> 164 us
    all_to_all x4 -> x2, blocking collectives: 80.2 us -> 43.1 us  [the longest x1 29.3 us: shards(): parts = lax.all_to_all(partial, 'zh', 0, 0, tiled=True)]
    all_to_all x1 -> x3, waiting for transfers between devices: 0.01 us -> 16 us  [the longest x2 16 us: sum_over(): return jnp.sum(lax.all_to_all(spread, axes, 0, 0, tiled=True), axis=0)]
    all_to_all x1 -> x3, starting transfers between devices: 5.3 us -> 16.4 us  [the longest x2 10.9 us: sum_over(): return jnp.sum(lax.all_to_all(spread, axes, 0, 0, tiled=True), axis=0)]
    ppermute x7, waiting for transfers between devices: 76.1 us -> 71.3 us  [turned(): return lax.ppermute(block, 'x', [(i, (i + distance) % 4) for i in range(4)])]
    ppermute x7 -> x8, starting transfers between devices: 22.2 us -> 25.5 us  [swap(): return lax.ppermute(block, axis, [(0, 1), (1, 0)])]
    ppermute x7 -> x8, waiting for transfers between devices: 8.98 us -> 8.98 us  [swap(): return lax.ppermute(block, axis, [(0, 1), (1, 0)])]
  transfers between devices with their start and end apart: 19 -> 22, of which waited for: 11 -> 13; matrix products, arithmetic and copies ran while one was open for 3% -> 3% of each run, Pallas kernels for 5% -> 5%
where the time goes in v9:
time: 384 us; the launch traced here: 383 us
  waiting for transfers between devices  164 us (43%)
  starting transfers between devices  78.5 us (20%)
  Pallas kernels  57.4 us (15%)
  blocking collectives  43.1 us (11%)
  local copies, waits for them, and re-layouts  16.9 us (4%)
  between operations  15.2 us (4%)
  other arithmetic  5.58 us (1%)
    ppermute x7, waiting for transfers between devices, turned(): return lax.ppermute(block, 'x', [(i, (i + distance) % 4) for i in range(4)])  71.3 us
    all_gather x1, waiting for transfers between devices, gather_layers(): whole = lax.all_gather(pair, Z + ('c',), axis=0).reshape(16, 2, 2, 64, COLS)  59.2 us
    pallas_call x4, Pallas kernels, call(): pl.pallas_call(kernel, out_shape=out_shape, in_specs=[SM] + [VM] * (len(i...  57.4 us
    all_to_all x1, blocking collectives, shards(): parts = lax.all_to_all(partial, 'zh', 0, 0, tiled=True)  29.3 us
    ppermute x7, starting transfers between devices, turned(): return lax.ppermute(block, 'x', [(i, (i + distance) % 4) for i in range(4)])  26.1 us
    ppermute x8, starting transfers between devices, swap(): return lax.ppermute(block, axis, [(0, 1), (1, 0)])  25.5 us
    all_to_all x2, waiting for transfers between devices, sum_over(): return jnp.sum(lax.all_to_all(spread, axes, 0, 0, tiled=True), axis=0)  16 us
    all_to_all x1, blocking collectives, shards(): cols = lax.all_to_all(grads, NEAR, 0, 0, tiled=True).reshape(-1, HEAD)  13.8 us
  transfers between devices with their start and end apart: 22, of which 13 were waited for; matrix products, arithmetic and copies ran while one was open for 3% of the time, Pallas kernels for 5%

profile of v9, /device:TPU:1, one launch (start us, length us, event | category | flops | bytes accessed | tf_op | source)
XLA Modules:
  0.0 382.8 jit_solution(4886667021056592222)
XLA Ops:
  9.0 4.0 %collective-permute-start = (bf16[64,1280]{1,0:T(8,128)(2,1)S(1)}, bf16[64,1280]{1,0:T(8,128)(2,1)S(1)}, u32[]{:S(2)}, u32[]{:S(2)}) collective-permute-start(bf16[64,1280]{1,0:T(8,128)(2,1)S(1)} %get-tuple-element.57), channel_id=1, source_target_pairs={{0,2},{2,0},{1,3},{3,1},{4,6},{6,4},{5,7},{7,5},{8,10},{10,8},{9,1... | collective-permute-start | bytes 491528 | tf_op jit(solution)/shard_map/gather_weights/ppermute | solution.py:315
  29.9 6.3 %collective-permute-start.5 = (bf16[2,64,1280]{2,1,0:T(8,128)(2,1)S(1)}, bf16[2,64,1280]{2,1,0:T(8,128)(2,1)S(1)}, u32[]{:S(2)}, u32[]{:S(2)}) collective-permute-start(bf16[2,64,1280]{2,1,0:T(8,128)(2,1)S(1)} %copy-done.9), channel_id=1, source_target_pairs={{0,128},{64,192},{128,0},{192,64},{1,129},{65,193},{129,1},{193,65... | collective-permute-start | bytes 983048 | tf_op jit(solution)/shard_map/gather_weights/ppermute | solution.py:319
  38.5 4.3 %collective-permute-start.4 = (bf16[2,64,384]{2,1,0:T(8,128)(2,1)S(1)}, bf16[2,64,384]{2,1,0:T(8,128)(2,1)S(1)}, u32[]{:S(2)}, u32[]{:S(2)}) collective-permute-start(bf16[2,64,384]{2,1,0:T(8,128)(2,1)S(1)} %slice.28), channel_id=1, source_target_pairs={{0,192},{64,0},{128,64},{192,128},{1,193},{65,1},{129,65},{193,129... | collective-permute-start | bytes 294920 | tf_op jit(solution)/shard_map/gather_weights/ppermute | solution.py:319
  46.2 59.2 %all-gather.5.cloned.1.call-done = bf16[64,64,1280]{2,1,0:T(8,128)(2,1)} async-done(((bf16[2,64,1280]{2,1,0:T(8,128)(2,1)}), bf16[64,64,1280]{2,1,0:T(8,128)(2,1)}) %all-gather.5.cloned.1.call-update) | async-done | bytes 10485776 | tf_op jit(solution)/shard_map/gather_weights/all_gather | solution.py:327
  108.8 4.2 %collective-permute-start.10 = (bf16[10,2,64,896]{3,2,1,0:T(8,128)(2,1)}, bf16[10,2,64,896]{3,2,1,0:T(8,128)(2,1)S(1)}, u32[]{:S(2)}, u32[]{:S(2)}) collective-permute-start(bf16[10,2,64,896]{3,2,1,0:T(8,128)(2,1)} %dynamic-slice_bitcast_fusion), channel_id=1, source_target_pairs={{0,192},{64,0},{128,64},{192,128},{1,193},{65,1},{129,65},{193,129... | collective-permute-start | bytes 6881288 | tf_op jit(solution)/shard_map/gather_weights/ppermute | solution.py:319
  116.4 45.8 %collective-permute-done.10.refs_6_.refs_7_ = bf16[10,2,64,896]{3,2,1,0:T(8,128)(2,1)S(1)} collective-permute-done((bf16[10,2,64,896]{3,2,1,0:T(8,128)(2,1)}, bf16[10,2,64,896]{3,2,1,0:T(8,128)(2,1)S(1)}, u32[]{:S(2)}, u32[]{:S(2)}) %collective-permute-start.10) | collective-permute-done | bytes 2293792 | tf_op jit(solution)/shard_map/gather_weights/ppermute | solution.py:319
  162.2 5.3 %collective-permute-start.12 = (bf16[6,2,64,896]{3,2,1,0:T(8,128)(2,1)S(1)}, bf16[6,2,64,896]{3,2,1,0:T(8,128)(2,1)}, u32[]{:S(2)}, u32[]{:S(2)}) collective-permute-start(bf16[6,2,64,896]{3,2,1,0:T(8,128)(2,1)S(1)} %dynamic-slice_bitcast_fusion.1), channel_id=1, source_target_pairs={{0,192},{64,0},{128,64},{192,128},{1,193},{65,1},{129,65},{193,129... | collective-permute-start | bytes 4128776 | tf_op jit(solution)/shard_map/gather_weights/ppermute | solution.py:319
  174.6 21.4 %collective-permute-done.12.refs_8_.refs_9_ = bf16[6,2,64,896]{3,2,1,0:T(8,128)(2,1)} collective-permute-done((bf16[6,2,64,896]{3,2,1,0:T(8,128)(2,1)S(1)}, bf16[6,2,64,896]{3,2,1,0:T(8,128)(2,1)}, u32[]{:S(2)}, u32[]{:S(2)}) %collective-permute-start.12) | collective-permute-done | bytes 1376288 | tf_op jit(solution)/shard_map/gather_weights/ppermute | solution.py:319
  201.2 4.1 %collective-permute-start.9 = (bf16[6,2,64,896]{3,2,1,0:T(8,128)(2,1)}, bf16[6,2,64,896]{3,2,1,0:T(8,128)(2,1)}, u32[]{:S(2)}, u32[]{:S(2)}) collective-permute-start(bf16[6,2,64,896]{3,2,1,0:T(8,128)(2,1)} %collective-permute-done.8.refs_4_.refs_5_), channel_id=1, source_target_pairs={{0,1},{1,0},{2,3},{3,2},{4,5},{5,4},{6,7},{7,6},{8,9},{9,8},{10,11... | collective-permute-start | bytes 4128776 | tf_op jit(solution)/shard_map/gather_weights/ppermute | solution.py:315
  210.3 17.1 %first_forward.1 = (bf16[32,4096]{1,0:T(8,128)(2,1)S(1)}, bf16[4,16,64,1280]{3,2,1,0:T(8,128)(2,1)S(1)}, bf16[4,16,64,1280]{3,2,1,0:T(8,128)(2,1)S(1)}, bf16[4,1...) custom-call(s32[4]{0:T(128)S(1)} %pad_add_fusion.place, bf16[32,4096]{1,0:T(8,128)(2,1)S(1)} %reshape.97.h_ref, ...), custom_call_target="tpu_custom_call" | custom-call | flops 1342177280 | bytes 41943040 | tf_op jit(solution)/shard_map/first_forward/pallas_call | solution.py:297
  227.4 4.7 %collective-permute-start.14 = (bf16[32,4096]{1,0:T(8,128)(2,1)S(1)}, bf16[32,4096]{1,0:T(8,128)(2,1)S(1)}, u32[]{:S(2)}, u32[]{:S(2)}) collective-permute-start(bf16[32,4096]{1,0:T(8,128)(2,1)S(1)} %get-tuple-element.37), channel_id=1, source_target_pairs={{0,258},{2,256},{256,2},{258,0},{1,259},{3,257},{257,3},{259,1},{4... | collective-permute-start | bytes 786440 | tf_op jit(solution)/shard_map/ppermute | solution.py:323
  232.1 6.3 %collective-permute-done.14.arrived = bf16[32,4096]{1,0:T(8,128)(2,1)S(1)} collective-permute-done((bf16[32,4096]{1,0:T(8,128)(2,1)S(1)}, bf16[32,4096]{1,0:T(8,128)(2,1)S(1)}, u32[]{:S(2)}, u32[]{:S(2)}) %collective-permute-start.14) | collective-permute-done | bytes 262176 | tf_op jit(solution)/shard_map/ppermute | solution.py:323
  238.3 22.9 %second_forward_backward.1 = (bf16[32,4096]{1,0:T(8,128)(2,1)S(1)}, bf16[4,32,4096]{2,1,0:T(8,128)(2,1)}, bf16[32,32,1024]{2,1,0:T(8,128)(2,1)}, f32[4,32,128]{2...) custom-call(s32[4]{0:T(128)S(1)} %pad_add_fusion.place, ...), custom_call_target="tpu_custom_call" | custom-call | flops 2684354560 | bytes 41943040 | tf_op jit(solution)/shard_map/second_forward_backward/pallas_call | solution.py:297
  261.3 5.5 %all-to-all-start = ((bf16[32,32,1024]{2,1,0:T(8,128)(2,1)}), bf16[32,32,1024]{2,1,0:T(8,128)(2,1)}, u32[]{:S(2)}, u32[]{:S(2)}) async-start(bf16[32,32,1024]{2,1,0:T(8,128)(2,1)} %get-tuple-element.51), calls=%async_computation | async-start | bytes 4194304 | tf_op jit(solution)/shard_map/normed_slices/all_to_all | solution.py:395
  266.8 5.7 %collective-permute-start.15 = (bf16[32,4096]{1,0:T(8,128)(2,1)S(1)}, bf16[32,4096]{1,0:T(8,128)(2,1)S(1)}, u32[]{:S(2)}, u32[]{:S(2)}) collective-permute-start(bf16[32,4096]{1,0:T(8,128)(2,1)S(1)} %get-tuple-element.43), channel_id=1, source_target_pairs={{0,258},{2,256},{256,2},{258,0},{1,259},{3,257},{257,3},{259,1},{4... | collective-permute-start | bytes 786440 | tf_op jit(solution)/shard_map/ppermute | solution.py:323
  272.5 4.0 %copy-done = bf16[64,64,1280]{2,1,0:T(8,128)(2,1)S(1)} copy-done((bf16[64,64,1280]{2,1,0:T(8,128)(2,1)S(1)}, bf16[64,64,1280]{2,1,0:T(8,128)(2,1)}, u32[]{:S(2)}) %copy-start) | copy-done | bytes 10485784
  278.1 4.7 %load_weights.1.refs_0_ = bf16[4,16,64,1280]{3,2,1,0:T(8,128)(2,1)S(1)} custom-call(s32[4]{0:T(128)S(1)} %pad_add_fusion.place, bf16[16,2,2,64,1280]{4,3,2,1,0:T(8,128)(2,1)S(1)} %bitcast.52, bf16[16,2,2,64,2048]{4,3,2,1,0:T(8,128)(2,1)} %bitcast.54, bf16[10,2,64,896]{3,2,1,0:T(8,128)(2,1)} %collective-permute-done.6.refs_2_.refs_3_, ...), custom_call_target="tpu_custom_call" | custom-call | flops 335544320 | bytes 41943040 | tf_op jit(solution)/shard_map/load_weights/pallas_call | solution.py:297
  282.9 12.7 %first_backward.1 = bf16[32,32,128]{2,1,0:T(8,128)(2,1)S(1)} custom-call(s32[4]{0:T(128)S(1)} %pad_add_fusion.place, bf16[32,4096]{1,0:T(8,128)(2,1)S(1)} %collective-permute-done.1.up_ref, bf16[32,4096]{1,0:T(8,128)(2,1)S(1)} %collective-permute-done.15.arrived, bf16[4,32,4096]{2,1,0:T(8,128)(2,1)S(1)} %copy-done.3, f32[4,32,128]{2,1,0:T(8,128)S(1)} %copy-done.6, ...), custom_call_target="tpu_custom_call" | custom-call | flops 1342177280 | bytes 41943040 | tf_op jit(solution)/shard_map/first_backward/pallas_call | solution.py:297
  295.6 13.8 %all_to_all.25 = bf16[32,32,128]{2,1,0:T(8,128)(2,1)S(1)} all-to-all(bf16[32,32,128]{2,1,0:T(8,128)(2,1)S(1)} %first_backward.1), channel_id=1, replica_groups=mesh['yh'=2,'x'=4,'zh'=8,'zl'=2,'yl'=2,'c'=2] {'x','zl','yl','c'}, dimensions={0} | all-to-all | bytes 524288 | tf_op jit(solution)/shard_map/gather_grads/all_to_all | solution.py:421
  311.8 29.3 %all_to_all.26 = bf16[8,128,128]{2,1,0:T(8,128)(2,1)S(1)} all-to-all(bf16[8,128,128]{2,1,0:T(8,128)(2,1)S(1)} %bitcast.58), channel_id=1, replica_groups=mesh['yh'=2,'x'=4,'zh'=8,'zl'=2,'yl'=2,'c'=2] {'zh'}, dimensions={0} | all-to-all | bytes 524288 | tf_op jit(solution)/shard_map/sum_grads/all_to_all | solution.py:425
  343.1 4.3 %all-to-all-start.3 = ((f32[16,8,128]{2,1,0:T(8,128)}), f32[16,8,128]{2,1,0:T(8,128)S(1)}, u32[]{:S(2)}, u32[]{:S(2)}) async-start(f32[16,8,128]{2,1,0:T(8,128)} %broadcast_in_dim.16), calls=%async_computation.3 | async-start | bytes 131072 | tf_op jit(solution)/shard_map/clip/all_to_all | solution.py:345
  350.6 8.4 %all-to-all-done.3 = f32[16,8,128]{2,1,0:T(8,128)S(1)} async-done(((f32[16,8,128]{2,1,0:T(8,128)}), f32[16,8,128]{2,1,0:T(8,128)S(1)}, u32[]{:S(2)}, u32[]{:S(2)}) %all-to-all-start.3) | async-done | bytes 65568 | tf_op jit(solution)/shard_map/clip/all_to_all | solution.py:345
  359.7 6.7 %all-to-all-start.4 = ((f32[32,8,128]{2,1,0:T(8,128)}), f32[32,8,128]{2,1,0:T(8,128)S(1)}, u32[]{:S(2)}, u32[]{:S(2)}) async-start(f32[32,8,128]{2,1,0:T(8,128)} %broadcast_in_dim.17), calls=%async_computation.4 | async-start | bytes 262144 | tf_op jit(solution)/shard_map/clip/all_to_all | solution.py:345
  366.4 7.7 %all-to-all-done.4 = f32[32,8,128]{2,1,0:T(8,128)S(1)} async-done(((f32[32,8,128]{2,1,0:T(8,128)}), f32[32,8,128]{2,1,0:T(8,128)S(1)}, u32[]{:S(2)}, u32[]{:S(2)}) %all-to-all-start.4) | async-done | bytes 131104 | tf_op jit(solution)/shard_map/clip/all_to_all | solution.py:345
  (84 shorter events, 59.4 us)
Async XLA Ops:
  7.2 98.3 %all-gather.5.cloned.1.call-start = ((), (), s32[]{:S(2)}) async-start(), calls=%async_computation.5 | async-start | bytes 10813440 | tf_op jit(solution)/shard_map/gather_weights/all_gather | solution.py:327
  9.0 6.7 %collective-permute-start = (bf16[64,1280]{1,0:T(8,128)(2,1)S(1)}, bf16[64,1280]{1,0:T(8,128)(2,1)S(1)}, u32[]{:S(2)}, u32[]{:S(2)}) collective-permute-start(bf16[64,1280]{1,0:T(8,128)(2,1)S(1)} %get-tuple-element.57), channel_id=1, source_target_pairs={{0,2},{2,0},{1,3},{3,1},{4,6},{6,4},{5,7},{7,5},{8,10},{10,8},{9,1... | collective-permute-start | bytes 491528 | tf_op jit(solution)/shard_map/gather_weights/ppermute | solution.py:315
  16.5 193.8 %all-gather.7.cloned.1.call-start = ((), (), s32[]{:S(2)}) async-start(), calls=%async_computation.6 | async-start | bytes 17301504 | tf_op jit(solution)/shard_map/gather_weights/all_gather | solution.py:330
  17.3 8.7 %collective-permute-start.2 = (s32[32]{0:T(128)S(1)}, s32[32]{0:T(128)S(1)}, u32[]{:S(2)}, u32[]{:S(2)}) collective-permute-start(s32[32]{0:T(128)S(1)} %fusion.4), channel_id=1, source_target_pairs={{0,2},{2,0},{1,3},{3,1},{4,6},{6,4},{5,7},{7,5},{8,10},{10,8},{9,1... | collective-permute-start | bytes 392 | tf_op jit(solution)/shard_map/ppermute | solution.py:315
  22.8 7.1 %collective-permute-start.1 = (bf16[32,4096]{1,0:T(8,128)(2,1)S(1)}, bf16[32,4096]{1,0:T(8,128)(2,1)S(1)}, u32[]{:S(2)}, u32[]{:S(2)}) collective-permute-start(bf16[32,4096]{1,0:T(8,128)(2,1)S(1)} %reshape.99), channel_id=1, source_target_pairs={{0,2},{2,0},{1,3},{3,1},{4,6},{6,4},{5,7},{7,5},{8,10},{10,8},{9,1... | collective-permute-start | bytes 786440 | tf_op jit(solution)/shard_map/ppermute | solution.py:315
  29.9 15.4 %collective-permute-start.5 = (bf16[2,64,1280]{2,1,0:T(8,128)(2,1)S(1)}, bf16[2,64,1280]{2,1,0:T(8,128)(2,1)S(1)}, u32[]{:S(2)}, u32[]{:S(2)}) collective-permute-start(bf16[2,64,1280]{2,1,0:T(8,128)(2,1)S(1)} %copy-done.9), channel_id=1, source_target_pairs={{0,128},{64,192},{128,0},{192,64},{1,129},{65,193},{129,1},{193,65... | collective-permute-start | bytes 983048 | tf_op jit(solution)/shard_map/gather_weights/ppermute | solution.py:319
  36.2 6.6 %collective-permute-start.3 = (bf16[2,64,384]{2,1,0:T(8,128)(2,1)S(1)}, bf16[2,64,384]{2,1,0:T(8,128)(2,1)S(1)}, u32[]{:S(2)}, u32[]{:S(2)}) collective-permute-start(bf16[2,64,384]{2,1,0:T(8,128)(2,1)S(1)} %slice.28), channel_id=1, source_target_pairs={{0,64},{64,128},{128,192},{192,0},{1,65},{65,129},{129,193},{193,1... | collective-permute-start | bytes 294920 | tf_op jit(solution)/shard_map/gather_weights/ppermute | solution.py:319
  38.5 6.9 %collective-permute-start.4 = (bf16[2,64,384]{2,1,0:T(8,128)(2,1)S(1)}, bf16[2,64,384]{2,1,0:T(8,128)(2,1)S(1)}, u32[]{:S(2)}, u32[]{:S(2)}) collective-permute-start(bf16[2,64,384]{2,1,0:T(8,128)(2,1)S(1)} %slice.28), channel_id=1, source_target_pairs={{0,192},{64,0},{128,64},{192,128},{1,193},{65,1},{129,65},{193,129... | collective-permute-start | bytes 294920 | tf_op jit(solution)/shard_map/gather_weights/ppermute | solution.py:319
  108.8 53.5 %collective-permute-start.10 = (bf16[10,2,64,896]{3,2,1,0:T(8,128)(2,1)}, bf16[10,2,64,896]{3,2,1,0:T(8,128)(2,1)S(1)}, u32[]{:S(2)}, u32[]{:S(2)}) collective-permute-start(bf16[10,2,64,896]{3,2,1,0:T(8,128)(2,1)} %dynamic-slice_bitcast_fusion), channel_id=1, source_target_pairs={{0,192},{64,0},{128,64},{192,128},{1,193},{65,1},{129,65},{193,129... | collective-permute-start | bytes 6881288 | tf_op jit(solution)/shard_map/gather_weights/ppermute | solution.py:319
  113.0 54.6 %collective-permute-start.6 = (bf16[10,2,64,896]{3,2,1,0:T(8,128)(2,1)}, bf16[10,2,64,896]{3,2,1,0:T(8,128)(2,1)}, u32[]{:S(2)}, u32[]{:S(2)}) collective-permute-start(bf16[10,2,64,896]{3,2,1,0:T(8,128)(2,1)} %dynamic-slice_bitcast_fusion), channel_id=1, source_target_pairs={{0,64},{64,128},{128,192},{192,0},{1,65},{65,129},{129,193},{193,1... | collective-permute-start | bytes 6881288 | tf_op jit(solution)/shard_map/gather_weights/ppermute | solution.py:319
  162.2 33.8 %collective-permute-start.12 = (bf16[6,2,64,896]{3,2,1,0:T(8,128)(2,1)S(1)}, bf16[6,2,64,896]{3,2,1,0:T(8,128)(2,1)}, u32[]{:S(2)}, u32[]{:S(2)}) collective-permute-start(bf16[6,2,64,896]{3,2,1,0:T(8,128)(2,1)S(1)} %dynamic-slice_bitcast_fusion.1), channel_id=1, source_target_pairs={{0,192},{64,0},{128,64},{192,128},{1,193},{65,1},{129,65},{193,129... | collective-permute-start | bytes 4128776 | tf_op jit(solution)/shard_map/gather_weights/ppermute | solution.py:319
  167.6 33.6 %collective-permute-start.8 = (bf16[6,2,64,896]{3,2,1,0:T(8,128)(2,1)S(1)}, bf16[6,2,64,896]{3,2,1,0:T(8,128)(2,1)}, u32[]{:S(2)}, u32[]{:S(2)}) collective-permute-start(bf16[6,2,64,896]{3,2,1,0:T(8,128)(2,1)S(1)} %dynamic-slice_bitcast_fusion.1), channel_id=1, source_target_pairs={{0,64},{64,128},{128,192},{192,0},{1,65},{65,129},{129,193},{193,1... | collective-permute-start | bytes 4128776 | tf_op jit(solution)/shard_map/gather_weights/ppermute | solution.py:319
  169.5 35.9 %collective-permute-start.11 = (bf16[10,2,64,896]{3,2,1,0:T(8,128)(2,1)S(1)}, bf16[10,2,64,896]{3,2,1,0:T(8,128)(2,1)}, u32[]{:S(2)}, u32[]{:S(2)}) collective-permute-start(bf16[10,2,64,896]{3,2,1,0:T(8,128)(2,1)S(1)} %collective-permute-done.10.refs_6_.refs_7_), channel_id=1, source_target_pairs={{0,1},{1,0},{2,3},{3,2},{4,5},{5,4},{6,7},{7,6},{8,9},{9,8},{10,11... | collective-permute-start | bytes 6881288 | tf_op jit(solution)/shard_map/gather_weights/ppermute | solution.py:315
  172.7 32.7 %collective-permute-start.7 = (bf16[10,2,64,896]{3,2,1,0:T(8,128)(2,1)}, bf16[10,2,64,896]{3,2,1,0:T(8,128)(2,1)}, u32[]{:S(2)}, u32[]{:S(2)}) collective-permute-start(bf16[10,2,64,896]{3,2,1,0:T(8,128)(2,1)} %collective-permute-done.6.refs_2_.refs_3_), channel_id=1, source_target_pairs={{0,1},{1,0},{2,3},{3,2},{4,5},{5,4},{6,7},{7,6},{8,9},{9,8},{10,11... | collective-permute-start | bytes 6881288 | tf_op jit(solution)/shard_map/gather_weights/ppermute | solution.py:315
  196.0 9.3 %collective-permute-start.13 = (bf16[6,2,64,896]{3,2,1,0:T(8,128)(2,1)}, bf16[6,2,64,896]{3,2,1,0:T(8,128)(2,1)}, u32[]{:S(2)}, u32[]{:S(2)}) collective-permute-start(bf16[6,2,64,896]{3,2,1,0:T(8,128)(2,1)} %collective-permute-done.12.refs_8_.refs_9_), channel_id=1, source_target_pairs={{0,1},{1,0},{2,3},{3,2},{4,5},{5,4},{6,7},{7,6},{8,9},{9,8},{10,11... | collective-permute-start | bytes 4128776 | tf_op jit(solution)/shard_map/gather_weights/ppermute | solution.py:315
  201.2 7.2 %collective-permute-start.9 = (bf16[6,2,64,896]{3,2,1,0:T(8,128)(2,1)}, bf16[6,2,64,896]{3,2,1,0:T(8,128)(2,1)}, u32[]{:S(2)}, u32[]{:S(2)}) collective-permute-start(bf16[6,2,64,896]{3,2,1,0:T(8,128)(2,1)} %collective-permute-done.8.refs_4_.refs_5_), channel_id=1, source_target_pairs={{0,1},{1,0},{2,3},{3,2},{4,5},{5,4},{6,7},{7,6},{8,9},{9,8},{10,11... | collective-permute-start | bytes 4128776 | tf_op jit(solution)/shard_map/gather_weights/ppermute | solution.py:315
  227.4 11.0 %collective-permute-start.14 = (bf16[32,4096]{1,0:T(8,128)(2,1)S(1)}, bf16[32,4096]{1,0:T(8,128)(2,1)S(1)}, u32[]{:S(2)}, u32[]{:S(2)}) collective-permute-start(bf16[32,4096]{1,0:T(8,128)(2,1)S(1)} %get-tuple-element.37), channel_id=1, source_target_pairs={{0,258},{2,256},{256,2},{258,0},{1,259},{3,257},{257,3},{259,1},{4... | collective-permute-start | bytes 786440 | tf_op jit(solution)/shard_map/ppermute | solution.py:323
  261.3 34.4 %all-to-all-start = ((bf16[32,32,1024]{2,1,0:T(8,128)(2,1)}), bf16[32,32,1024]{2,1,0:T(8,128)(2,1)}, u32[]{:S(2)}, u32[]{:S(2)}) async-start(bf16[32,32,1024]{2,1,0:T(8,128)(2,1)} %get-tuple-element.51), calls=%async_computation | async-start | bytes 4194304 | tf_op jit(solution)/shard_map/normed_slices/all_to_all | solution.py:395
  266.8 16.1 %collective-permute-start.15 = (bf16[32,4096]{1,0:T(8,128)(2,1)S(1)}, bf16[32,4096]{1,0:T(8,128)(2,1)S(1)}, u32[]{:S(2)}, u32[]{:S(2)}) collective-permute-start(bf16[32,4096]{1,0:T(8,128)(2,1)S(1)} %get-tuple-element.43), channel_id=1, source_target_pairs={{0,258},{2,256},{256,2},{258,0},{1,259},{3,257},{257,3},{259,1},{4... | collective-permute-start | bytes 786440 | tf_op jit(solution)/shard_map/ppermute | solution.py:323
  309.4 65.8 %copy-start.11 = (f32[1,2,64,128]{3,2,1,0:T(8,128)S(1)}, f32[1,2,64,128]{3,2,1,0:T(8,128)}, u32[]{:S(2)}) copy-start(f32[1,2,64,128]{3,2,1,0:T(8,128)} %param.15) | copy-start | bytes 196612
  309.4 65.9 %copy-start.12 = (f32[1,2,64,128]{3,2,1,0:T(8,128)S(1)}, f32[1,2,64,128]{3,2,1,0:T(8,128)}, u32[]{:S(2)}) copy-start(f32[1,2,64,128]{3,2,1,0:T(8,128)} %param.14) | copy-start | bytes 196612
  343.1 16.0 %all-to-all-start.3 = ((f32[16,8,128]{2,1,0:T(8,128)}), f32[16,8,128]{2,1,0:T(8,128)S(1)}, u32[]{:S(2)}, u32[]{:S(2)}) async-start(f32[16,8,128]{2,1,0:T(8,128)} %broadcast_in_dim.16), calls=%async_computation.3 | async-start | bytes 131072 | tf_op jit(solution)/shard_map/clip/all_to_all | solution.py:345
  347.4 19.0 %collective-permute-start.16 = (f32[64,128]{1,0:T(8,128)S(1)}, f32[64,128]{1,0:T(8,128)S(1)}, u32[]{:S(2)}, u32[]{:S(2)}) collective-permute-start(f32[64,128]{1,0:T(8,128)S(1)} %constant_dynamic-slice_fusion), channel_id=1, source_target_pairs={{0,4},{4,0},{1,5},{5,1},{2,6},{6,2},{3,7},{7,3},{8,12},{12,8},{9,1... | collective-permute-start | bytes 98312 | tf_op jit(solution)/shard_map/sum_grads/ppermute | solution.py:315
  359.7 14.4 %all-to-all-start.4 = ((f32[32,8,128]{2,1,0:T(8,128)}), f32[32,8,128]{2,1,0:T(8,128)S(1)}, u32[]{:S(2)}, u32[]{:S(2)}) async-start(f32[32,8,128]{2,1,0:T(8,128)} %broadcast_in_dim.17), calls=%async_computation.4 | async-start | bytes 262144 | tf_op jit(solution)/shard_map/clip/all_to_all | solution.py:345
  (11 other events, 156.0 us)
Sparse Core Ops, SparseCore 0:
  16.6 88.8 all-gather.4
  107.6 102.6 all-gather.6
